TPU v7x, 32 devices: a whole 2x2x4 slice. The times are simulated.
32 devices in a mesh: cols: 16 (over z, y, x), walk: 2 (over core).
Axes of the slice: x: 2, y: 2, z: 4, core: 2. Of those that a mesh axis runs over, the one named last changes fastest.
Arguments:
- green_by_column: float32 [2, 4096, 4096], P('walk', 'cols'), parts along dimension 0, may hold values from -1.5 to 1.5
- field: int32 [2, 3, 4096], P('walk'), parts along dimension 0, may hold values from 0 to 1
Outputs:
- wrapped: float32 [2, 4096, 4096], P('walk', 'cols'), parts along dimension 0
There are 2 independent parts, one for each index of `walk`. A program takes and returns all parts, laid end to end along the dimension named above; each array names one. Nothing has to cross between parts.
All inputs are finite; a program needn't handle non-finite values.
Results may differ from a plain program's by a relative error of at most 0.00012.
Values sent between devices are 32-bit elements; how exact they have to be, the bound alone decides.
No kernel may reach another device: no remote copies, remote signals or barrier semaphores. Data moves between devices by JAX's collectives and lax.ppermute only.
A program may use at most 64 MiB of HBM per device.

v0:
```python
import functools
import jax
import jax.numpy as jnp
import ml_dtypes
import numpy as np
from jax import lax
from jax.experimental import pallas as pl
from jax.experimental.pallas import tpu as pltpu
from jax.sharding import PartitionSpec as P

LX = 64
LY = 64
SLICES = 3
hop_rate = 0.6
coupling = 0.65373
LANES = 128
TALL = 256
UNROLL = 8
VMEM_LIMIT = 60 << 20
IN_FLIGHT = 5
AHEAD = 5
LATE = 5
BF = jnp.bfloat16
F32 = jnp.float32


def circulant(length, growth):
    angles = 2.0 * np.pi * np.arange(length) / length
    column = np.cos(np.outer(np.arange(length), angles)) @ np.exp(growth * np.cos(angles)) / length
    differ = (np.arange(length)[:, None] - np.arange(length)[None, :]) % length
    return column[differ]


def split_matrix(matrix):
    high = matrix.astype(ml_dtypes.bfloat16)
    return high, (matrix - high.astype(np.float64)).astype(ml_dtypes.bfloat16)


def lane_side(matrix):
    high, low = split_matrix(np.kron(np.eye(LANES // matrix.shape[0]), matrix).T)
    return jnp.asarray(np.tile(np.concatenate([high, low], axis=1), (2, 1)))


def row_side(matrix):
    high, low = split_matrix(np.kron(np.eye(LANES // matrix.shape[0]), matrix))
    return jnp.asarray(np.tile(np.concatenate([high, low], axis=0), (1, 2)))


def halves(value):
    high = value.astype(BF)
    return high, (value - high.astype(F32)).astype(BF)


def mix_lanes(data, right):
    high, low = halves(data)
    both = jnp.dot(jnp.concatenate([high, low], axis=1), right, preferred_element_type=F32)
    return both[:, :LANES] + both[:, LANES:]


def mix_rows(left, data):
    high, low = halves(data)
    mid = data.shape[0] // 2
    stacked = jnp.concatenate(
        [jnp.concatenate([part[:mid], part[mid:]], axis=1) for part in (high, low)], axis=0
    )
    both = jnp.dot(left, stacked, preferred_element_type=F32)
    both = both[:mid] + both[mid:]
    return jnp.concatenate([both[:, :LANES], both[:, LANES:]], axis=0)


def swap_halves(first, second):
    low = lax.broadcasted_iota(jnp.int32, first.shape, 1) < LANES // 2
    return (
        jnp.where(low, first, pltpu.roll(second, LANES // 2, 1)),
        jnp.where(low, pltpu.roll(first, LANES // 2, 1), second),
    )


def partner(parts, mask):
    return lax.axis_index("cols").astype(jnp.int32) ^ mask


def left_body(parts, x_ref, field_ref, right_ref, left_ref, *rest):
    outs, gain_ref, work = rest[:-2], rest[-2], rest[-1]
    rows = x_ref.shape[0]

    @pl.when(pl.program_id(0) == 0)
    def _():
        gain = [jnp.exp(coupling * (2.0 * field_ref[moment].astype(F32) - 1.0)) for moment in range(SLICES)]
        for moment in range(SLICES):
            for c in range(LX // 2):
                row = jnp.broadcast_to(gain[moment][:, c * LANES : (c + 1) * LANES], (8, LANES))
                even, odd = swap_halves(row, row)
                gain_ref[moment, 2 * c : 2 * c + 1, :] = even[:1]
                gain_ref[moment, 2 * c + 1 : 2 * c + 2, :] = odd[:1]

    for group in range(rows // 16):
        for c in range(LX // 2):
            lanes = slice(c * LANES, (c + 1) * LANES)
            even, odd = swap_halves(x_ref[group * 16 : group * 16 + 8, lanes], x_ref[group * 16 + 8 : group * 16 + 16, lanes])
            work[pl.ds(group * 8 * LX + 2 * c, 8, stride=LX), :] = even
            work[pl.ds(group * 8 * LX + 2 * c + 1, 8, stride=LX), :] = odd
    for moment in range(SLICES):
        gain = jnp.concatenate([gain_ref[moment]] * (TALL // LX), axis=0)
        for top in range(0, work.shape[0], TALL):
            work[top : top + TALL, :] = mix_lanes(work[top : top + TALL, :] * gain, right_ref[...])
        for top in range(0, work.shape[0], TALL):
            work[top : top + TALL, :] = mix_rows(left_ref[...], work[top : top + TALL, :])
    far = parts // 2
    for mask in range(parts):
        for half in range(2):
            ref = outs[mask if mask < far else half * far + mask]
            lanes = slice(half * LANES, (half + 1) * LANES) if mask < far else slice(0, LANES)
            start = partner(parts, mask) * (LX // parts) + 2 * half
            for group in range(rows // 16):
                even = work[pl.ds(group * 8 * LX + start, 8, stride=LX), :]
                odd = work[pl.ds(group * 8 * LX + start + 1, 8, stride=LX), :]
                above, below = swap_halves(even, odd)
                ref[group * 16 : group * 16 + 8, lanes] = above
                ref[group * 16 + 8 : group * 16 + 16, lanes] = below


def left_chain(parts, block, x, field, right, left):
    rows, sites = x.shape
    far = parts // 2
    widths = [2 * LANES] * far + [LANES] * parts
    whole = lambda array: pl.BlockSpec(array.shape, lambda g: (0,) * array.ndim)
    outs = pl.pallas_call(
        functools.partial(left_body, parts),
        grid=(rows // block,),
        in_specs=[pl.BlockSpec((block, sites), lambda g: (g, 0)), whole(field), whole(right), whole(left)],
        out_specs=[pl.BlockSpec((block, width), lambda g: (g, 0)) for width in widths],
        out_shape=[jax.ShapeDtypeStruct((rows, width), F32) for width in widths],
        scratch_shapes=[pltpu.VMEM((SLICES, LX, LANES), F32), pltpu.VMEM((block // 2 * LX, LANES), F32)],
        compiler_params=pltpu.CompilerParams(vmem_limit_bytes=VMEM_LIMIT),
        cost_estimate=pl.CostEstimate(flops=rows * sites * 256 * 2 * 6, bytes_accessed=rows * sites * 8, transcendentals=0),
        name="left_chain",
    )(x, field, right, left)
    return outs[:far], outs[far:parts], outs[parts:]


def right_body(parts, joined, loss_ref, left_y_ref, left_x_ref, *rest):
    pieces, outs, work = rest[:parts], rest[-parts - 1 : -1], rest[-1]
    sites = work.shape[0]
    local = sites // parts

    def rows_of(mask):
        return pl.ds(pl.multiple_of(partner(parts, mask) * local, local), local)

    for mask in range(parts):
        work[rows_of(mask), :] = pieces[mask][...]
    step = TALL // LX
    for moment in range(SLICES):

        @pl.loop(0, sites // TALL // UNROLL)
        def _(turn):
            for q in range(UNROLL):
                at = pl.ds(pl.multiple_of((turn * UNROLL + q) * TALL, TALL), TALL)
                work[at, :] = mix_rows(left_y_ref[...], work[at, :] * loss_ref[at, moment : moment + 1])

        @pl.loop(0, LY // step // UNROLL)
        def _(turn):
            for r in range(UNROLL):
                y = (turn * UNROLL + r) * step
                data = jnp.concatenate([work[pl.ds(y + q, LX, stride=LY), :] for q in range(step)], axis=0)
                data = mix_rows(left_x_ref[...], data)
                for q in range(step):
                    work[pl.ds(y + q, LX, stride=LY), :] = data[q * LX : (q + 1) * LX]

    for mask in range(parts):
        if joined and mask < parts // 2:
            outs[mask][:, :LANES] = rest[parts + mask][...]
            outs[mask][:, LANES:] = work[rows_of(mask), :]
        else:
            outs[mask][...] = work[rows_of(mask), :]


def right_chain(parts, half, loss, left_y, left_x, pieces, before=()):
    sites = loss.shape[0]
    rows = pieces[0].shape[0]
    widths = [LANES * 2 if before and mask < parts // 2 else LANES for mask in range(parts)]
    lane = lambda array: half if array.shape[1] > LANES else 0
    whole = lambda array: pl.BlockSpec(array.shape, lambda g: (0,) * array.ndim)
    return pl.pallas_call(
        functools.partial(right_body, parts, bool(before)),
        grid=(1,),
        in_specs=[whole(loss), whole(left_y), whole(left_x)]
        + [pl.BlockSpec((rows, LANES), functools.partial(lambda at, g: (0, at), lane(piece))) for piece in pieces]
        + [whole(array) for array in before],
        out_specs=[pl.BlockSpec((rows, width), lambda g: (0, 0)) for width in widths],
        out_shape=[jax.ShapeDtypeStruct((rows, width), F32) for width in widths],
        scratch_shapes=[pltpu.VMEM((sites, LANES), F32)],
        compiler_params=pltpu.CompilerParams(vmem_limit_bytes=VMEM_LIMIT),
        cost_estimate=pl.CostEstimate(flops=sites * LANES * 256 * 2 * 6, bytes_accessed=sites * LANES * 12, transcendentals=0),
        name="right_chain",
    )(loss, left_y, left_x, *pieces, *before)


def place_body(parts, spots, held, *rest):
    count = len(spots)
    blocks, out, landed, came, went = rest[:count], rest[count + held], rest[-3], rest[-2], rest[-1]
    local = out.shape[1] // parts
    copies = []
    column = 0
    for at, (mask, lane) in enumerate(spots):
        width = blocks[at].shape[1]
        spot = landed.at[:, pl.ds(column, width)]
        column += width
        start = pl.multiple_of(partner(parts, mask) * local + lane, LANES)
        copies.append((
            pltpu.make_async_copy(blocks[at], spot, came.at[at]),
            pltpu.make_async_copy(spot, out.at[:, pl.ds(start, width)], went.at[at]),
        ))
    for copy, _ in copies:
        copy.start()
    for copy, onward in copies:
        copy.wait()
        onward.start()
    for _, onward in copies:
        onward.wait()


def place(parts, spots, blocks, held=None):
    rows = blocks[0].shape[0]
    width = sum(block.shape[1] for block in blocks)
    held = [] if held is None else [held]
    anywhere = pl.BlockSpec(memory_space=pl.ANY)
    return pl.pallas_call(
        functools.partial(place_body, parts, spots, len(held)),
        in_specs=[anywhere] * (len(blocks) + len(held)),
        out_specs=anywhere,
        out_shape=jax.ShapeDtypeStruct((rows, rows * parts), F32),
        scratch_shapes=[pltpu.VMEM((rows, width), F32)] + [pltpu.SemaphoreType.DMA((len(blocks),))] * 2,
        input_output_aliases={len(blocks): 0} if held else {},
        compiler_params=pltpu.CompilerParams(vmem_limit_bytes=VMEM_LIMIT),
        cost_estimate=pl.CostEstimate(flops=0, bytes_accessed=rows * width * 8, transcendentals=0),
        name="place",
    )(*blocks, *held)


def kernel(length, growth):
    indices = jnp.arange(length, dtype=jnp.int32)
    phases = indices[:, None] * indices[None, :] % length
    angles = 2.0 * jnp.pi * phases.astype(jnp.float32) / length
    cosines = jnp.cos(angles)
    sines = jnp.sin(angles)
    spectrum = jnp.exp(growth * jnp.cos(2.0 * jnp.pi * indices.astype(jnp.float32) / length))
    highest = lax.Precision.HIGHEST
    total = jnp.dot(cosines * spectrum[None, :], cosines.T, precision=highest)
    total = total + jnp.dot(sines * spectrum[None, :], sines.T, precision=highest)
    return total / length


def whole_exchange(green_by_column, field):
    highest = lax.Precision.HIGHEST
    walkers, local_cols, sites = green_by_column.shape
    fwd_x = kernel(LX, hop_rate)
    fwd_y = kernel(LY, hop_rate)
    inv_x = kernel(LX, -hop_rate)
    inv_y = kernel(LY, -hop_rate)
    spins = 2.0 * field.astype(jnp.float32) - 1.0
    green = green_by_column
    for moment in range(SLICES):
        left_green = green
        left_green = left_green * jnp.exp(coupling * spins[:, moment, :])[:, None, :]
        left_blocks = left_green.reshape(walkers, local_cols, LX, LY)
        left_blocks = jnp.einsum("xa,wcab->wcxb", fwd_x, left_blocks, precision=highest)
        left_blocks = jnp.einsum("yb,wcxb->wcxy", fwd_y, left_blocks, precision=highest)
        green = left_blocks.reshape(walkers, local_cols, sites)
    parts = lax.axis_size("cols")
    shaped_in = green.reshape(walkers, local_cols, parts, sites // parts)
    row_block = lax.all_to_all(shaped_in, "cols", split_axis=2, concat_axis=1, tiled=True)
    count = row_block.shape[0]
    width = row_block.shape[3]
    blocks = row_block.reshape(count, sites, width)
    for moment in range(SLICES):
        blocks = blocks * jnp.exp(-coupling * spins[:, moment, :])[:, :, None]
        shaped = blocks.reshape(count, LX, LY, width)
        shaped = jnp.einsum("by,wabr->wayr", inv_y, shaped, precision=highest)
        shaped = jnp.einsum("ax,wayr->wxyr", inv_x, shaped, precision=highest)
        blocks = shaped.reshape(count, sites, width)
    rows_done = blocks.reshape(count, sites, 1, width)
    rows_done = rows_done.reshape(walkers, sites, sites // parts)
    green = lax.all_to_all(rows_done, "cols", split_axis=1, concat_axis=2, tiled=True)
    return green


class Links:
    def __init__(self, parts):
        self.parts = parts
        self.sent = []
        self.after = None

    def send(self, block, mask):
        hold = [self.after] if self.after is not None else []
        back = len(self.sent) - IN_FLIGHT
        if back >= 0:
            hold.append(self.sent[back]["value"])
        if hold:
            got = lax.optimization_barrier(tuple([block] + hold))
            block = got[0]
            if back >= 0:
                self.sent[back]["value"] = got[-1]
        value = lax.ppermute(block, "cols", [(s, s ^ mask) for s in range(self.parts)])
        self.sent.append({"value": value})
        return self.sent[-1]


def woven(first, second):
    pairs = [(first[at : at + 1], second[at : at + 1]) for at in range(max(len(first), len(second)))]
    return [mask for pair in pairs for part in pair for mask in part]


def pipelined(green_by_column, field):
    _, rows, sites = green_by_column.shape
    parts = lax.axis_size("cols")
    half = parts // 2
    x = green_by_column.reshape(rows, sites)
    loss = jnp.exp(-coupling * (2.0 * field[0].astype(F32) - 1.0)).T
    right = lane_side(circulant(LY, hop_rate))
    left = row_side(circulant(LX, hop_rate))
    left_y = row_side(circulant(LY, -hop_rate))
    left_x = row_side(circulant(LX, -hop_rate))
    far = [m for pair in zip(range(3 * parts // 4, parts), range(half, 3 * parts // 4)) for m in pair]
    near = [m for pair in zip(range(parts // 4, half), range(1, parts // 4 + 1)) for m in pair][: half - 1]
    every = range(half, parts)
    links = Links(parts)

    def chain(h, near_held, far_held, before=()):
        pieces = [near_held[m]["value"] for m in range(half)] + [far_held[m]["value"] for m in every]
        outs = right_chain(parts, h, loss, left_y, left_x, pieces, before)
        links.after = outs[0]
        return outs

    near_blocks, *far_blocks = left_chain(parts, rows // 4, x, field.transpose(1, 0, 2), right, left)
    near_held = {0: {"value": near_blocks[0]}}
    far_held = [{}, {}]
    for mask in woven(far, near):
        if mask < half:
            near_held[mask] = links.send(near_blocks[mask], mask)
        else:
            far_held[0][mask] = links.send(far_blocks[0][mask - half], mask)
    for at, mask in enumerate(far):
        if at == LATE:
            early = chain(0, near_held, far_held[0])
        far_held[1][mask] = links.send(far_blocks[1][mask - half], mask)
    far_done = [{}, {}]
    for at, mask in enumerate(far):
        if at == AHEAD:
            late = chain(1, near_held, far_held[1], early[:half])
        far_done[0][mask] = links.send(early[mask], mask)
    near_done = {0: {"value": late[0]}}
    for mask in woven(far, near):
        if mask < half:
            near_done[mask] = links.send(late[mask], mask)
        else:
            far_done[1][mask] = links.send(late[mask], mask)
    result = place(parts, [(m, 0) for m in every], [far_done[0][m]["value"] for m in every])
    spots = [(m, 0) for m in range(half)] + [(m, LANES) for m in every]
    blocks = [near_done[m]["value"] for m in range(half)] + [far_done[1][m]["value"] for m in every]
    return place(parts, spots, blocks, result).reshape(green_by_column.shape)


def shards(green_by_column, field):
    walkers, rows, sites = green_by_column.shape
    parts = lax.axis_size("cols")
    fits = walkers == 1 and rows == 256 and rows * parts == sites and parts & (parts - 1) == 0 and parts >= 8
    if fits and LX * LY == sites and LX == LY == 64:
        return pipelined(green_by_column, field)
    return whole_exchange(green_by_column, field)


def solution(mesh):
    return jax.shard_map(
        shards,
        mesh=mesh,
        in_specs=(P("walk", "cols", None), P("walk", None, None)),
        out_specs=P("walk", "cols", None),
        check_vma=False,
    )
```

profile of v0, /device:TPU:0, one launch (start us, length us, event | category | flops | bytes accessed | tf_op | source)
XLA Modules:
  0.0 228.7 jit_solution(16478706997749999499)
XLA Ops:
  0.0 15.0 %left_chain.1 = (f32[256,256]{1,0:T(8,128)}, f32[256,256]{1,0:T(8,128)}, f32[256,256]{1,0:T(8,128)}, f32[256,256]{1,0:T(8,128)}, f32[256,256]{1,0:T(8,128)}, /*i...) custom-call(f32[256,4096]{1,0:T(8,128)} %bitcast.8, ...), custom_call_target="tpu_custom_call" | custom-call | flops 3221225472 | bytes 8388608 | tf_op jit(solution)/shard_map/left_chain/pallas_call | solution.py:128
  15.0 3.0 %collective-permute-start = (f32[256,256]{1,0:T(8,128)}, f32[256,256]{1,0:T(8,128)S(1)}, u32[]{:S(2)}, u32[]{:S(2)}) collective-permute-start(f32[256,256]{1,0:T(8,128)} %get-tuple-element.145), channel_id=1, source_target_pairs={{0,2},{2,0},{4,6},{6,4},{8,10},{10,8},{12,14},{14,12},{16,18},{18,... | collective-permute-start | bytes 786440 | tf_op jit(solution)/shard_map/ppermute | solution.py:304
  19.6 2.6 %collective-permute-start.1 = (f32[256,128]{1,0:T(8,128)}, f32[256,128]{1,0:T(8,128)S(1)}, u32[]{:S(2)}, u32[]{:S(2)}) collective-permute-start(f32[256,128]{1,0:T(8,128)} %get-tuple-element.149), channel_id=1, source_target_pairs={{0,16},{2,18},{4,20},{6,22},{8,24},{10,26},{12,28},{14,30},{16,0},... | collective-permute-start | bytes 393224 | tf_op jit(solution)/shard_map/ppermute | solution.py:304
  22.4 3.6 %collective-permute-start.8 = (f32[256,128]{1,0:T(8,128)}, f32[256,128]{1,0:T(8,128)S(1)}, u32[]{:S(2)}, u32[]{:S(2)}) collective-permute-start(f32[256,128]{1,0:T(8,128)} %get-tuple-element.167), channel_id=1, source_target_pairs={{0,26},{2,24},{4,30},{6,28},{8,18},{10,16},{12,22},{14,20},{16,10}... | collective-permute-start | bytes 393224 | tf_op jit(solution)/shard_map/ppermute | solution.py:304
  26.0 3.5 %collective-permute-done.1.rest_8_ = f32[256,128]{1,0:T(8,128)S(1)} collective-permute-done((f32[256,128]{1,0:T(8,128)}, f32[256,128]{1,0:T(8,128)S(1)}, u32[]{:S(2)}, u32[]{:S(2)}) %collective-permute-start.1) | collective-permute-done | bytes 131104 | tf_op jit(solution)/shard_map/ppermute | solution.py:304
  29.6 5.6 %collective-permute-done.6.rest_12_ = f32[256,128]{1,0:T(8,128)S(1)} collective-permute-done((f32[256,128]{1,0:T(8,128)}, f32[256,128]{1,0:T(8,128)S(1)}, u32[]{:S(2)}, u32[]{:S(2)}) %collective-permute-start.6) | collective-permute-done | bytes 131104 | tf_op jit(solution)/shard_map/ppermute | solution.py:304
  36.5 4.4 %collective-permute-start.9 = (f32[256,256]{1,0:T(8,128)}, f32[256,256]{1,0:T(8,128)S(1)}, u32[]{:S(2)}, u32[]{:S(2)}) collective-permute-start(f32[256,256]{1,0:T(8,128)} %get-tuple-element.168), channel_id=1, source_target_pairs={{0,12},{2,14},{4,8},{6,10},{8,4},{10,6},{12,0},{14,2},{16,28},{18,... | collective-permute-start | bytes 786440 | tf_op jit(solution)/shard_map/ppermute | solution.py:304
  49.8 4.8 %collective-permute-start.13 = (f32[256,128]{1,0:T(8,128)}, f32[256,128]{1,0:T(8,128)S(1)}, u32[]{:S(2)}, u32[]{:S(2)}) collective-permute-start(f32[256,128]{1,0:T(8,128)} %get-tuple-element.182), channel_id=1, source_target_pairs={{0,22},{2,20},{4,18},{6,16},{8,30},{10,28},{12,26},{14,24},{16,6},... | collective-permute-start | bytes 393224 | tf_op jit(solution)/shard_map/ppermute | solution.py:304
  54.7 4.3 %collective-permute-done.7.rest_5_ = f32[256,256]{1,0:T(8,128)S(1)} collective-permute-done((f32[256,256]{1,0:T(8,128)}, f32[256,256]{1,0:T(8,128)S(1)}, u32[]{:S(2)}, u32[]{:S(2)}) %collective-permute-start.7) | collective-permute-done | bytes 262176 | tf_op jit(solution)/shard_map/ppermute | solution.py:304
  59.0 2.8 %collective-permute-start.14 = (f32[256,128]{1,0:T(8,128)}, f32[256,128]{1,0:T(8,128)S(1)}, u32[]{:S(2)}, u32[]{:S(2)}) collective-permute-start(f32[256,128]{1,0:T(8,128)} %get-tuple-element.188), channel_id=1, source_target_pairs={{0,30},{2,28},{4,26},{6,24},{8,22},{10,20},{12,18},{14,16},{16,14}... | collective-permute-start | bytes 393224 | tf_op jit(solution)/shard_map/ppermute | solution.py:304
  61.7 3.1 %collective-permute-start.11 = (f32[256,256]{1,0:T(8,128)}, f32[256,256]{1,0:T(8,128)S(1)}, u32[]{:S(2)}, u32[]{:S(2)}) collective-permute-start(f32[256,256]{1,0:T(8,128)} %get-tuple-element.173), channel_id=1, source_target_pairs={{0,14},{2,12},{4,10},{6,8},{8,6},{10,4},{12,2},{14,0},{16,30},{18,... | collective-permute-start | bytes 786440 | tf_op jit(solution)/shard_map/ppermute | solution.py:304
  66.5 3.8 %collective-permute-done.13.rest_11_ = f32[256,128]{1,0:T(8,128)S(1)} collective-permute-done((f32[256,128]{1,0:T(8,128)}, f32[256,128]{1,0:T(8,128)S(1)}, u32[]{:S(2)}, u32[]{:S(2)}) %collective-permute-start.13) | collective-permute-done | bytes 131104 | tf_op jit(solution)/shard_map/ppermute | solution.py:304
  71.4 4.7 %collective-permute-done.12.rest_10_ = f32[256,128]{1,0:T(8,128)S(1)} collective-permute-done((f32[256,128]{1,0:T(8,128)}, f32[256,128]{1,0:T(8,128)S(1)}, u32[]{:S(2)}, u32[]{:S(2)}) %collective-permute-start.12) | collective-permute-done | bytes 131104 | tf_op jit(solution)/shard_map/ppermute | solution.py:304
  80.4 8.9 %collective-permute-start.16 = (f32[256,128]{1,0:T(8,128)S(1)}, f32[256,128]{1,0:T(8,128)S(1)}, u32[]{:S(2)}, u32[]{:S(2)}) collective-permute-start(f32[256,128]{1,0:T(8,128)S(1)} %copy-done.42), channel_id=1, source_target_pairs={{0,18},{2,16},{4,22},{6,20},{8,26},{10,24},{12,30},{14,28},{16,2},... | collective-permute-start | bytes 393224 | tf_op jit(solution)/shard_map/ppermute | solution.py:304
  90.0 15.3 %right_chain.2 = (f32[256,128]{1,0:T(8,128)}, f32[256,128]{1,0:T(8,128)}, f32[256,128]{1,0:T(8,128)}, f32[256,128]{1,0:T(8,128)}, f32[256,128]{1,0:T(8,128)}, /*...) custom-call(f32[4096,3]{1,0:T(8,128)} %exponential_bitcast_fusion.lo, ...), custom_call_target="tpu_custom_call" | custom-call | flops 1610612736 | bytes 6291456 | tf_op jit(solution)/shard_map/right_chain/pallas_call | solution.py:184
  105.3 3.4 %collective-permute-start.18 = (f32[256,128]{1,0:T(8,128)S(1)}, f32[256,128]{1,0:T(8,128)S(1)}, u32[]{:S(2)}, u32[]{:S(2)}) collective-permute-start(f32[256,128]{1,0:T(8,128)S(1)} %copy-done.41), channel_id=1, source_target_pairs={{0,20},{2,22},{4,16},{6,18},{8,28},{10,30},{12,24},{14,26},{16,4},... | collective-permute-start | bytes 393224 | tf_op jit(solution)/shard_map/ppermute | solution.py:304
  108.8 4.8 %collective-permute-start.22 = (f32[256,128]{1,0:T(8,128)S(1)}, f32[256,128]{1,0:T(8,128)S(1)}, u32[]{:S(2)}, u32[]{:S(2)}) collective-permute-start(f32[256,128]{1,0:T(8,128)S(1)} %copy-done.39), channel_id=1, source_target_pairs={{0,30},{2,28},{4,26},{6,24},{8,22},{10,20},{12,18},{14,16},{16,14}... | collective-permute-start | bytes 393224 | tf_op jit(solution)/shard_map/ppermute | solution.py:304
  113.7 8.4 %collective-permute-done.18.rest_10_ = f32[256,128]{1,0:T(8,128)S(1)} collective-permute-done((f32[256,128]{1,0:T(8,128)S(1)}, f32[256,128]{1,0:T(8,128)S(1)}, u32[]{:S(2)}, u32[]{:S(2)}) %collective-permute-start.18) | collective-permute-done | bytes 131104 | tf_op jit(solution)/shard_map/ppermute | solution.py:304
  122.1 4.3 %collective-permute-start.37 = (f32[256,128]{1,0:T(8,128)}, f32[256,128]{1,0:T(8,128)S(1)}, u32[]{:S(2)}, u32[]{:S(2)}) collective-permute-start(f32[256,128]{1,0:T(8,128)} %get-tuple-element.257), channel_id=1, source_target_pairs={{0,26},{2,24},{4,30},{6,28},{8,18},{10,16},{12,22},{14,20},{16,10}... | collective-permute-start | bytes 393224 | tf_op jit(solution)/shard_map/ppermute | solution.py:304
  132.2 16.2 %right_chain.3 = (f32[256,256]{1,0:T(8,128)}, f32[256,256]{1,0:T(8,128)}, f32[256,256]{1,0:T(8,128)}, f32[256,256]{1,0:T(8,128)}, f32[256,256]{1,0:T(8,128)}, /*...) custom-call(f32[4096,3]{1,0:T(8,128)} %exponential_bitcast_fusion.lo, ...), custom_call_target="tpu_custom_call" | custom-call | flops 1610612736 | bytes 6291456 | tf_op jit(solution)/shard_map/right_chain/pallas_call | solution.py:184
  148.4 2.9 %collective-permute-start.24 = (f32[256,128]{1,0:T(8,128)S(1)}, f32[256,128]{1,0:T(8,128)S(1)}, u32[]{:S(2)}, u32[]{:S(2)}) collective-permute-start(f32[256,128]{1,0:T(8,128)S(1)} %copy-done.46), channel_id=1, source_target_pairs={{0,30},{2,28},{4,26},{6,24},{8,22},{10,20},{12,18},{14,16},{16,14}... | collective-permute-start | bytes 393224 | tf_op jit(solution)/shard_map/ppermute | solution.py:304
  151.8 4.4 %collective-permute-start.38 = (f32[256,128]{1,0:T(8,128)S(1)}, f32[256,128]{1,0:T(8,128)S(1)}, u32[]{:S(2)}, u32[]{:S(2)}) collective-permute-start(f32[256,128]{1,0:T(8,128)S(1)} %copy-done.44), channel_id=1, source_target_pairs={{0,22},{2,20},{4,18},{6,16},{8,30},{10,28},{12,26},{14,24},{16,6},... | collective-permute-start | bytes 393224 | tf_op jit(solution)/shard_map/ppermute | solution.py:304
  156.3 3.3 %collective-permute-start.31 = (f32[256,256]{1,0:T(8,128)}, f32[256,256]{1,0:T(8,128)S(1)}, u32[]{:S(2)}, u32[]{:S(2)}) collective-permute-start(f32[256,256]{1,0:T(8,128)} %get-tuple-element.242), channel_id=1, source_target_pairs={{0,8},{2,10},{4,12},{6,14},{8,0},{10,2},{12,4},{14,6},{16,24},{18,... | collective-permute-start | bytes 786440 | tf_op jit(solution)/shard_map/ppermute | solution.py:304
  160.3 7.7 %collective-permute-done.34.rest_1_ = f32[256,128]{1,0:T(8,128)S(1)} collective-permute-done((f32[256,128]{1,0:T(8,128)S(1)}, f32[256,128]{1,0:T(8,128)S(1)}, u32[]{:S(2)}, u32[]{:S(2)}) %collective-permute-start.34) | collective-permute-done | bytes 131104 | tf_op jit(solution)/shard_map/ppermute | solution.py:304
  169.3 4.9 %collective-permute-start.39 = (f32[256,128]{1,0:T(8,128)}, f32[256,128]{1,0:T(8,128)S(1)}, u32[]{:S(2)}, u32[]{:S(2)}) collective-permute-start(f32[256,128]{1,0:T(8,128)} %get-tuple-element.259), channel_id=1, source_target_pairs={{0,26},{2,24},{4,30},{6,28},{8,18},{10,16},{12,22},{14,20},{16,10}... | collective-permute-start | bytes 393224 | tf_op jit(solution)/shard_map/ppermute | solution.py:304
  177.5 5.1 %collective-permute-done.35.rest_12_ = f32[256,128]{1,0:T(8,128)S(1)} collective-permute-done((f32[256,128]{1,0:T(8,128)}, f32[256,128]{1,0:T(8,128)S(1)}, u32[]{:S(2)}, u32[]{:S(2)}) %collective-permute-start.35) | collective-permute-done | bytes 131104 | tf_op jit(solution)/shard_map/ppermute | solution.py:304
  188.9 4.1 %collective-permute-start.41 = (f32[256,128]{1,0:T(8,128)}, f32[256,128]{1,0:T(8,128)S(1)}, u32[]{:S(2)}, u32[]{:S(2)}) collective-permute-start(f32[256,128]{1,0:T(8,128)} %get-tuple-element.263), channel_id=1, source_target_pairs={{0,28},{2,30},{4,24},{6,26},{8,20},{10,22},{12,16},{14,18},{16,12}... | collective-permute-start | bytes 393224 | tf_op jit(solution)/shard_map/ppermute | solution.py:304
  193.0 3.4 %collective-permute-done.32.rest_9_ = f32[256,128]{1,0:T(8,128)S(1)} collective-permute-done((f32[256,128]{1,0:T(8,128)}, f32[256,128]{1,0:T(8,128)S(1)}, u32[]{:S(2)}, u32[]{:S(2)}) %collective-permute-start.32) | collective-permute-done | bytes 131104 | tf_op jit(solution)/shard_map/ppermute | solution.py:304
  197.0 8.8 %collective-permute-done.41.rest_14_ = f32[256,128]{1,0:T(8,128)S(1)} collective-permute-done((f32[256,128]{1,0:T(8,128)}, f32[256,128]{1,0:T(8,128)S(1)}, u32[]{:S(2)}, u32[]{:S(2)}) %collective-permute-start.41) | collective-permute-done | bytes 131104 | tf_op jit(solution)/shard_map/ppermute | solution.py:304
  207.5 7.7 %collective-permute-start.43 = (f32[256,128]{1,0:T(8,128)}, f32[256,128]{1,0:T(8,128)S(1)}, u32[]{:S(2)}, u32[]{:S(2)}) collective-permute-start(f32[256,128]{1,0:T(8,128)} %get-tuple-element.267), channel_id=1, source_target_pairs={{0,20},{2,22},{4,16},{6,18},{8,28},{10,30},{12,24},{14,26},{16,4},... | collective-permute-start | bytes 393224 | tf_op jit(solution)/shard_map/ppermute | solution.py:304
  217.6 6.2 %collective-permute-done.43.rest_10_ = f32[256,128]{1,0:T(8,128)S(1)} collective-permute-done((f32[256,128]{1,0:T(8,128)}, f32[256,128]{1,0:T(8,128)S(1)}, u32[]{:S(2)}, u32[]{:S(2)}) %collective-permute-start.43) | collective-permute-done | bytes 131104 | tf_op jit(solution)/shard_map/ppermute | solution.py:304
  225.7 2.9 %place.3 = f32[256,4096]{1,0:T(8,128)} custom-call(f32[256,256]{1,0:T(8,128)} %get-tuple-element.221.rest_0_, f32[256,256]{1,0:T(8,128)} %copy-done.8, f32[256,256]{1,0:T(8,128)} %copy-done.9, f32[256,256]{1,0:T(8,128)} %copy-done.12, f32[256,256]{1,0:T(8,128)} %copy-done.7, f32[256,256]{1,0:T(8,128)} %copy-done.10, ...), custom_call_target="tpu_custom_call", output_to_operand_aliasing={{}: (16, {})} | custom-call | bytes 6291456 | tf_op jit(solution)/shard_map/place/pallas_call | solution.py:228
  (174 shorter events, 44.2 us)
Async XLA Ops:
  15.0 27.4 %collective-permute-start = (f32[256,256]{1,0:T(8,128)}, f32[256,256]{1,0:T(8,128)S(1)}, u32[]{:S(2)}, u32[]{:S(2)}) collective-permute-start(f32[256,256]{1,0:T(8,128)} %get-tuple-element.145), channel_id=1, source_target_pairs={{0,2},{2,0},{4,6},{6,4},{8,10},{10,8},{12,14},{14,12},{16,18},{18,... | collective-permute-start | bytes 786440 | tf_op jit(solution)/shard_map/ppermute | solution.py:304
  18.0 26.9 %collective-permute-start.3 = (f32[256,256]{1,0:T(8,128)}, f32[256,256]{1,0:T(8,128)S(1)}, u32[]{:S(2)}, u32[]{:S(2)}) collective-permute-start(f32[256,256]{1,0:T(8,128)} %get-tuple-element.155), channel_id=1, source_target_pairs={{0,8},{2,10},{4,12},{6,14},{8,0},{10,2},{12,4},{14,6},{16,24},{18,... | collective-permute-start | bytes 786440 | tf_op jit(solution)/shard_map/ppermute | solution.py:304
  41.0 18.0 %collective-permute-start.7 = (f32[256,256]{1,0:T(8,128)}, f32[256,256]{1,0:T(8,128)S(1)}, u32[]{:S(2)}, u32[]{:S(2)}) collective-permute-start(f32[256,256]{1,0:T(8,128)} %get-tuple-element.163), channel_id=1, source_target_pairs={{0,10},{2,8},{4,14},{6,12},{8,2},{10,0},{12,6},{14,4},{16,26},{18,... | collective-permute-start | bytes 786440 | tf_op jit(solution)/shard_map/ppermute | solution.py:304
  41.0 18.0 %collective-permute-start.2 = (f32[256,256]{1,0:T(8,128)}, f32[256,256]{1,0:T(8,128)S(1)}, u32[]{:S(2)}, u32[]{:S(2)}) collective-permute-start(f32[256,256]{1,0:T(8,128)} %get-tuple-element.150), channel_id=1, source_target_pairs={{0,4},{2,6},{4,0},{6,2},{8,12},{10,14},{12,8},{14,10},{16,20},{18,... | collective-permute-start | bytes 786440 | tf_op jit(solution)/shard_map/ppermute | solution.py:304
  42.5 19.2 %collective-permute-start.10 = (f32[256,128]{1,0:T(8,128)}, f32[256,128]{1,0:T(8,128)}, u32[]{:S(2)}, u32[]{:S(2)}) collective-permute-start(f32[256,128]{1,0:T(8,128)} %get-tuple-element.172), channel_id=1, source_target_pairs={{0,28},{2,30},{4,24},{6,26},{8,20},{10,22},{12,16},{14,18},{16,12}... | collective-permute-start | bytes 393224 | tf_op jit(solution)/shard_map/ppermute | solution.py:304
  44.9 19.9 %collective-permute-start.4 = (f32[256,128]{1,0:T(8,128)}, f32[256,128]{1,0:T(8,128)}, u32[]{:S(2)}, u32[]{:S(2)}) collective-permute-start(f32[256,128]{1,0:T(8,128)} %get-tuple-element.156), channel_id=1, source_target_pairs={{0,18},{2,16},{4,22},{6,20},{8,26},{10,24},{12,30},{14,28},{16,2},... | collective-permute-start | bytes 393224 | tf_op jit(solution)/shard_map/ppermute | solution.py:304
  49.8 20.5 %collective-permute-start.13 = (f32[256,128]{1,0:T(8,128)}, f32[256,128]{1,0:T(8,128)S(1)}, u32[]{:S(2)}, u32[]{:S(2)}) collective-permute-start(f32[256,128]{1,0:T(8,128)} %get-tuple-element.182), channel_id=1, source_target_pairs={{0,22},{2,20},{4,18},{6,16},{8,30},{10,28},{12,26},{14,24},{16,6},... | collective-permute-start | bytes 393224 | tf_op jit(solution)/shard_map/ppermute | solution.py:304
  59.0 17.1 %collective-permute-start.12 = (f32[256,128]{1,0:T(8,128)}, f32[256,128]{1,0:T(8,128)S(1)}, u32[]{:S(2)}, u32[]{:S(2)}) collective-permute-start(f32[256,128]{1,0:T(8,128)} %get-tuple-element.179), channel_id=1, source_target_pairs={{0,20},{2,22},{4,16},{6,18},{8,28},{10,30},{12,24},{14,26},{16,4},... | collective-permute-start | bytes 393224 | tf_op jit(solution)/shard_map/ppermute | solution.py:304
  59.0 18.9 %collective-permute-start.14 = (f32[256,128]{1,0:T(8,128)}, f32[256,128]{1,0:T(8,128)S(1)}, u32[]{:S(2)}, u32[]{:S(2)}) collective-permute-start(f32[256,128]{1,0:T(8,128)} %get-tuple-element.188), channel_id=1, source_target_pairs={{0,30},{2,28},{4,26},{6,24},{8,22},{10,20},{12,18},{14,16},{16,14}... | collective-permute-start | bytes 393224 | tf_op jit(solution)/shard_map/ppermute | solution.py:304
  61.7 18.7 %collective-permute-start.11 = (f32[256,256]{1,0:T(8,128)}, f32[256,256]{1,0:T(8,128)S(1)}, u32[]{:S(2)}, u32[]{:S(2)}) collective-permute-start(f32[256,256]{1,0:T(8,128)} %get-tuple-element.173), channel_id=1, source_target_pairs={{0,14},{2,12},{4,10},{6,8},{8,6},{10,4},{12,2},{14,0},{16,30},{18,... | collective-permute-start | bytes 786440 | tf_op jit(solution)/shard_map/ppermute | solution.py:304
  64.8 24.5 %collective-permute-start.5 = (f32[256,256]{1,0:T(8,128)}, f32[256,256]{1,0:T(8,128)S(1)}, u32[]{:S(2)}, u32[]{:S(2)}) collective-permute-start(f32[256,256]{1,0:T(8,128)} %get-tuple-element.157), channel_id=1, source_target_pairs={{0,6},{2,4},{4,2},{6,0},{8,14},{10,12},{12,10},{14,8},{16,22},{18,... | collective-permute-start | bytes 786440 | tf_op jit(solution)/shard_map/ppermute | solution.py:304
  70.3 43.4 %collective-permute-start.21 = (f32[256,128]{1,0:T(8,128)}, f32[256,128]{1,0:T(8,128)S(1)}, u32[]{:S(2)}, u32[]{:S(2)}) collective-permute-start(f32[256,128]{1,0:T(8,128)} %get-tuple-element.209), channel_id=1, source_target_pairs={{0,28},{2,30},{4,24},{6,26},{8,20},{10,22},{12,16},{14,18},{16,12}... | collective-permute-start | bytes 393224 | tf_op jit(solution)/shard_map/ppermute | solution.py:304
  76.0 29.3 %collective-permute-start.17 = (f32[256,128]{1,0:T(8,128)}, f32[256,128]{1,0:T(8,128)S(1)}, u32[]{:S(2)}, u32[]{:S(2)}) collective-permute-start(f32[256,128]{1,0:T(8,128)} %get-tuple-element.198), channel_id=1, source_target_pairs={{0,24},{2,26},{4,28},{6,30},{8,16},{10,18},{12,20},{14,22},{16,8},... | collective-permute-start | bytes 393224 | tf_op jit(solution)/shard_map/ppermute | solution.py:304
  77.8 30.9 %collective-permute-start.19 = (f32[256,128]{1,0:T(8,128)}, f32[256,128]{1,0:T(8,128)S(1)}, u32[]{:S(2)}, u32[]{:S(2)}) collective-permute-start(f32[256,128]{1,0:T(8,128)} %get-tuple-element.203), channel_id=1, source_target_pairs={{0,26},{2,24},{4,30},{6,28},{8,18},{10,16},{12,22},{14,20},{16,10}... | collective-permute-start | bytes 393224 | tf_op jit(solution)/shard_map/ppermute | solution.py:304
  80.4 33.3 %collective-permute-start.16 = (f32[256,128]{1,0:T(8,128)S(1)}, f32[256,128]{1,0:T(8,128)S(1)}, u32[]{:S(2)}, u32[]{:S(2)}) collective-permute-start(f32[256,128]{1,0:T(8,128)S(1)} %copy-done.42), channel_id=1, source_target_pairs={{0,18},{2,16},{4,22},{6,20},{8,26},{10,24},{12,30},{14,28},{16,2},... | collective-permute-start | bytes 393224 | tf_op jit(solution)/shard_map/ppermute | solution.py:304
  89.3 19.5 %collective-permute-start.15 = (f32[256,128]{1,0:T(8,128)}, f32[256,128]{1,0:T(8,128)S(1)}, u32[]{:S(2)}, u32[]{:S(2)}) collective-permute-start(f32[256,128]{1,0:T(8,128)} %get-tuple-element.191), channel_id=1, source_target_pairs={{0,16},{2,18},{4,20},{6,22},{8,24},{10,26},{12,28},{14,30},{16,0},... | collective-permute-start | bytes 393224 | tf_op jit(solution)/shard_map/ppermute | solution.py:304
  108.7 19.2 %collective-permute-start.20 = (f32[256,128]{1,0:T(8,128)S(1)}, f32[256,128]{1,0:T(8,128)S(1)}, u32[]{:S(2)}, u32[]{:S(2)}) collective-permute-start(f32[256,128]{1,0:T(8,128)S(1)} %copy-done.40), channel_id=1, source_target_pairs={{0,22},{2,20},{4,18},{6,16},{8,30},{10,28},{12,26},{14,24},{16,6},... | collective-permute-start | bytes 393224 | tf_op jit(solution)/shard_map/ppermute | solution.py:304
  108.8 22.7 %collective-permute-start.22 = (f32[256,128]{1,0:T(8,128)S(1)}, f32[256,128]{1,0:T(8,128)S(1)}, u32[]{:S(2)}, u32[]{:S(2)}) collective-permute-start(f32[256,128]{1,0:T(8,128)S(1)} %copy-done.39), channel_id=1, source_target_pairs={{0,30},{2,28},{4,26},{6,24},{8,22},{10,20},{12,18},{14,16},{16,14}... | collective-permute-start | bytes 393224 | tf_op jit(solution)/shard_map/ppermute | solution.py:304
  113.7 34.7 %collective-permute-start.23 = (f32[256,128]{1,0:T(8,128)}, f32[256,128]{1,0:T(8,128)S(1)}, u32[]{:S(2)}, u32[]{:S(2)}) collective-permute-start(f32[256,128]{1,0:T(8,128)} %get-tuple-element.225), channel_id=1, source_target_pairs={{0,16},{2,18},{4,20},{6,22},{8,24},{10,26},{12,28},{14,30},{16,0},... | collective-permute-start | bytes 393224 | tf_op jit(solution)/shard_map/ppermute | solution.py:304
  122.1 29.7 %collective-permute-start.37 = (f32[256,128]{1,0:T(8,128)}, f32[256,128]{1,0:T(8,128)S(1)}, u32[]{:S(2)}, u32[]{:S(2)}) collective-permute-start(f32[256,128]{1,0:T(8,128)} %get-tuple-element.257), channel_id=1, source_target_pairs={{0,26},{2,24},{4,30},{6,28},{8,18},{10,16},{12,22},{14,20},{16,10}... | collective-permute-start | bytes 393224 | tf_op jit(solution)/shard_map/ppermute | solution.py:304
  127.9 28.4 %collective-permute-start.30 = (f32[256,128]{1,0:T(8,128)}, f32[256,128]{1,0:T(8,128)S(1)}, u32[]{:S(2)}, u32[]{:S(2)}) collective-permute-start(f32[256,128]{1,0:T(8,128)} %get-tuple-element.241), channel_id=1, source_target_pairs={{0,28},{2,30},{4,24},{6,26},{8,20},{10,22},{12,16},{14,18},{16,12}... | collective-permute-start | bytes 393224 | tf_op jit(solution)/shard_map/ppermute | solution.py:304
  129.2 27.0 %collective-permute-start.26 = (f32[256,128]{1,0:T(8,128)}, f32[256,128]{1,0:T(8,128)S(1)}, u32[]{:S(2)}, u32[]{:S(2)}) collective-permute-start(f32[256,128]{1,0:T(8,128)} %get-tuple-element.233), channel_id=1, source_target_pairs={{0,24},{2,26},{4,28},{6,30},{8,16},{10,18},{12,20},{14,22},{16,8},... | collective-permute-start | bytes 393224 | tf_op jit(solution)/shard_map/ppermute | solution.py:304
  151.8 17.5 %collective-permute-start.38 = (f32[256,128]{1,0:T(8,128)S(1)}, f32[256,128]{1,0:T(8,128)S(1)}, u32[]{:S(2)}, u32[]{:S(2)}) collective-permute-start(f32[256,128]{1,0:T(8,128)S(1)} %copy-done.44), channel_id=1, source_target_pairs={{0,22},{2,20},{4,18},{6,16},{8,30},{10,28},{12,26},{14,24},{16,6},... | collective-permute-start | bytes 393224 | tf_op jit(solution)/shard_map/ppermute | solution.py:304
  156.2 19.7 %collective-permute-start.27 = (f32[256,128]{1,0:T(8,128)S(1)}, f32[256,128]{1,0:T(8,128)S(1)}, u32[]{:S(2)}, u32[]{:S(2)}) collective-permute-start(f32[256,128]{1,0:T(8,128)S(1)} %copy-done.43), channel_id=1, source_target_pairs={{0,20},{2,22},{4,16},{6,18},{8,28},{10,30},{12,24},{14,26},{16,4},... | collective-permute-start | bytes 393224 | tf_op jit(solution)/shard_map/ppermute | solution.py:304
  156.3 31.1 %collective-permute-start.31 = (f32[256,256]{1,0:T(8,128)}, f32[256,256]{1,0:T(8,128)S(1)}, u32[]{:S(2)}, u32[]{:S(2)}) collective-permute-start(f32[256,256]{1,0:T(8,128)} %get-tuple-element.242), channel_id=1, source_target_pairs={{0,8},{2,10},{4,12},{6,14},{8,0},{10,2},{12,4},{14,6},{16,24},{18,... | collective-permute-start | bytes 786440 | tf_op jit(solution)/shard_map/ppermute | solution.py:304
  159.5 29.4 %collective-permute-start.25 = (f32[256,256]{1,0:T(8,128)}, f32[256,256]{1,0:T(8,128)S(1)}, u32[]{:S(2)}, u32[]{:S(2)}) collective-permute-start(f32[256,256]{1,0:T(8,128)} %get-tuple-element.227), channel_id=1, source_target_pairs={{0,2},{2,0},{4,6},{6,4},{8,10},{10,8},{12,14},{14,12},{16,18},{18,... | collective-permute-start | bytes 786440 | tf_op jit(solution)/shard_map/ppermute | solution.py:304
  183.3 22.5 %collective-permute-start.29 = (f32[256,256]{1,0:T(8,128)}, f32[256,256]{1,0:T(8,128)S(1)}, u32[]{:S(2)}, u32[]{:S(2)}) collective-permute-start(f32[256,256]{1,0:T(8,128)} %get-tuple-element.236), channel_id=1, source_target_pairs={{0,4},{2,6},{4,0},{6,2},{8,12},{10,14},{12,8},{14,10},{16,20},{18,... | collective-permute-start | bytes 786440 | tf_op jit(solution)/shard_map/ppermute | solution.py:304
  185.0 22.6 %collective-permute-start.36 = (f32[256,256]{1,0:T(8,128)}, f32[256,256]{1,0:T(8,128)S(1)}, u32[]{:S(2)}, u32[]{:S(2)}) collective-permute-start(f32[256,256]{1,0:T(8,128)} %get-tuple-element.251), channel_id=1, source_target_pairs={{0,10},{2,8},{4,14},{6,12},{8,2},{10,0},{12,6},{14,4},{16,26},{18,... | collective-permute-start | bytes 786440 | tf_op jit(solution)/shard_map/ppermute | solution.py:304
  185.1 30.2 %collective-permute-start.40 = (f32[256,256]{1,0:T(8,128)}, f32[256,256]{1,0:T(8,128)S(1)}, u32[]{:S(2)}, u32[]{:S(2)}) collective-permute-start(f32[256,256]{1,0:T(8,128)} %get-tuple-element.260), channel_id=1, source_target_pairs={{0,12},{2,14},{4,8},{6,10},{8,4},{10,6},{12,0},{14,2},{16,28},{18,... | collective-permute-start | bytes 786440 | tf_op jit(solution)/shard_map/ppermute | solution.py:304
  188.9 16.9 %collective-permute-start.41 = (f32[256,128]{1,0:T(8,128)}, f32[256,128]{1,0:T(8,128)S(1)}, u32[]{:S(2)}, u32[]{:S(2)}) collective-permute-start(f32[256,128]{1,0:T(8,128)} %get-tuple-element.263), channel_id=1, source_target_pairs={{0,28},{2,30},{4,24},{6,26},{8,20},{10,22},{12,16},{14,18},{16,12}... | collective-permute-start | bytes 393224 | tf_op jit(solution)/shard_map/ppermute | solution.py:304
  196.4 27.8 %collective-permute-start.33 = (f32[256,256]{1,0:T(8,128)}, f32[256,256]{1,0:T(8,128)S(1)}, u32[]{:S(2)}, u32[]{:S(2)}) collective-permute-start(f32[256,256]{1,0:T(8,128)} %get-tuple-element.244), channel_id=1, source_target_pairs={{0,6},{2,4},{4,2},{6,0},{8,14},{10,12},{12,10},{14,8},{16,22},{18,... | collective-permute-start | bytes 786440 | tf_op jit(solution)/shard_map/ppermute | solution.py:304
  205.8 18.4 %collective-permute-start.42 = (f32[256,256]{1,0:T(8,128)}, f32[256,256]{1,0:T(8,128)S(1)}, u32[]{:S(2)}, u32[]{:S(2)}) collective-permute-start(f32[256,256]{1,0:T(8,128)} %get-tuple-element.264), channel_id=1, source_target_pairs={{0,14},{2,12},{4,10},{6,8},{8,6},{10,4},{12,2},{14,0},{16,30},{18,... | collective-permute-start | bytes 786440 | tf_op jit(solution)/shard_map/ppermute | solution.py:304
  (67 other events, 1321.0 us)
where the time goes:
time: 229 us
  starting transfers between devices  100 us (44%)
  waiting for transfers between devices  70.9 us (31%)
  Pallas kernels  51.5 us (22%)
  local copies, waits for them, and re-layouts  5.09 us (2%)
    ppermute x46, starting transfers between devices, send(): lax.ppermute(block, 'cols', [(s, s ^ mask) for s in range(self.parts)])  100 us
    ppermute x46, waiting for transfers between devices, send(): lax.ppermute(block, 'cols', [(s, s ^ mask) for s in range(self.parts)])  70.9 us
    pallas_call x2, Pallas kernels, right_chain(): pl.pallas_call(functools.partial(right_body, parts, bool(before)), grid=(...  31.5 us
    pallas_call x1, Pallas kernels, left_chain(): pl.pallas_call(functools.partial(left_body, parts), grid=(rows // block,)...  15 us
    pallas_call x2, Pallas kernels, place(): pl.pallas_call(functools.partial(place_body, parts, spots, len(held)), in...  4.98 us
  transfers between devices with their start and end apart: 46, of which 18 were waited for; matrix products, arithmetic and copies ran while one was open for 1% of the time, Pallas kernels for 15%

commit v1 on v0

v1 whole, which is shorter than its diff:
```python
import functools
import jax
import jax.numpy as jnp
import ml_dtypes
import numpy as np
from jax import lax
from jax.experimental import pallas as pl
from jax.experimental.pallas import tpu as pltpu
from jax.sharding import PartitionSpec as P

LX = 64
LY = 64
SLICES = 3
hop_rate = 0.6
coupling = 0.65373
LANES = 128
TALL = 256
ROW_PAD = 8
PAIR_PAD = 8
UNROLL = 8
VMEM_LIMIT = 60 << 20
RIGHT_LIMIT = 24 << 20
IN_FLIGHT = 5
PATTERNS = ('nfnfnfnfnfnfnff', 'fnfnfnfnfnfnfnf', 'fnfnfnfnfnfnfnf', 'nfnfnfnfnfnfnff')
LATE = 5
AHEAD = 5
BF = jnp.bfloat16
F32 = jnp.float32


def circulant(length, growth):
    angles = 2.0 * np.pi * np.arange(length) / length
    column = np.cos(np.outer(np.arange(length), angles)) @ np.exp(growth * np.cos(angles)) / length
    differ = (np.arange(length)[:, None] - np.arange(length)[None, :]) % length
    return column[differ]


def split_matrix(matrix):
    high = matrix.astype(ml_dtypes.bfloat16)
    return high, (matrix - high.astype(np.float64)).astype(ml_dtypes.bfloat16)


def lane_side(matrix):
    high, low = split_matrix(np.kron(np.eye(LANES // matrix.shape[0]), matrix).T)
    return jnp.asarray(np.tile(np.concatenate([high, low], axis=1), (2, 1)))


def row_side(matrix):
    high, low = split_matrix(np.kron(np.eye(LANES // matrix.shape[0]), matrix))
    return jnp.asarray(np.tile(np.concatenate([high, low], axis=0), (1, 2)))


def halves(value):
    high = value.astype(BF)
    return high, (value - high.astype(F32)).astype(BF)


def mix_lanes(data, right):
    high, low = halves(data)
    both = jnp.dot(jnp.concatenate([high, low], axis=1), right, preferred_element_type=F32)
    return both[:, :LANES] + both[:, LANES:]


def mix_rows(left, data):
    high, low = halves(data)
    mid = data.shape[0] // 2
    stacked = jnp.concatenate(
        [jnp.concatenate([part[:mid], part[mid:]], axis=1) for part in (high, low)], axis=0
    )
    both = jnp.dot(left, stacked, preferred_element_type=F32)
    both = both[:mid] + both[mid:]
    return jnp.concatenate([both[:, :LANES], both[:, LANES:]], axis=0)


def swap_halves(first, second):
    low = lax.broadcasted_iota(jnp.int32, first.shape, 1) < LANES // 2
    return (
        jnp.where(low, first, pltpu.roll(second, LANES // 2, 1)),
        jnp.where(low, pltpu.roll(first, LANES // 2, 1), second),
    )


def partner(parts, mask):
    return lax.axis_index("cols").astype(jnp.int32) ^ mask


def left_body(parts, x_ref, field_ref, right_ref, left_ref, *rest):
    outs, gain_ref, work = rest[:-2], rest[-2], rest[-1]
    rows = x_ref.shape[0]

    @pl.when(pl.program_id(0) == 0)
    def _():
        gain = [jnp.exp(coupling * (2.0 * field_ref[moment].astype(F32) - 1.0)) for moment in range(SLICES)]
        for moment in range(SLICES):
            for c in range(LX // 2):
                row = jnp.broadcast_to(gain[moment][:, c * LANES : (c + 1) * LANES], (8, LANES))
                even, odd = swap_halves(row, row)
                gain_ref[moment, 2 * c : 2 * c + 1, :] = even[:1]
                gain_ref[moment, 2 * c + 1 : 2 * c + 2, :] = odd[:1]

    for group in range(rows // 16):
        for c in range(LX // 2):
            lanes = slice(c * LANES, (c + 1) * LANES)
            even, odd = swap_halves(x_ref[group * 16 : group * 16 + 8, lanes], x_ref[group * 16 + 8 : group * 16 + 16, lanes])
            work[pl.ds(group * 8 * (LX + PAIR_PAD) + 2 * c, 8, stride=LX + PAIR_PAD), :] = even
            work[pl.ds(group * 8 * (LX + PAIR_PAD) + 2 * c + 1, 8, stride=LX + PAIR_PAD), :] = odd
    for moment in range(SLICES):
        gain = jnp.concatenate([gain_ref[moment]] * (TALL // LX), axis=0)
        pairs = TALL // LX
        for part in (lambda data: mix_lanes(data * gain, right_ref[...]), lambda data: mix_rows(left_ref[...], data)):
            for top in range(0, rows // 2, pairs):
                spans = [slice((top + q) * (LX + PAIR_PAD), (top + q) * (LX + PAIR_PAD) + LX) for q in range(pairs)]
                data = part(jnp.concatenate([work[span, :] for span in spans], axis=0))
                for q, span in enumerate(spans):
                    work[span, :] = data[q * LX : (q + 1) * LX]
    for mask in range(parts):
        for half in range(2):
            ref = outs[half * parts + mask]
            start = partner(parts, mask) * (LX // parts) + 2 * half
            for group in range(rows // 16):
                even = work[pl.ds(group * 8 * (LX + PAIR_PAD) + start, 8, stride=LX + PAIR_PAD), :]
                odd = work[pl.ds(group * 8 * (LX + PAIR_PAD) + start + 1, 8, stride=LX + PAIR_PAD), :]
                above, below = swap_halves(even, odd)
                ref[group * 16 : group * 16 + 8, :] = above
                ref[group * 16 + 8 : group * 16 + 16, :] = below


def left_chain(parts, block, x, field, right, left):
    rows, sites = x.shape
    whole = lambda array: pl.BlockSpec(array.shape, lambda g: (0,) * array.ndim)
    outs = pl.pallas_call(
        functools.partial(left_body, parts),
        grid=(rows // block,),
        in_specs=[pl.BlockSpec((block, sites), lambda g: (g, 0)), whole(field), whole(right), whole(left)],
        out_specs=[pl.BlockSpec((block, LANES), lambda g: (g, 0))] * (2 * parts),
        out_shape=[jax.ShapeDtypeStruct((rows, LANES), F32)] * (2 * parts),
        scratch_shapes=[pltpu.VMEM((SLICES, LX, LANES), F32), pltpu.VMEM((block // 2 * (LX + PAIR_PAD), LANES), F32)],
        compiler_params=pltpu.CompilerParams(vmem_limit_bytes=VMEM_LIMIT),
        cost_estimate=pl.CostEstimate(flops=rows * sites * 256 * 2 * 6, bytes_accessed=rows * sites * 8, transcendentals=0),
        name="left_chain",
    )(x, field, right, left)
    return outs[:parts], outs[parts:]


def right_body(parts, loss_ref, left_y_ref, left_x_ref, *rest):
    pieces, outs, work = rest[:parts], rest[parts:-1], rest[-1]
    sites = loss_ref.shape[0]
    local = sites // parts

    def rows_of(mask):
        return pl.ds(pl.multiple_of(partner(parts, mask) * local, local), local)

    rows = local // LY
    tall = LY + ROW_PAD

    def span(x):
        start = x * tall
        return pl.ds(pl.multiple_of(start, 8) if ROW_PAD % 8 == 0 else start, LY)

    for mask in range(parts):
        for row in range(rows):
            work[span(partner(parts, mask) * rows + row), :] = pieces[mask][row * LY : (row + 1) * LY, :]
    step = TALL // LX
    for moment in range(SLICES):

        @pl.loop(0, sites // TALL // UNROLL)
        def _(turn):
            for q in range(UNROLL):
                x = (turn * UNROLL + q) * step
                data = jnp.concatenate([work[span(x + r), :] for r in range(step)], axis=0)
                loss = loss_ref[pl.ds(pl.multiple_of(x * LY, TALL), TALL), moment : moment + 1]
                data = mix_rows(left_y_ref[...], data * loss)
                for r in range(step):
                    work[span(x + r), :] = data[r * LY : (r + 1) * LY]

        @pl.loop(0, LY // step // UNROLL)
        def _(turn):
            for r in range(UNROLL):
                y = (turn * UNROLL + r) * step
                data = jnp.concatenate([work[pl.ds(y + q, LX, stride=tall), :] for q in range(step)], axis=0)
                data = mix_rows(left_x_ref[...], data)
                for q in range(step):
                    work[pl.ds(y + q, LX, stride=tall), :] = data[q * LX : (q + 1) * LX]

    for mask in range(parts):
        for row in range(rows):
            outs[mask][row * LY : (row + 1) * LY, :] = work[span(partner(parts, mask) * rows + row), :]


def right_chain(parts, loss, left_y, left_x, pieces):
    sites = loss.shape[0]
    whole = lambda array: pl.BlockSpec(array.shape, lambda g: (0,) * array.ndim)
    return pl.pallas_call(
        functools.partial(right_body, parts),
        grid=(1,),
        in_specs=[whole(loss), whole(left_y), whole(left_x)] + [whole(piece) for piece in pieces],
        out_specs=[whole(piece) for piece in pieces],
        out_shape=[jax.ShapeDtypeStruct(piece.shape, F32) for piece in pieces],
        scratch_shapes=[pltpu.VMEM((sites // LY * (LY + ROW_PAD), LANES), F32)],
        compiler_params=pltpu.CompilerParams(vmem_limit_bytes=RIGHT_LIMIT),
        cost_estimate=pl.CostEstimate(flops=sites * LANES * 256 * 2 * 6, bytes_accessed=sites * LANES * 12, transcendentals=0),
        name="right_chain",
    )(loss, left_y, left_x, *pieces)


def place_body(parts, lane, held, *rest):
    blocks, out, landed, came, went = rest[:parts], rest[parts + held], rest[-3], rest[-2], rest[-1]
    local = out.shape[1] // parts
    copies = []
    for mask in range(parts):
        start = pl.multiple_of(partner(parts, mask) * local + lane, LANES)
        copies.append((
            pltpu.make_async_copy(blocks[mask], landed.at[mask], came.at[mask]),
            pltpu.make_async_copy(landed.at[mask], out.at[:, pl.ds(start, LANES)], went.at[mask]),
        ))
    for copy, _ in copies:
        copy.start()
    for copy, onward in copies:
        copy.wait()
        onward.start()
    for _, onward in copies:
        onward.wait()


def place(parts, lane, blocks, held=None):
    rows = blocks[0].shape[0]
    held = [] if held is None else [held]
    anywhere = pl.BlockSpec(memory_space=pl.ANY)
    return pl.pallas_call(
        functools.partial(place_body, parts, lane, len(held)),
        in_specs=[anywhere] * (parts + len(held)),
        out_specs=anywhere,
        out_shape=jax.ShapeDtypeStruct((rows, rows * parts), F32),
        scratch_shapes=[pltpu.VMEM((parts, rows, LANES), F32)] + [pltpu.SemaphoreType.DMA((parts,))] * 2,
        input_output_aliases={parts: 0} if held else {},
        compiler_params=pltpu.CompilerParams(vmem_limit_bytes=VMEM_LIMIT),
        cost_estimate=pl.CostEstimate(flops=0, bytes_accessed=rows * LANES * parts * 8, transcendentals=0),
        name="place",
    )(*blocks, *held)


def kernel(length, growth):
    indices = jnp.arange(length, dtype=jnp.int32)
    phases = indices[:, None] * indices[None, :] % length
    angles = 2.0 * jnp.pi * phases.astype(jnp.float32) / length
    cosines = jnp.cos(angles)
    sines = jnp.sin(angles)
    spectrum = jnp.exp(growth * jnp.cos(2.0 * jnp.pi * indices.astype(jnp.float32) / length))
    highest = lax.Precision.HIGHEST
    total = jnp.dot(cosines * spectrum[None, :], cosines.T, precision=highest)
    total = total + jnp.dot(sines * spectrum[None, :], sines.T, precision=highest)
    return total / length


def whole_exchange(green_by_column, field):
    highest = lax.Precision.HIGHEST
    walkers, local_cols, sites = green_by_column.shape
    fwd_x = kernel(LX, hop_rate)
    fwd_y = kernel(LY, hop_rate)
    inv_x = kernel(LX, -hop_rate)
    inv_y = kernel(LY, -hop_rate)
    spins = 2.0 * field.astype(jnp.float32) - 1.0
    green = green_by_column
    for moment in range(SLICES):
        left_green = green
        left_green = left_green * jnp.exp(coupling * spins[:, moment, :])[:, None, :]
        left_blocks = left_green.reshape(walkers, local_cols, LX, LY)
        left_blocks = jnp.einsum("xa,wcab->wcxb", fwd_x, left_blocks, precision=highest)
        left_blocks = jnp.einsum("yb,wcxb->wcxy", fwd_y, left_blocks, precision=highest)
        green = left_blocks.reshape(walkers, local_cols, sites)
    parts = lax.axis_size("cols")
    shaped_in = green.reshape(walkers, local_cols, parts, sites // parts)
    row_block = lax.all_to_all(shaped_in, "cols", split_axis=2, concat_axis=1, tiled=True)
    count = row_block.shape[0]
    width = row_block.shape[3]
    blocks = row_block.reshape(count, sites, width)
    for moment in range(SLICES):
        blocks = blocks * jnp.exp(-coupling * spins[:, moment, :])[:, :, None]
        shaped = blocks.reshape(count, LX, LY, width)
        shaped = jnp.einsum("by,wabr->wayr", inv_y, shaped, precision=highest)
        shaped = jnp.einsum("ax,wayr->wxyr", inv_x, shaped, precision=highest)
        blocks = shaped.reshape(count, sites, width)
    rows_done = blocks.reshape(count, sites, 1, width)
    rows_done = rows_done.reshape(walkers, sites, sites // parts)
    green = lax.all_to_all(rows_done, "cols", split_axis=1, concat_axis=2, tiled=True)
    return green


class Links:
    def __init__(self, parts):
        self.parts = parts
        self.sent = []
        self.after = None

    def send(self, block, mask):
        hold = [self.after] if self.after is not None else []
        back = len(self.sent) - IN_FLIGHT
        if back >= 0:
            hold.append(self.sent[back]["value"])
        if hold:
            got = lax.optimization_barrier(tuple([block] + hold))
            block = got[0]
            if back >= 0:
                self.sent[back]["value"] = got[-1]
        value = lax.ppermute(block, "cols", [(s, s ^ mask) for s in range(self.parts)])
        self.sent.append({"value": value})
        return self.sent[-1]


def send_order(parts, pattern):
    far = [m for pair in zip(range(3 * parts // 4, parts), range(parts // 2, 3 * parts // 4)) for m in pair]
    near = [m for pair in zip(range(parts // 4, parts // 2), range(1, parts // 4 + 1)) for m in pair][: parts // 2 - 1]
    order = []
    for kind in pattern:
        side = far if kind == "f" else near
        if side:
            order.append(side.pop(0))
    return order + near + far


def pipelined(green_by_column, field):
    _, rows, sites = green_by_column.shape
    parts = lax.axis_size("cols")
    x = green_by_column.reshape(rows, sites)
    loss = jnp.exp(-coupling * (2.0 * field[0].astype(F32) - 1.0)).T
    right = lane_side(circulant(LY, hop_rate))
    left = row_side(circulant(LX, hop_rate))
    left_y = row_side(circulant(LY, -hop_rate))
    left_x = row_side(circulant(LX, -hop_rate))
    links = Links(parts)

    def chain(pieces):
        return right_chain(parts, loss, left_y, left_x, [pieces[mask]["value"] for mask in range(parts)])

    halves_ = left_chain(parts, rows // 4, x, field.transpose(1, 0, 2), right, left)
    sent = [{0: {"value": blocks[0]}} for blocks in halves_]
    done = []
    for h in range(2):
        for at, mask in enumerate(send_order(parts, PATTERNS[h])):
            if h == 1 and at == LATE:
                done.append(chain(sent[0]))
                links.after = done[0][0]
            sent[h][mask] = links.send(halves_[h][mask], mask)
    back = []
    for h in range(2):
        back.append({0: {"value": done[h][0]}})
        for at, mask in enumerate(send_order(parts, PATTERNS[2 + h])):
            if h == 0 and at == AHEAD:
                done.append(chain(sent[1]))
                links.after = done[1][0]
            back[h][mask] = links.send(done[h][mask], mask)
    result = None
    for h in range(2):
        result = place(parts, h * LANES, [back[h][mask]["value"] for mask in range(parts)], result)
    return result.reshape(green_by_column.shape)


def shards(green_by_column, field):
    walkers, rows, sites = green_by_column.shape
    parts = lax.axis_size("cols")
    fits = walkers == 1 and rows == 256 and rows * parts == sites and parts & (parts - 1) == 0 and parts >= 8
    if fits and LX * LY == sites and LX == LY == 64:
        return pipelined(green_by_column, field)
    return whole_exchange(green_by_column, field)


def solution(mesh):
    return jax.shard_map(
        shards,
        mesh=mesh,
        in_specs=(P("walk", "cols", None), P("walk", None, None)),
        out_specs=P("walk", "cols", None),
        check_vma=False,
    )
```

time: 229 us -> 210 us (0.917)
  Pallas kernels: 51.5 us -> 30.5 us
  starting transfers between devices: 100 us -> 118 us
  waiting for transfers between devices: 70.9 us -> 57.9 us
    pallas_call x4, Pallas kernels: 36.5 us -> 18.6 us  [the longest x2 13.4 us: right_chain(): pl.pallas_call(functools.partial(right_body, parts), grid=(1,), in_specs=...]
    ppermute x46 -> x60, starting transfers between devices: 100 us -> 118 us  [send(): lax.ppermute(block, 'cols', [(s, s ^ mask) for s in range(self.parts)])]
    ppermute x46 -> x60, waiting for transfers between devices: 70.9 us -> 57.9 us  [send(): lax.ppermute(block, 'cols', [(s, s ^ mask) for s in range(self.parts)])]
    pallas_call x1, Pallas kernels: 15 us -> 11.9 us  [left_chain(): pl.pallas_call(functools.partial(left_body, parts), grid=(rows // block,)...]
  transfers between devices with their start and end apart: 46 -> 60, of which waited for: 18 -> 17; matrix products, arithmetic and copies ran while one was open for 1% -> 0% of each run, Pallas kernels for 15% -> 8%
where the time goes in v1:
time: 210 us
  starting transfers between devices  118 us (56%)
  waiting for transfers between devices  57.9 us (28%)
  Pallas kernels  30.5 us (15%)
  local copies, waits for them, and re-layouts  3.01 us (1%)
    ppermute x60, starting transfers between devices, send(): lax.ppermute(block, 'cols', [(s, s ^ mask) for s in range(self.parts)])  118 us
    ppermute x60, waiting for transfers between devices, send(): lax.ppermute(block, 'cols', [(s, s ^ mask) for s in range(self.parts)])  57.9 us
    pallas_call x2, Pallas kernels, right_chain(): pl.pallas_call(functools.partial(right_body, parts), grid=(1,), in_specs=...  13.4 us
    pallas_call x1, Pallas kernels, left_chain(): pl.pallas_call(functools.partial(left_body, parts), grid=(rows // block,)...  11.9 us
    pallas_call x2, Pallas kernels, place(): pl.pallas_call(functools.partial(place_body, parts, lane, len(held)), in_...  5.15 us
  transfers between devices with their start and end apart: 60, of which 17 were waited for; matrix products, arithmetic and copies ran while one was open for 0% of the time, Pallas kernels for 8%

profile of v1, /device:TPU:0, one launch (start us, length us, event | category | flops | bytes accessed | tf_op | source)
XLA Modules:
  0.0 209.9 jit_solution(5869723695957463357)
XLA Ops:
  0.0 11.9 %left_chain.1 = (f32[256,128]{1,0:T(8,128)}, f32[256,128]{1,0:T(8,128)}, f32[256,128]{1,0:T(8,128)}, f32[256,128]{1,0:T(8,128)}, f32[256,128]{1,0:T(8,128)}, /*i...) custom-call(f32[256,4096]{1,0:T(8,128)} %bitcast.8, ...), custom_call_target="tpu_custom_call" | custom-call | flops 3221225472 | bytes 8388608 | tf_op jit(solution)/shard_map/left_chain/pallas_call | solution.py:131
  11.9 3.0 %collective-permute-start = (f32[256,128]{1,0:T(8,128)}, f32[256,128]{1,0:T(8,128)S(1)}, u32[]{:S(2)}, u32[]{:S(2)}) collective-permute-start(f32[256,128]{1,0:T(8,128)} %get-tuple-element.183), channel_id=1, source_target_pairs={{0,2},{2,0},{4,6},{6,4},{8,10},{10,8},{12,14},{14,12},{16,18},{18,... | collective-permute-start | bytes 393224 | tf_op jit(solution)/shard_map/ppermute | solution.py:305
  14.9 3.6 %collective-permute-start.1 = (f32[256,128]{1,0:T(8,128)}, f32[256,128]{1,0:T(8,128)S(1)}, u32[]{:S(2)}, u32[]{:S(2)}) collective-permute-start(f32[256,128]{1,0:T(8,128)} %get-tuple-element.187), channel_id=1, source_target_pairs={{0,24},{2,26},{4,28},{6,30},{8,16},{10,18},{12,20},{14,22},{16,8},... | collective-permute-start | bytes 393224 | tf_op jit(solution)/shard_map/ppermute | solution.py:305
  20.5 3.9 %collective-permute-start.9 = (f32[256,128]{1,0:T(8,128)}, f32[256,128]{1,0:T(8,128)S(1)}, u32[]{:S(2)}, u32[]{:S(2)}) collective-permute-start(f32[256,128]{1,0:T(8,128)} %get-tuple-element.208), channel_id=1, source_target_pairs={{0,18},{2,16},{4,22},{6,20},{8,26},{10,24},{12,30},{14,28},{16,2},... | collective-permute-start | bytes 393224 | tf_op jit(solution)/shard_map/ppermute | solution.py:305
  25.9 3.6 %collective-permute-done.3.rest_4_ = f32[256,128]{1,0:T(8,128)S(1)} collective-permute-done((f32[256,128]{1,0:T(8,128)}, f32[256,128]{1,0:T(8,128)S(1)}, u32[]{:S(2)}, u32[]{:S(2)}) %collective-permute-start.3) | collective-permute-done | bytes 131104 | tf_op jit(solution)/shard_map/ppermute | solution.py:305
  29.5 3.2 %collective-permute-start.4 = (f32[256,128]{1,0:T(8,128)}, f32[256,128]{1,0:T(8,128)S(1)}, u32[]{:S(2)}, u32[]{:S(2)}) collective-permute-start(f32[256,128]{1,0:T(8,128)} %get-tuple-element.194), channel_id=1, source_target_pairs={{0,26},{2,24},{4,30},{6,28},{8,18},{10,16},{12,22},{14,20},{16,10}... | collective-permute-start | bytes 393224 | tf_op jit(solution)/shard_map/ppermute | solution.py:305
  35.0 2.9 %collective-permute-done.7.rest_8_ = f32[256,128]{1,0:T(8,128)S(1)} collective-permute-done((f32[256,128]{1,0:T(8,128)}, f32[256,128]{1,0:T(8,128)S(1)}, u32[]{:S(2)}, u32[]{:S(2)}) %collective-permute-start.7) | collective-permute-done | bytes 131104 | tf_op jit(solution)/shard_map/ppermute | solution.py:305
  38.7 4.0 %collective-permute-done.9.rest_9_ = f32[256,128]{1,0:T(8,128)S(1)} collective-permute-done((f32[256,128]{1,0:T(8,128)}, f32[256,128]{1,0:T(8,128)S(1)}, u32[]{:S(2)}, u32[]{:S(2)}) %collective-permute-start.9) | collective-permute-done | bytes 131104 | tf_op jit(solution)/shard_map/ppermute | solution.py:305
  42.7 3.8 %collective-permute-start.11 = (f32[256,128]{1,0:T(8,128)}, f32[256,128]{1,0:T(8,128)S(1)}, u32[]{:S(2)}, u32[]{:S(2)}) collective-permute-start(f32[256,128]{1,0:T(8,128)} %get-tuple-element.214), channel_id=1, source_target_pairs={{0,20},{2,22},{4,16},{6,18},{8,28},{10,30},{12,24},{14,26},{16,4},... | collective-permute-start | bytes 393224 | tf_op jit(solution)/shard_map/ppermute | solution.py:305
  47.8 7.1 %collective-permute-start.13 = (f32[256,128]{1,0:T(8,128)}, f32[256,128]{1,0:T(8,128)S(1)}, u32[]{:S(2)}, u32[]{:S(2)}) collective-permute-start(f32[256,128]{1,0:T(8,128)} %get-tuple-element.219), channel_id=1, source_target_pairs={{0,22},{2,20},{4,18},{6,16},{8,30},{10,28},{12,26},{14,24},{16,6},... | collective-permute-start | bytes 393224 | tf_op jit(solution)/shard_map/ppermute | solution.py:305
  54.9 5.1 %collective-permute-start.14 = (f32[256,128]{1,0:T(8,128)}, f32[256,128]{1,0:T(8,128)S(1)}, u32[]{:S(2)}, u32[]{:S(2)}) collective-permute-start(f32[256,128]{1,0:T(8,128)} %get-tuple-element.225), channel_id=1, source_target_pairs={{0,30},{2,28},{4,26},{6,24},{8,22},{10,20},{12,18},{14,16},{16,14}... | collective-permute-start | bytes 393224 | tf_op jit(solution)/shard_map/ppermute | solution.py:305
  62.0 2.9 %collective-permute-start.21 = (f32[256,128]{1,0:T(8,128)S(1)}, f32[256,128]{1,0:T(8,128)S(1)}, u32[]{:S(2)}, u32[]{:S(2)}) collective-permute-start(f32[256,128]{1,0:T(8,128)S(1)} %copy-done.48), channel_id=1, source_target_pairs={{0,24},{2,26},{4,28},{6,30},{8,16},{10,18},{12,20},{14,22},{16,8},... | collective-permute-start | bytes 393224 | tf_op jit(solution)/shard_map/ppermute | solution.py:305
  64.8 4.9 %collective-permute-done.13.rest_11_ = f32[256,128]{1,0:T(8,128)S(1)} collective-permute-done((f32[256,128]{1,0:T(8,128)}, f32[256,128]{1,0:T(8,128)S(1)}, u32[]{:S(2)}, u32[]{:S(2)}) %collective-permute-start.13) | collective-permute-done | bytes 131104 | tf_op jit(solution)/shard_map/ppermute | solution.py:305
  69.7 3.6 %collective-permute-start.23 = (f32[256,128]{1,0:T(8,128)S(1)}, f32[256,128]{1,0:T(8,128)S(1)}, u32[]{:S(2)}, u32[]{:S(2)}) collective-permute-start(f32[256,128]{1,0:T(8,128)S(1)} %copy-done.47), channel_id=1, source_target_pairs={{0,26},{2,24},{4,30},{6,28},{8,18},{10,16},{12,22},{14,20},{16,10}... | collective-permute-start | bytes 393224 | tf_op jit(solution)/shard_map/ppermute | solution.py:305
  73.5 6.6 %right_chain.2 = (f32[256,128]{1,0:T(8,128)S(1)}, f32[256,128]{1,0:T(8,128)S(1)}, f32[256,128]{1,0:T(8,128)S(1)}, f32[256,128]{1,0:T(8,128)S(1)}, f32[256,128]{1...) custom-call(f32[4096,3]{1,0:T(8,128)S(1)} %exponential_bitcast_fusio, ...), custom_call_target="tpu_custom_call" | custom-call | flops 1610612736 | bytes 6291456 | tf_op jit(solution)/shard_map/right_chain/pallas_call | solution.py:193
  96.6 3.0 %collective-permute-start.28 = (f32[256,128]{1,0:T(8,128)S(1)}, f32[256,128]{1,0:T(8,128)S(1)}, u32[]{:S(2)}, u32[]{:S(2)}) collective-permute-start(f32[256,128]{1,0:T(8,128)S(1)} %copy-done.37), channel_id=1, source_target_pairs={{0,22},{2,20},{4,18},{6,16},{8,30},{10,28},{12,26},{14,24},{16,6},... | collective-permute-start | bytes 393224 | tf_op jit(solution)/shard_map/ppermute | solution.py:305
  102.4 3.8 %collective-permute-start.26 = (f32[256,128]{1,0:T(8,128)S(1)}, f32[256,128]{1,0:T(8,128)S(1)}, u32[]{:S(2)}, u32[]{:S(2)}) collective-permute-start(f32[256,128]{1,0:T(8,128)S(1)} %copy-done.36), channel_id=1, source_target_pairs={{0,14},{2,12},{4,10},{6,8},{8,6},{10,4},{12,2},{14,0},{16,30},{18,... | collective-permute-start | bytes 393224 | tf_op jit(solution)/shard_map/ppermute | solution.py:305
  106.2 6.1 %collective-permute-start.30 = (f32[256,128]{1,0:T(8,128)S(1)}, f32[256,128]{1,0:T(8,128)S(1)}, u32[]{:S(2)}, u32[]{:S(2)}) collective-permute-start(f32[256,128]{1,0:T(8,128)S(1)} %get-tuple-element.277), channel_id=1, source_target_pairs={{0,16},{2,18},{4,20},{6,22},{8,24},{10,26},{12,28},{14,30},{16,0},... | collective-permute-start | bytes 393224 | tf_op jit(solution)/shard_map/ppermute | solution.py:305
  116.2 6.5 %collective-permute-done.28.rest_11_ = f32[256,128]{1,0:T(8,128)S(1)} collective-permute-done((f32[256,128]{1,0:T(8,128)S(1)}, f32[256,128]{1,0:T(8,128)S(1)}, u32[]{:S(2)}, u32[]{:S(2)}) %collective-permute-start.28) | collective-permute-done | bytes 131104 | tf_op jit(solution)/shard_map/ppermute | solution.py:305
  122.8 2.7 %collective-permute-start.45 = (f32[256,128]{1,0:T(8,128)S(1)}, f32[256,128]{1,0:T(8,128)S(1)}, u32[]{:S(2)}, u32[]{:S(2)}) collective-permute-start(f32[256,128]{1,0:T(8,128)S(1)} %get-tuple-element.309), channel_id=1, source_target_pairs={{0,26},{2,24},{4,30},{6,28},{8,18},{10,16},{12,22},{14,20},{16,10}... | collective-permute-start | bytes 393224 | tf_op jit(solution)/shard_map/ppermute | solution.py:305
  125.5 6.8 %right_chain.3 = (f32[256,128]{1,0:T(8,128)S(1)}, f32[256,128]{1,0:T(8,128)S(1)}, f32[256,128]{1,0:T(8,128)S(1)}, f32[256,128]{1,0:T(8,128)S(1)}, f32[256,128]{1...) custom-call(f32[4096,3]{1,0:T(8,128)S(1)} %exponential_bitcast_fusio, ...), custom_call_target="tpu_custom_call" | custom-call | flops 1610612736 | bytes 6291456 | tf_op jit(solution)/shard_map/right_chain/pallas_call | solution.py:193
  133.6 3.5 %collective-permute-start.40 = (f32[256,128]{1,0:T(8,128)S(1)}, f32[256,128]{1,0:T(8,128)S(1)}, u32[]{:S(2)}, u32[]{:S(2)}) collective-permute-start(f32[256,128]{1,0:T(8,128)S(1)} %get-tuple-element.299), channel_id=1, source_target_pairs={{0,10},{2,8},{4,14},{6,12},{8,2},{10,0},{12,6},{14,4},{16,26},{18,... | collective-permute-start | bytes 393224 | tf_op jit(solution)/shard_map/ppermute | solution.py:305
  143.3 2.8 %collective-permute-done.35.rest_9_ = f32[256,128]{1,0:T(8,128)S(1)} collective-permute-done((f32[256,128]{1,0:T(8,128)S(1)}, f32[256,128]{1,0:T(8,128)S(1)}, u32[]{:S(2)}, u32[]{:S(2)}) %collective-permute-start.35) | collective-permute-done | bytes 131104 | tf_op jit(solution)/shard_map/ppermute | solution.py:305
  147.3 5.8 %collective-permute-done.46.rest_6_ = f32[256,128]{1,0:T(8,128)S(1)} collective-permute-done((f32[256,128]{1,0:T(8,128)S(1)}, f32[256,128]{1,0:T(8,128)S(1)}, u32[]{:S(2)}, u32[]{:S(2)}) %collective-permute-start.46) | collective-permute-done | bytes 131104 | tf_op jit(solution)/shard_map/ppermute | solution.py:305
  153.1 3.3 %collective-permute-start.51 = (f32[256,128]{1,0:T(8,128)S(1)}, f32[256,128]{1,0:T(8,128)S(1)}, u32[]{:S(2)}, u32[]{:S(2)}) collective-permute-start(f32[256,128]{1,0:T(8,128)S(1)} %get-tuple-element.321), channel_id=1, source_target_pairs={{0,14},{2,12},{4,10},{6,8},{8,6},{10,4},{12,2},{14,0},{16,30},{18,... | collective-permute-start | bytes 393224 | tf_op jit(solution)/shard_map/ppermute | solution.py:305
  160.8 8.8 %collective-permute-done.47.rest_11_ = f32[256,128]{1,0:T(8,128)S(1)} collective-permute-done((f32[256,128]{1,0:T(8,128)S(1)}, f32[256,128]{1,0:T(8,128)S(1)}, u32[]{:S(2)}, u32[]{:S(2)}) %collective-permute-start.47) | collective-permute-done | bytes 131104 | tf_op jit(solution)/shard_map/ppermute | solution.py:305
  169.6 3.0 %collective-permute-start.52 = (f32[256,128]{1,0:T(8,128)S(1)}, f32[256,128]{1,0:T(8,128)S(1)}, u32[]{:S(2)}, u32[]{:S(2)}) collective-permute-start(f32[256,128]{1,0:T(8,128)S(1)} %get-tuple-element.322), channel_id=1, source_target_pairs={{0,16},{2,18},{4,20},{6,22},{8,24},{10,26},{12,28},{14,30},{16,0},... | collective-permute-start | bytes 393224 | tf_op jit(solution)/shard_map/ppermute | solution.py:305
  177.6 5.0 %collective-permute-start.57 = (f32[256,128]{1,0:T(8,128)S(1)}, f32[256,128]{1,0:T(8,128)S(1)}, u32[]{:S(2)}, u32[]{:S(2)}) collective-permute-start(f32[256,128]{1,0:T(8,128)S(1)} %get-tuple-element.332), channel_id=1, source_target_pairs={{0,28},{2,30},{4,24},{6,26},{8,20},{10,22},{12,16},{14,18},{16,12}... | collective-permute-start | bytes 393224 | tf_op jit(solution)/shard_map/ppermute | solution.py:305
  182.7 3.2 %collective-permute-start.53 = (f32[256,128]{1,0:T(8,128)S(1)}, f32[256,128]{1,0:T(8,128)S(1)}, u32[]{:S(2)}, u32[]{:S(2)}) collective-permute-start(f32[256,128]{1,0:T(8,128)S(1)} %get-tuple-element.323), channel_id=1, source_target_pairs={{0,12},{2,14},{4,8},{6,10},{8,4},{10,6},{12,0},{14,2},{16,28},{18,... | collective-permute-start | bytes 393224 | tf_op jit(solution)/shard_map/ppermute | solution.py:305
  185.9 5.2 %collective-permute-done.54.rest_9_ = f32[256,128]{1,0:T(8,128)S(1)} collective-permute-done((f32[256,128]{1,0:T(8,128)S(1)}, f32[256,128]{1,0:T(8,128)S(1)}, u32[]{:S(2)}, u32[]{:S(2)}) %collective-permute-start.54) | collective-permute-done | bytes 131104 | tf_op jit(solution)/shard_map/ppermute | solution.py:305
  191.2 3.8 %collective-permute-start.56 = (f32[256,128]{1,0:T(8,128)S(1)}, f32[256,128]{1,0:T(8,128)S(1)}, u32[]{:S(2)}, u32[]{:S(2)}) collective-permute-start(f32[256,128]{1,0:T(8,128)S(1)} %get-tuple-element.330), channel_id=1, source_target_pairs={{0,20},{2,22},{4,16},{6,18},{8,28},{10,30},{12,24},{14,26},{16,4},... | collective-permute-start | bytes 393224 | tf_op jit(solution)/shard_map/ppermute | solution.py:305
  197.8 3.1 %collective-permute-start.59 = (f32[256,128]{1,0:T(8,128)S(1)}, f32[256,128]{1,0:T(8,128)S(1)}, u32[]{:S(2)}, u32[]{:S(2)}) collective-permute-start(f32[256,128]{1,0:T(8,128)S(1)} %get-tuple-element.337), channel_id=1, source_target_pairs={{0,30},{2,28},{4,26},{6,24},{8,22},{10,20},{12,18},{14,16},{16,14}... | collective-permute-start | bytes 393224 | tf_op jit(solution)/shard_map/ppermute | solution.py:305
  (198 shorter events, 62.7 us)
Async XLA Ops:
  20.5 17.5 %collective-permute-start.7 = (f32[256,128]{1,0:T(8,128)}, f32[256,128]{1,0:T(8,128)S(1)}, u32[]{:S(2)}, u32[]{:S(2)}) collective-permute-start(f32[256,128]{1,0:T(8,128)} %get-tuple-element.203), channel_id=1, source_target_pairs={{0,16},{2,18},{4,20},{6,22},{8,24},{10,26},{12,28},{14,30},{16,0},... | collective-permute-start | bytes 393224 | tf_op jit(solution)/shard_map/ppermute | solution.py:305
  20.5 22.2 %collective-permute-start.9 = (f32[256,128]{1,0:T(8,128)}, f32[256,128]{1,0:T(8,128)S(1)}, u32[]{:S(2)}, u32[]{:S(2)}) collective-permute-start(f32[256,128]{1,0:T(8,128)} %get-tuple-element.208), channel_id=1, source_target_pairs={{0,18},{2,16},{4,22},{6,20},{8,26},{10,24},{12,30},{14,28},{16,2},... | collective-permute-start | bytes 393224 | tf_op jit(solution)/shard_map/ppermute | solution.py:305
  24.3 18.3 %collective-permute-start.2 = (f32[256,128]{1,0:T(8,128)}, f32[256,128]{1,0:T(8,128)S(1)}, u32[]{:S(2)}, u32[]{:S(2)}) collective-permute-start(f32[256,128]{1,0:T(8,128)} %get-tuple-element.188), channel_id=1, source_target_pairs={{0,4},{2,6},{4,0},{6,2},{8,12},{10,14},{12,8},{14,10},{16,20},{18,... | collective-permute-start | bytes 393224 | tf_op jit(solution)/shard_map/ppermute | solution.py:305
  29.5 17.0 %collective-permute-start.4 = (f32[256,128]{1,0:T(8,128)}, f32[256,128]{1,0:T(8,128)S(1)}, u32[]{:S(2)}, u32[]{:S(2)}) collective-permute-start(f32[256,128]{1,0:T(8,128)} %get-tuple-element.194), channel_id=1, source_target_pairs={{0,26},{2,24},{4,30},{6,28},{8,18},{10,16},{12,22},{14,20},{16,10}... | collective-permute-start | bytes 393224 | tf_op jit(solution)/shard_map/ppermute | solution.py:305
  37.9 16.9 %collective-permute-start.8 = (f32[256,128]{1,0:T(8,128)}, f32[256,128]{1,0:T(8,128)S(1)}, u32[]{:S(2)}, u32[]{:S(2)}) collective-permute-start(f32[256,128]{1,0:T(8,128)} %get-tuple-element.204), channel_id=1, source_target_pairs={{0,12},{2,14},{4,8},{6,10},{8,4},{10,6},{12,0},{14,2},{16,28},{18,... | collective-permute-start | bytes 393224 | tf_op jit(solution)/shard_map/ppermute | solution.py:305
  42.6 17.7 %collective-permute-start.10 = (f32[256,128]{1,0:T(8,128)}, f32[256,128]{1,0:T(8,128)S(1)}, u32[]{:S(2)}, u32[]{:S(2)}) collective-permute-start(f32[256,128]{1,0:T(8,128)} %get-tuple-element.209), channel_id=1, source_target_pairs={{0,14},{2,12},{4,10},{6,8},{8,6},{10,4},{12,2},{14,0},{16,30},{18,... | collective-permute-start | bytes 393224 | tf_op jit(solution)/shard_map/ppermute | solution.py:305
  42.7 19.3 %collective-permute-start.11 = (f32[256,128]{1,0:T(8,128)}, f32[256,128]{1,0:T(8,128)S(1)}, u32[]{:S(2)}, u32[]{:S(2)}) collective-permute-start(f32[256,128]{1,0:T(8,128)} %get-tuple-element.214), channel_id=1, source_target_pairs={{0,20},{2,22},{4,16},{6,18},{8,28},{10,30},{12,24},{14,26},{16,4},... | collective-permute-start | bytes 393224 | tf_op jit(solution)/shard_map/ppermute | solution.py:305
  46.4 15.5 %collective-permute-start.5 = (f32[256,128]{1,0:T(8,128)}, f32[256,128]{1,0:T(8,128)S(1)}, u32[]{:S(2)}, u32[]{:S(2)}) collective-permute-start(f32[256,128]{1,0:T(8,128)} %get-tuple-element.195), channel_id=1, source_target_pairs={{0,6},{2,4},{4,2},{6,0},{8,14},{10,12},{12,10},{14,8},{16,22},{18,... | collective-permute-start | bytes 393224 | tf_op jit(solution)/shard_map/ppermute | solution.py:305
  47.8 21.9 %collective-permute-start.13 = (f32[256,128]{1,0:T(8,128)}, f32[256,128]{1,0:T(8,128)S(1)}, u32[]{:S(2)}, u32[]{:S(2)}) collective-permute-start(f32[256,128]{1,0:T(8,128)} %get-tuple-element.219), channel_id=1, source_target_pairs={{0,22},{2,20},{4,18},{6,16},{8,30},{10,28},{12,26},{14,24},{16,6},... | collective-permute-start | bytes 393224 | tf_op jit(solution)/shard_map/ppermute | solution.py:305
  54.9 18.4 %collective-permute-start.14 = (f32[256,128]{1,0:T(8,128)}, f32[256,128]{1,0:T(8,128)S(1)}, u32[]{:S(2)}, u32[]{:S(2)}) collective-permute-start(f32[256,128]{1,0:T(8,128)} %get-tuple-element.225), channel_id=1, source_target_pairs={{0,30},{2,28},{4,26},{6,24},{8,22},{10,20},{12,18},{14,16},{16,14}... | collective-permute-start | bytes 393224 | tf_op jit(solution)/shard_map/ppermute | solution.py:305
  60.4 20.4 %collective-permute-start.16 = (f32[256,128]{1,0:T(8,128)S(1)}, f32[256,128]{1,0:T(8,128)S(1)}, u32[]{:S(2)}, u32[]{:S(2)}) collective-permute-start(f32[256,128]{1,0:T(8,128)S(1)} %copy-done.50), channel_id=1, source_target_pairs={{0,16},{2,18},{4,20},{6,22},{8,24},{10,26},{12,28},{14,30},{16,0},... | collective-permute-start | bytes 393224 | tf_op jit(solution)/shard_map/ppermute | solution.py:305
  61.9 20.7 %collective-permute-start.18 = (f32[256,128]{1,0:T(8,128)S(1)}, f32[256,128]{1,0:T(8,128)S(1)}, u32[]{:S(2)}, u32[]{:S(2)}) collective-permute-start(f32[256,128]{1,0:T(8,128)S(1)} %copy-done.49), channel_id=1, source_target_pairs={{0,8},{2,10},{4,12},{6,14},{8,0},{10,2},{12,4},{14,6},{16,24},{18,... | collective-permute-start | bytes 393224 | tf_op jit(solution)/shard_map/ppermute | solution.py:305
  62.0 22.9 %collective-permute-start.21 = (f32[256,128]{1,0:T(8,128)S(1)}, f32[256,128]{1,0:T(8,128)S(1)}, u32[]{:S(2)}, u32[]{:S(2)}) collective-permute-start(f32[256,128]{1,0:T(8,128)S(1)} %copy-done.48), channel_id=1, source_target_pairs={{0,24},{2,26},{4,28},{6,30},{8,16},{10,18},{12,20},{14,22},{16,8},... | collective-permute-start | bytes 393224 | tf_op jit(solution)/shard_map/ppermute | solution.py:305
  69.7 15.8 %collective-permute-start.23 = (f32[256,128]{1,0:T(8,128)S(1)}, f32[256,128]{1,0:T(8,128)S(1)}, u32[]{:S(2)}, u32[]{:S(2)}) collective-permute-start(f32[256,128]{1,0:T(8,128)S(1)} %copy-done.47), channel_id=1, source_target_pairs={{0,26},{2,24},{4,30},{6,28},{8,18},{10,16},{12,22},{14,20},{16,10}... | collective-permute-start | bytes 393224 | tf_op jit(solution)/shard_map/ppermute | solution.py:305
  90.3 15.9 %collective-permute-start.29 = (f32[256,128]{1,0:T(8,128)S(1)}, f32[256,128]{1,0:T(8,128)S(1)}, u32[]{:S(2)}, u32[]{:S(2)}) collective-permute-start(f32[256,128]{1,0:T(8,128)S(1)} %copy-done.40), channel_id=1, source_target_pairs={{0,30},{2,28},{4,26},{6,24},{8,22},{10,20},{12,18},{14,16},{16,14}... | collective-permute-start | bytes 393224 | tf_op jit(solution)/shard_map/ppermute | solution.py:305
  94.4 17.9 %collective-permute-start.20 = (f32[256,128]{1,0:T(8,128)S(1)}, f32[256,128]{1,0:T(8,128)S(1)}, u32[]{:S(2)}, u32[]{:S(2)}) collective-permute-start(f32[256,128]{1,0:T(8,128)S(1)} %copy-done.39), channel_id=1, source_target_pairs={{0,6},{2,4},{4,2},{6,0},{8,14},{10,12},{12,10},{14,8},{16,22},{18,... | collective-permute-start | bytes 393224 | tf_op jit(solution)/shard_map/ppermute | solution.py:305
  95.9 18.6 %collective-permute-start.27 = (f32[256,128]{1,0:T(8,128)S(1)}, f32[256,128]{1,0:T(8,128)S(1)}, u32[]{:S(2)}, u32[]{:S(2)}) collective-permute-start(f32[256,128]{1,0:T(8,128)S(1)} %copy-done.38), channel_id=1, source_target_pairs={{0,20},{2,22},{4,16},{6,18},{8,28},{10,30},{12,24},{14,26},{16,4},... | collective-permute-start | bytes 393224 | tf_op jit(solution)/shard_map/ppermute | solution.py:305
  96.6 26.2 %collective-permute-start.28 = (f32[256,128]{1,0:T(8,128)S(1)}, f32[256,128]{1,0:T(8,128)S(1)}, u32[]{:S(2)}, u32[]{:S(2)}) collective-permute-start(f32[256,128]{1,0:T(8,128)S(1)} %copy-done.37), channel_id=1, source_target_pairs={{0,22},{2,20},{4,18},{6,16},{8,30},{10,28},{12,26},{14,24},{16,6},... | collective-permute-start | bytes 393224 | tf_op jit(solution)/shard_map/ppermute | solution.py:305
  102.4 23.1 %collective-permute-start.26 = (f32[256,128]{1,0:T(8,128)S(1)}, f32[256,128]{1,0:T(8,128)S(1)}, u32[]{:S(2)}, u32[]{:S(2)}) collective-permute-start(f32[256,128]{1,0:T(8,128)S(1)} %copy-done.36), channel_id=1, source_target_pairs={{0,14},{2,12},{4,10},{6,8},{8,6},{10,4},{12,2},{14,0},{16,30},{18,... | collective-permute-start | bytes 393224 | tf_op jit(solution)/shard_map/ppermute | solution.py:305
  106.2 26.8 %collective-permute-start.30 = (f32[256,128]{1,0:T(8,128)S(1)}, f32[256,128]{1,0:T(8,128)S(1)}, u32[]{:S(2)}, u32[]{:S(2)}) collective-permute-start(f32[256,128]{1,0:T(8,128)S(1)} %get-tuple-element.277), channel_id=1, source_target_pairs={{0,16},{2,18},{4,20},{6,22},{8,24},{10,26},{12,28},{14,30},{16,0},... | collective-permute-start | bytes 393224 | tf_op jit(solution)/shard_map/ppermute | solution.py:305
  112.3 21.2 %collective-permute-start.34 = (f32[256,128]{1,0:T(8,128)S(1)}, f32[256,128]{1,0:T(8,128)S(1)}, u32[]{:S(2)}, u32[]{:S(2)}) collective-permute-start(f32[256,128]{1,0:T(8,128)S(1)} %get-tuple-element.287), channel_id=1, source_target_pairs={{0,8},{2,10},{4,12},{6,14},{8,0},{10,2},{12,4},{14,6},{16,24},{18,... | collective-permute-start | bytes 393224 | tf_op jit(solution)/shard_map/ppermute | solution.py:305
  114.4 19.1 %collective-permute-start.39 = (f32[256,128]{1,0:T(8,128)S(1)}, f32[256,128]{1,0:T(8,128)S(1)}, u32[]{:S(2)}, u32[]{:S(2)}) collective-permute-start(f32[256,128]{1,0:T(8,128)S(1)} %get-tuple-element.298), channel_id=1, source_target_pairs={{0,24},{2,26},{4,28},{6,30},{8,16},{10,18},{12,20},{14,22},{16,8},... | collective-permute-start | bytes 393224 | tf_op jit(solution)/shard_map/ppermute | solution.py:305
  137.1 16.0 %collective-permute-start.46 = (f32[256,128]{1,0:T(8,128)S(1)}, f32[256,128]{1,0:T(8,128)S(1)}, u32[]{:S(2)}, u32[]{:S(2)}) collective-permute-start(f32[256,128]{1,0:T(8,128)S(1)} %get-tuple-element.310), channel_id=1, source_target_pairs={{0,12},{2,14},{4,8},{6,10},{8,4},{10,6},{12,0},{14,2},{16,28},{18,... | collective-permute-start | bytes 393224 | tf_op jit(solution)/shard_map/ppermute | solution.py:305
  140.8 15.6 %collective-permute-start.32 = (f32[256,128]{1,0:T(8,128)S(1)}, f32[256,128]{1,0:T(8,128)S(1)}, u32[]{:S(2)}, u32[]{:S(2)}) collective-permute-start(f32[256,128]{1,0:T(8,128)S(1)} %get-tuple-element.279), channel_id=1, source_target_pairs={{0,30},{2,28},{4,26},{6,24},{8,22},{10,20},{12,18},{14,16},{16,14}... | collective-permute-start | bytes 393224 | tf_op jit(solution)/shard_map/ppermute | solution.py:305
  153.1 16.5 %collective-permute-start.47 = (f32[256,128]{1,0:T(8,128)S(1)}, f32[256,128]{1,0:T(8,128)S(1)}, u32[]{:S(2)}, u32[]{:S(2)}) collective-permute-start(f32[256,128]{1,0:T(8,128)S(1)} %get-tuple-element.311), channel_id=1, source_target_pairs={{0,22},{2,20},{4,18},{6,16},{8,30},{10,28},{12,26},{14,24},{16,6},... | collective-permute-start | bytes 393224 | tf_op jit(solution)/shard_map/ppermute | solution.py:305
  153.1 16.5 %collective-permute-start.51 = (f32[256,128]{1,0:T(8,128)S(1)}, f32[256,128]{1,0:T(8,128)S(1)}, u32[]{:S(2)}, u32[]{:S(2)}) collective-permute-start(f32[256,128]{1,0:T(8,128)S(1)} %get-tuple-element.321), channel_id=1, source_target_pairs={{0,14},{2,12},{4,10},{6,8},{8,6},{10,4},{12,2},{14,0},{16,30},{18,... | collective-permute-start | bytes 393224 | tf_op jit(solution)/shard_map/ppermute | solution.py:305
  156.3 16.3 %collective-permute-start.33 = (f32[256,128]{1,0:T(8,128)S(1)}, f32[256,128]{1,0:T(8,128)S(1)}, u32[]{:S(2)}, u32[]{:S(2)}) collective-permute-start(f32[256,128]{1,0:T(8,128)S(1)} %get-tuple-element.280), channel_id=1, source_target_pairs={{0,2},{2,0},{4,6},{6,4},{8,10},{10,8},{12,14},{14,12},{16,18},{18,... | collective-permute-start | bytes 393224 | tf_op jit(solution)/shard_map/ppermute | solution.py:305
  159.1 15.3 %collective-permute-start.37 = (f32[256,128]{1,0:T(8,128)S(1)}, f32[256,128]{1,0:T(8,128)S(1)}, u32[]{:S(2)}, u32[]{:S(2)}) collective-permute-start(f32[256,128]{1,0:T(8,128)S(1)} %get-tuple-element.290), channel_id=1, source_target_pairs={{0,24},{2,26},{4,28},{6,30},{8,16},{10,18},{12,20},{14,22},{16,8},... | collective-permute-start | bytes 393224 | tf_op jit(solution)/shard_map/ppermute | solution.py:305
  172.6 18.5 %collective-permute-start.54 = (f32[256,128]{1,0:T(8,128)S(1)}, f32[256,128]{1,0:T(8,128)S(1)}, u32[]{:S(2)}, u32[]{:S(2)}) collective-permute-start(f32[256,128]{1,0:T(8,128)S(1)} %get-tuple-element.326), channel_id=1, source_target_pairs={{0,18},{2,16},{4,22},{6,20},{8,26},{10,24},{12,30},{14,28},{16,2},... | collective-permute-start | bytes 393224 | tf_op jit(solution)/shard_map/ppermute | solution.py:305
  174.4 16.8 %collective-permute-start.38 = (f32[256,128]{1,0:T(8,128)S(1)}, f32[256,128]{1,0:T(8,128)S(1)}, u32[]{:S(2)}, u32[]{:S(2)}) collective-permute-start(f32[256,128]{1,0:T(8,128)S(1)} %get-tuple-element.291), channel_id=1, source_target_pairs={{0,4},{2,6},{4,0},{6,2},{8,12},{10,14},{12,8},{14,10},{16,20},{18,... | collective-permute-start | bytes 393224 | tf_op jit(solution)/shard_map/ppermute | solution.py:305
  175.3 19.7 %collective-permute-start.43 = (f32[256,128]{1,0:T(8,128)S(1)}, f32[256,128]{1,0:T(8,128)S(1)}, u32[]{:S(2)}, u32[]{:S(2)}) collective-permute-start(f32[256,128]{1,0:T(8,128)S(1)} %get-tuple-element.302), channel_id=1, source_target_pairs={{0,26},{2,24},{4,30},{6,28},{8,18},{10,16},{12,22},{14,20},{16,10}... | collective-permute-start | bytes 393224 | tf_op jit(solution)/shard_map/ppermute | solution.py:305
  177.6 17.7 %collective-permute-start.57 = (f32[256,128]{1,0:T(8,128)S(1)}, f32[256,128]{1,0:T(8,128)S(1)}, u32[]{:S(2)}, u32[]{:S(2)}) collective-permute-start(f32[256,128]{1,0:T(8,128)S(1)} %get-tuple-element.332), channel_id=1, source_target_pairs={{0,28},{2,30},{4,24},{6,26},{8,20},{10,22},{12,16},{14,18},{16,12}... | collective-permute-start | bytes 393224 | tf_op jit(solution)/shard_map/ppermute | solution.py:305
  (79 other events, 1648.2 us)

commit v2 on v1

--- a/solution.py
+++ b/solution.py
@@ -21,7 +21,7 @@
 VMEM_LIMIT = 60 << 20
 RIGHT_LIMIT = 24 << 20
 IN_FLIGHT = 5
-PATTERNS = ('nfnfnfnfnfnfnff', 'fnfnfnfnfnfnfnf', 'fnfnfnfnfnfnfnf', 'nfnfnfnfnfnfnff')
+PATTERNS = ('ffnfnfnfnnfnnff', 'ffnfnfnfnfnfnfn', 'ffnfnfnfnfnfnfn', 'ffnfnfnfnnfnnff')
 LATE = 5
 AHEAD = 5
 BF = jnp.bfloat16
@@ -134,7 +134,7 @@
         in_specs=[pl.BlockSpec((block, sites), lambda g: (g, 0)), whole(field), whole(right), whole(left)],
         out_specs=[pl.BlockSpec((block, LANES), lambda g: (g, 0))] * (2 * parts),
         out_shape=[jax.ShapeDtypeStruct((rows, LANES), F32)] * (2 * parts),
-        scratch_shapes=[pltpu.VMEM((SLICES, LX, LANES), F32), pltpu.VMEM((block // 2 * (LX + PAIR_PAD), LANES), F32)],
+        scratch_shapes=[pltpu.VMEM((SLICES, LX, LANES), F32), pltpu.VMEM(((block // 2 + 1) * (LX + PAIR_PAD), LANES), F32)],
         compiler_params=pltpu.CompilerParams(vmem_limit_bytes=VMEM_LIMIT),
         cost_estimate=pl.CostEstimate(flops=rows * sites * 256 * 2 * 6, bytes_accessed=rows * sites * 8, transcendentals=0),
         name="left_chain",
@@ -196,7 +196,7 @@
         in_specs=[whole(loss), whole(left_y), whole(left_x)] + [whole(piece) for piece in pieces],
         out_specs=[whole(piece) for piece in pieces],
         out_shape=[jax.ShapeDtypeStruct(piece.shape, F32) for piece in pieces],
-        scratch_shapes=[pltpu.VMEM((sites // LY * (LY + ROW_PAD), LANES), F32)],
+        scratch_shapes=[pltpu.VMEM(((sites // LY + 1) * (LY + ROW_PAD), LANES), F32)],
         compiler_params=pltpu.CompilerParams(vmem_limit_bytes=RIGHT_LIMIT),
         cost_estimate=pl.CostEstimate(flops=sites * LANES * 256 * 2 * 6, bytes_accessed=sites * LANES * 12, transcendentals=0),
         name="right_chain",

time: 210 us -> 203 us (0.967)
  waiting for transfers between devices: 57.9 us -> 48.4 us
    ppermute x60, waiting for transfers between devices: 57.9 us -> 48.4 us  [send(): lax.ppermute(block, 'cols', [(s, s ^ mask) for s in range(self.parts)])]
    ppermute x60, starting transfers between devices: 118 us -> 120 us  [send(): lax.ppermute(block, 'cols', [(s, s ^ mask) for s in range(self.parts)])]
  transfers between devices with their start and end apart: 60 -> 60, of which waited for: 17 -> 16; matrix products, arithmetic and copies ran while one was open for 0% -> 0% of each run, Pallas kernels for 8% -> 8%
where the time goes in v2:
time: 203 us
  starting transfers between devices  120 us (59%)
  waiting for transfers between devices  48.4 us (24%)
  Pallas kernels  30.5 us (15%)
  local copies, waits for them, and re-layouts  3 us (1%)
    ppermute x60, starting transfers between devices, send(): lax.ppermute(block, 'cols', [(s, s ^ mask) for s in range(self.parts)])  120 us
    ppermute x60, waiting for transfers between devices, send(): lax.ppermute(block, 'cols', [(s, s ^ mask) for s in range(self.parts)])  48.4 us
    pallas_call x2, Pallas kernels, right_chain(): pl.pallas_call(functools.partial(right_body, parts), grid=(1,), in_specs=...  13.4 us
    pallas_call x1, Pallas kernels, left_chain(): pl.pallas_call(functools.partial(left_body, parts), grid=(rows // block,)...  11.9 us
    pallas_call x2, Pallas kernels, place(): pl.pallas_call(functools.partial(place_body, parts, lane, len(held)), in_...  5.15 us
  transfers between devices with their start and end apart: 60, of which 16 were waited for; matrix products, arithmetic and copies ran while one was open for 0% of the time, Pallas kernels for 8%

profile of v2, /device:TPU:0, one launch (start us, length us, event | category | flops | bytes accessed | tf_op | source)
XLA Modules:
  0.0 203.2 jit_solution(3890500969715929697)
XLA Ops:
  0.0 11.9 %left_chain.1 = (f32[256,128]{1,0:T(8,128)}, f32[256,128]{1,0:T(8,128)}, f32[256,128]{1,0:T(8,128)}, f32[256,128]{1,0:T(8,128)}, f32[256,128]{1,0:T(8,128)}, /*i...) custom-call(f32[256,4096]{1,0:T(8,128)} %bitcast.8, ...), custom_call_target="tpu_custom_call" | custom-call | flops 3221225472 | bytes 8388608 | tf_op jit(solution)/shard_map/left_chain/pallas_call | solution.py:131
  11.9 3.0 %collective-permute-start = (f32[256,128]{1,0:T(8,128)}, f32[256,128]{1,0:T(8,128)S(1)}, u32[]{:S(2)}, u32[]{:S(2)}) collective-permute-start(f32[256,128]{1,0:T(8,128)} %get-tuple-element.183), channel_id=1, source_target_pairs={{0,2},{2,0},{4,6},{6,4},{8,10},{10,8},{12,14},{14,12},{16,18},{18,... | collective-permute-start | bytes 393224 | tf_op jit(solution)/shard_map/ppermute | solution.py:305
  14.9 3.6 %collective-permute-start.1 = (f32[256,128]{1,0:T(8,128)}, f32[256,128]{1,0:T(8,128)S(1)}, u32[]{:S(2)}, u32[]{:S(2)}) collective-permute-start(f32[256,128]{1,0:T(8,128)} %get-tuple-element.187), channel_id=1, source_target_pairs={{0,26},{2,24},{4,30},{6,28},{8,18},{10,16},{12,22},{14,20},{16,10}... | collective-permute-start | bytes 393224 | tf_op jit(solution)/shard_map/ppermute | solution.py:305
  19.1 3.8 %collective-permute-start.10 = (f32[256,128]{1,0:T(8,128)}, f32[256,128]{1,0:T(8,128)S(1)}, u32[]{:S(2)}, u32[]{:S(2)}) collective-permute-start(f32[256,128]{1,0:T(8,128)} %get-tuple-element.212), channel_id=1, source_target_pairs={{0,24},{2,26},{4,28},{6,30},{8,16},{10,18},{12,20},{14,22},{16,8},... | collective-permute-start | bytes 393224 | tf_op jit(solution)/shard_map/ppermute | solution.py:305
  25.9 7.4 %collective-permute-done.3.rest_8_ = f32[256,128]{1,0:T(8,128)S(1)} collective-permute-done((f32[256,128]{1,0:T(8,128)}, f32[256,128]{1,0:T(8,128)S(1)}, u32[]{:S(2)}, u32[]{:S(2)}) %collective-permute-start.3) | collective-permute-done | bytes 131104 | tf_op jit(solution)/shard_map/ppermute | solution.py:305
  34.4 2.8 %collective-permute-start.8 = (f32[256,128]{1,0:T(8,128)}, f32[256,128]{1,0:T(8,128)S(1)}, u32[]{:S(2)}, u32[]{:S(2)}) collective-permute-start(f32[256,128]{1,0:T(8,128)} %get-tuple-element.206), channel_id=1, source_target_pairs={{0,28},{2,30},{4,24},{6,26},{8,20},{10,22},{12,16},{14,18},{16,12}... | collective-permute-start | bytes 393224 | tf_op jit(solution)/shard_map/ppermute | solution.py:305
  37.2 2.9 %collective-permute-start.11 = (f32[256,128]{1,0:T(8,128)}, f32[256,128]{1,0:T(8,128)S(1)}, u32[]{:S(2)}, u32[]{:S(2)}) collective-permute-start(f32[256,128]{1,0:T(8,128)} %get-tuple-element.213), channel_id=1, source_target_pairs={{0,18},{2,16},{4,22},{6,20},{8,26},{10,24},{12,30},{14,28},{16,2},... | collective-permute-start | bytes 393224 | tf_op jit(solution)/shard_map/ppermute | solution.py:305
  46.1 7.9 %collective-permute-start.9 = (f32[256,128]{1,0:T(8,128)}, f32[256,128]{1,0:T(8,128)S(1)}, u32[]{:S(2)}, u32[]{:S(2)}) collective-permute-start(f32[256,128]{1,0:T(8,128)} %get-tuple-element.207), channel_id=1, source_target_pairs={{0,14},{2,12},{4,10},{6,8},{8,6},{10,4},{12,2},{14,0},{16,30},{18,... | collective-permute-start | bytes 393224 | tf_op jit(solution)/shard_map/ppermute | solution.py:305
  57.0 3.1 %collective-permute-done.13.rest_11_ = f32[256,128]{1,0:T(8,128)S(1)} collective-permute-done((f32[256,128]{1,0:T(8,128)}, f32[256,128]{1,0:T(8,128)S(1)}, u32[]{:S(2)}, u32[]{:S(2)}) %collective-permute-start.13) | collective-permute-done | bytes 131104 | tf_op jit(solution)/shard_map/ppermute | solution.py:305
  61.3 3.3 %collective-permute-start.16 = (f32[256,128]{1,0:T(8,128)S(1)}, f32[256,128]{1,0:T(8,128)S(1)}, u32[]{:S(2)}, u32[]{:S(2)}) collective-permute-start(f32[256,128]{1,0:T(8,128)S(1)} %copy-done.49), channel_id=1, source_target_pairs={{0,26},{2,24},{4,30},{6,28},{8,18},{10,16},{12,22},{14,20},{16,10}... | collective-permute-start | bytes 393224 | tf_op jit(solution)/shard_map/ppermute | solution.py:305
  64.6 4.9 %collective-permute-start.21 = (f32[256,128]{1,0:T(8,128)S(1)}, f32[256,128]{1,0:T(8,128)S(1)}, u32[]{:S(2)}, u32[]{:S(2)}) collective-permute-start(f32[256,128]{1,0:T(8,128)S(1)} %copy-done.47), channel_id=1, source_target_pairs={{0,16},{2,18},{4,20},{6,22},{8,24},{10,26},{12,28},{14,30},{16,0},... | collective-permute-start | bytes 393224 | tf_op jit(solution)/shard_map/ppermute | solution.py:305
  70.7 4.0 %collective-permute-start.23 = (f32[256,128]{1,0:T(8,128)S(1)}, f32[256,128]{1,0:T(8,128)S(1)}, u32[]{:S(2)}, u32[]{:S(2)}) collective-permute-start(f32[256,128]{1,0:T(8,128)S(1)} %copy-done.46), channel_id=1, source_target_pairs={{0,24},{2,26},{4,28},{6,30},{8,16},{10,18},{12,20},{14,22},{16,8},... | collective-permute-start | bytes 393224 | tf_op jit(solution)/shard_map/ppermute | solution.py:305
  74.9 6.6 %right_chain.2 = (f32[256,128]{1,0:T(8,128)S(1)}, f32[256,128]{1,0:T(8,128)S(1)}, f32[256,128]{1,0:T(8,128)S(1)}, f32[256,128]{1,0:T(8,128)S(1)}, f32[256,128]{1...) custom-call(f32[4096,3]{1,0:T(8,128)S(1)} %exponential_bitcast_fusio, ...), custom_call_target="tpu_custom_call" | custom-call | flops 1610612736 | bytes 6291456 | tf_op jit(solution)/shard_map/right_chain/pallas_call | solution.py:193
  84.0 4.2 %collective-permute-start.22 = (f32[256,128]{1,0:T(8,128)S(1)}, f32[256,128]{1,0:T(8,128)S(1)}, u32[]{:S(2)}, u32[]{:S(2)}) collective-permute-start(f32[256,128]{1,0:T(8,128)S(1)} %copy-done.42), channel_id=1, source_target_pairs={{0,10},{2,8},{4,14},{6,12},{8,2},{10,0},{12,6},{14,4},{16,26},{18,... | collective-permute-start | bytes 393224 | tf_op jit(solution)/shard_map/ppermute | solution.py:305
  88.2 3.4 %collective-permute-start.24 = (f32[256,128]{1,0:T(8,128)S(1)}, f32[256,128]{1,0:T(8,128)S(1)}, u32[]{:S(2)}, u32[]{:S(2)}) collective-permute-start(f32[256,128]{1,0:T(8,128)S(1)} %copy-done.41), channel_id=1, source_target_pairs={{0,18},{2,16},{4,22},{6,20},{8,26},{10,24},{12,30},{14,28},{16,2},... | collective-permute-start | bytes 393224 | tf_op jit(solution)/shard_map/ppermute | solution.py:305
  93.9 5.2 %collective-permute-start.28 = (f32[256,128]{1,0:T(8,128)S(1)}, f32[256,128]{1,0:T(8,128)S(1)}, u32[]{:S(2)}, u32[]{:S(2)}) collective-permute-start(f32[256,128]{1,0:T(8,128)S(1)} %copy-done.39), channel_id=1, source_target_pairs={{0,22},{2,20},{4,18},{6,16},{8,30},{10,28},{12,26},{14,24},{16,6},... | collective-permute-start | bytes 393224 | tf_op jit(solution)/shard_map/ppermute | solution.py:305
  99.2 3.2 %collective-permute-start.29 = (f32[256,128]{1,0:T(8,128)S(1)}, f32[256,128]{1,0:T(8,128)S(1)}, u32[]{:S(2)}, u32[]{:S(2)}) collective-permute-start(f32[256,128]{1,0:T(8,128)S(1)} %copy-done.37), channel_id=1, source_target_pairs={{0,30},{2,28},{4,26},{6,24},{8,22},{10,20},{12,18},{14,16},{16,14}... | collective-permute-start | bytes 393224 | tf_op jit(solution)/shard_map/ppermute | solution.py:305
  105.6 3.2 %collective-permute-done.28.rest_11_ = f32[256,128]{1,0:T(8,128)S(1)} collective-permute-done((f32[256,128]{1,0:T(8,128)S(1)}, f32[256,128]{1,0:T(8,128)S(1)}, u32[]{:S(2)}, u32[]{:S(2)}) %collective-permute-start.28) | collective-permute-done | bytes 131104 | tf_op jit(solution)/shard_map/ppermute | solution.py:305
  108.8 4.9 %collective-permute-start.34 = (f32[256,128]{1,0:T(8,128)S(1)}, f32[256,128]{1,0:T(8,128)S(1)}, u32[]{:S(2)}, u32[]{:S(2)}) collective-permute-start(f32[256,128]{1,0:T(8,128)S(1)} %get-tuple-element.287), channel_id=1, source_target_pairs={{0,26},{2,24},{4,30},{6,28},{8,18},{10,16},{12,22},{14,20},{16,10}... | collective-permute-start | bytes 393224 | tf_op jit(solution)/shard_map/ppermute | solution.py:305
  113.7 5.4 %collective-permute-start.39 = (f32[256,128]{1,0:T(8,128)S(1)}, f32[256,128]{1,0:T(8,128)S(1)}, u32[]{:S(2)}, u32[]{:S(2)}) collective-permute-start(f32[256,128]{1,0:T(8,128)S(1)} %get-tuple-element.298), channel_id=1, source_target_pairs={{0,16},{2,18},{4,20},{6,22},{8,24},{10,26},{12,28},{14,30},{16,0},... | collective-permute-start | bytes 393224 | tf_op jit(solution)/shard_map/ppermute | solution.py:305
  119.1 6.8 %right_chain.3 = (f32[256,128]{1,0:T(8,128)S(1)}, f32[256,128]{1,0:T(8,128)S(1)}, f32[256,128]{1,0:T(8,128)S(1)}, f32[256,128]{1,0:T(8,128)S(1)}, f32[256,128]{1...) custom-call(f32[4096,3]{1,0:T(8,128)S(1)} %exponential_bitcast_fusio, ...), custom_call_target="tpu_custom_call" | custom-call | flops 1610612736 | bytes 6291456 | tf_op jit(solution)/shard_map/right_chain/pallas_call | solution.py:193
  129.1 2.6 %collective-permute-start.40 = (f32[256,128]{1,0:T(8,128)S(1)}, f32[256,128]{1,0:T(8,128)S(1)}, u32[]{:S(2)}, u32[]{:S(2)}) collective-permute-start(f32[256,128]{1,0:T(8,128)S(1)} %get-tuple-element.299), channel_id=1, source_target_pairs={{0,10},{2,8},{4,14},{6,12},{8,2},{10,0},{12,6},{14,4},{16,26},{18,... | collective-permute-start | bytes 393224 | tf_op jit(solution)/shard_map/ppermute | solution.py:305
  132.4 2.8 %collective-permute-start.53 = (f32[256,128]{1,0:T(8,128)S(1)}, f32[256,128]{1,0:T(8,128)S(1)}, u32[]{:S(2)}, u32[]{:S(2)}) collective-permute-start(f32[256,128]{1,0:T(8,128)S(1)} %get-tuple-element.327), channel_id=1, source_target_pairs={{0,18},{2,16},{4,22},{6,20},{8,26},{10,24},{12,30},{14,28},{16,2},... | collective-permute-start | bytes 393224 | tf_op jit(solution)/shard_map/ppermute | solution.py:305
  137.9 4.2 %collective-permute-start.36 = (f32[256,128]{1,0:T(8,128)S(1)}, f32[256,128]{1,0:T(8,128)S(1)}, u32[]{:S(2)}, u32[]{:S(2)}) collective-permute-start(f32[256,128]{1,0:T(8,128)S(1)} %get-tuple-element.289), channel_id=1, source_target_pairs={{0,22},{2,20},{4,18},{6,16},{8,30},{10,28},{12,26},{14,24},{16,6},... | collective-permute-start | bytes 393224 | tf_op jit(solution)/shard_map/ppermute | solution.py:305
  145.8 5.1 %collective-permute-done.53.rest_9_ = f32[256,128]{1,0:T(8,128)S(1)} collective-permute-done((f32[256,128]{1,0:T(8,128)S(1)}, f32[256,128]{1,0:T(8,128)S(1)}, u32[]{:S(2)}, u32[]{:S(2)}) %collective-permute-start.53) | collective-permute-done | bytes 131104 | tf_op jit(solution)/shard_map/ppermute | solution.py:305
  154.7 3.7 %collective-permute-start.37 = (f32[256,128]{1,0:T(8,128)S(1)}, f32[256,128]{1,0:T(8,128)S(1)}, u32[]{:S(2)}, u32[]{:S(2)}) collective-permute-start(f32[256,128]{1,0:T(8,128)S(1)} %get-tuple-element.290), channel_id=1, source_target_pairs={{0,26},{2,24},{4,30},{6,28},{8,18},{10,16},{12,22},{14,20},{16,10}... | collective-permute-start | bytes 393224 | tf_op jit(solution)/shard_map/ppermute | solution.py:305
  158.5 2.8 %collective-permute-start.42 = (f32[256,128]{1,0:T(8,128)S(1)}, f32[256,128]{1,0:T(8,128)S(1)}, u32[]{:S(2)}, u32[]{:S(2)}) collective-permute-start(f32[256,128]{1,0:T(8,128)S(1)} %get-tuple-element.301), channel_id=1, source_target_pairs={{0,16},{2,18},{4,20},{6,22},{8,24},{10,26},{12,28},{14,30},{16,0},... | collective-permute-start | bytes 393224 | tf_op jit(solution)/shard_map/ppermute | solution.py:305
  165.8 4.8 %collective-permute-done.42.rest_8_ = f32[256,128]{1,0:T(8,128)S(1)} collective-permute-done((f32[256,128]{1,0:T(8,128)S(1)}, f32[256,128]{1,0:T(8,128)S(1)}, u32[]{:S(2)}, u32[]{:S(2)}) %collective-permute-start.42) | collective-permute-done | bytes 131104 | tf_op jit(solution)/shard_map/ppermute | solution.py:305
  175.4 2.6 %collective-permute-start.58 = (f32[256,128]{1,0:T(8,128)S(1)}, f32[256,128]{1,0:T(8,128)S(1)}, u32[]{:S(2)}, u32[]{:S(2)}) collective-permute-start(f32[256,128]{1,0:T(8,128)S(1)} %get-tuple-element.333), channel_id=1, source_target_pairs={{0,22},{2,20},{4,18},{6,16},{8,30},{10,28},{12,26},{14,24},{16,6},... | collective-permute-start | bytes 393224 | tf_op jit(solution)/shard_map/ppermute | solution.py:305
  178.0 7.3 %collective-permute-start.59 = (f32[256,128]{1,0:T(8,128)S(1)}, f32[256,128]{1,0:T(8,128)S(1)}, u32[]{:S(2)}, u32[]{:S(2)}) collective-permute-start(f32[256,128]{1,0:T(8,128)S(1)} %get-tuple-element.337), channel_id=1, source_target_pairs={{0,30},{2,28},{4,26},{6,24},{8,22},{10,20},{12,18},{14,16},{16,14}... | collective-permute-start | bytes 393224 | tf_op jit(solution)/shard_map/ppermute | solution.py:305
  185.4 6.5 %collective-permute-done.56.rest_9_ = f32[256,128]{1,0:T(8,128)S(1)} collective-permute-done((f32[256,128]{1,0:T(8,128)S(1)}, f32[256,128]{1,0:T(8,128)S(1)}, u32[]{:S(2)}, u32[]{:S(2)}) %collective-permute-start.56) | collective-permute-done | bytes 131104 | tf_op jit(solution)/shard_map/ppermute | solution.py:305
  192.1 2.6 %place.2.rest_16_ = f32[256,4096]{1,0:T(8,128)} custom-call(f32[256,128]{1,0:T(8,128)} %copy-done.1, f32[256,128]{1,0:T(8,128)} %copy-done.20, f32[256,128]{1,0:T(8,128)} %copy-done.26, f32[256,128]{1,0:T(8,128)} %copy-done.33, f32[256,128]{1,0:T(8,128)} %copy-done.22, f32[256,128]{1,0:T(8,128)} %copy-done.27, f32[256,128]{1,0:T(8,128)} %copy-done.34, ...), custom_call_target="tpu_custom_call" | custom-call | bytes 4194304 | tf_op jit(solution)/shard_map/place/pallas_call | solution.py:229
  (198 shorter events, 55.9 us)
Async XLA Ops:
  18.5 14.8 %collective-permute-start.3 = (f32[256,128]{1,0:T(8,128)}, f32[256,128]{1,0:T(8,128)S(1)}, u32[]{:S(2)}, u32[]{:S(2)}) collective-permute-start(f32[256,128]{1,0:T(8,128)} %get-tuple-element.193), channel_id=1, source_target_pairs={{0,16},{2,18},{4,20},{6,22},{8,24},{10,26},{12,28},{14,30},{16,0},... | collective-permute-start | bytes 393224 | tf_op jit(solution)/shard_map/ppermute | solution.py:305
  18.5 15.9 %collective-permute-start.6 = (f32[256,128]{1,0:T(8,128)}, f32[256,128]{1,0:T(8,128)S(1)}, u32[]{:S(2)}, u32[]{:S(2)}) collective-permute-start(f32[256,128]{1,0:T(8,128)} %get-tuple-element.198), channel_id=1, source_target_pairs={{0,8},{2,10},{4,12},{6,14},{8,0},{10,2},{12,4},{14,6},{16,24},{18,... | collective-permute-start | bytes 393224 | tf_op jit(solution)/shard_map/ppermute | solution.py:305
  19.1 18.1 %collective-permute-start.10 = (f32[256,128]{1,0:T(8,128)}, f32[256,128]{1,0:T(8,128)S(1)}, u32[]{:S(2)}, u32[]{:S(2)}) collective-permute-start(f32[256,128]{1,0:T(8,128)} %get-tuple-element.212), channel_id=1, source_target_pairs={{0,24},{2,26},{4,28},{6,30},{8,16},{10,18},{12,20},{14,22},{16,8},... | collective-permute-start | bytes 393224 | tf_op jit(solution)/shard_map/ppermute | solution.py:305
  22.9 17.9 %collective-permute-start.7 = (f32[256,128]{1,0:T(8,128)}, f32[256,128]{1,0:T(8,128)S(1)}, u32[]{:S(2)}, u32[]{:S(2)}) collective-permute-start(f32[256,128]{1,0:T(8,128)} %get-tuple-element.202), channel_id=1, source_target_pairs={{0,12},{2,14},{4,8},{6,10},{8,4},{10,6},{12,0},{14,2},{16,28},{18,... | collective-permute-start | bytes 393224 | tf_op jit(solution)/shard_map/ppermute | solution.py:305
  24.3 18.3 %collective-permute-start.2 = (f32[256,128]{1,0:T(8,128)}, f32[256,128]{1,0:T(8,128)S(1)}, u32[]{:S(2)}, u32[]{:S(2)}) collective-permute-start(f32[256,128]{1,0:T(8,128)} %get-tuple-element.188), channel_id=1, source_target_pairs={{0,4},{2,6},{4,0},{6,2},{8,12},{10,14},{12,8},{14,10},{16,20},{18,... | collective-permute-start | bytes 393224 | tf_op jit(solution)/shard_map/ppermute | solution.py:305
  37.2 19.5 %collective-permute-start.11 = (f32[256,128]{1,0:T(8,128)}, f32[256,128]{1,0:T(8,128)S(1)}, u32[]{:S(2)}, u32[]{:S(2)}) collective-permute-start(f32[256,128]{1,0:T(8,128)} %get-tuple-element.213), channel_id=1, source_target_pairs={{0,18},{2,16},{4,22},{6,20},{8,26},{10,24},{12,30},{14,28},{16,2},... | collective-permute-start | bytes 393224 | tf_op jit(solution)/shard_map/ppermute | solution.py:305
  40.8 19.3 %collective-permute-start.13 = (f32[256,128]{1,0:T(8,128)}, f32[256,128]{1,0:T(8,128)S(1)}, u32[]{:S(2)}, u32[]{:S(2)}) collective-permute-start(f32[256,128]{1,0:T(8,128)} %get-tuple-element.219), channel_id=1, source_target_pairs={{0,22},{2,20},{4,18},{6,16},{8,30},{10,28},{12,26},{14,24},{16,6},... | collective-permute-start | bytes 393224 | tf_op jit(solution)/shard_map/ppermute | solution.py:305
  42.7 18.7 %collective-permute-start.14 = (f32[256,128]{1,0:T(8,128)}, f32[256,128]{1,0:T(8,128)S(1)}, u32[]{:S(2)}, u32[]{:S(2)}) collective-permute-start(f32[256,128]{1,0:T(8,128)} %get-tuple-element.225), channel_id=1, source_target_pairs={{0,30},{2,28},{4,26},{6,24},{8,22},{10,20},{12,18},{14,16},{16,14}... | collective-permute-start | bytes 393224 | tf_op jit(solution)/shard_map/ppermute | solution.py:305
  44.7 19.9 %collective-permute-start.5 = (f32[256,128]{1,0:T(8,128)}, f32[256,128]{1,0:T(8,128)S(1)}, u32[]{:S(2)}, u32[]{:S(2)}) collective-permute-start(f32[256,128]{1,0:T(8,128)} %get-tuple-element.195), channel_id=1, source_target_pairs={{0,6},{2,4},{4,2},{6,0},{8,14},{10,12},{12,10},{14,8},{16,22},{18,... | collective-permute-start | bytes 393224 | tf_op jit(solution)/shard_map/ppermute | solution.py:305
  46.1 23.3 %collective-permute-start.9 = (f32[256,128]{1,0:T(8,128)}, f32[256,128]{1,0:T(8,128)S(1)}, u32[]{:S(2)}, u32[]{:S(2)}) collective-permute-start(f32[256,128]{1,0:T(8,128)} %get-tuple-element.207), channel_id=1, source_target_pairs={{0,14},{2,12},{4,10},{6,8},{8,6},{10,4},{12,2},{14,0},{16,30},{18,... | collective-permute-start | bytes 393224 | tf_op jit(solution)/shard_map/ppermute | solution.py:305
  60.1 22.1 %collective-permute-start.15 = (f32[256,128]{1,0:T(8,128)S(1)}, f32[256,128]{1,0:T(8,128)S(1)}, u32[]{:S(2)}, u32[]{:S(2)}) collective-permute-start(f32[256,128]{1,0:T(8,128)S(1)} %copy-done.50), channel_id=1, source_target_pairs={{0,2},{2,0},{4,6},{6,4},{8,10},{10,8},{12,14},{14,12},{16,18},{18,... | collective-permute-start | bytes 393224 | tf_op jit(solution)/shard_map/ppermute | solution.py:305
  61.3 20.9 %collective-permute-start.16 = (f32[256,128]{1,0:T(8,128)S(1)}, f32[256,128]{1,0:T(8,128)S(1)}, u32[]{:S(2)}, u32[]{:S(2)}) collective-permute-start(f32[256,128]{1,0:T(8,128)S(1)} %copy-done.49), channel_id=1, source_target_pairs={{0,26},{2,24},{4,30},{6,28},{8,18},{10,16},{12,22},{14,20},{16,10}... | collective-permute-start | bytes 393224 | tf_op jit(solution)/shard_map/ppermute | solution.py:305
  64.6 19.5 %collective-permute-start.21 = (f32[256,128]{1,0:T(8,128)S(1)}, f32[256,128]{1,0:T(8,128)S(1)}, u32[]{:S(2)}, u32[]{:S(2)}) collective-permute-start(f32[256,128]{1,0:T(8,128)S(1)} %copy-done.47), channel_id=1, source_target_pairs={{0,16},{2,18},{4,20},{6,22},{8,24},{10,26},{12,28},{14,30},{16,0},... | collective-permute-start | bytes 393224 | tf_op jit(solution)/shard_map/ppermute | solution.py:305
  70.7 17.5 %collective-permute-start.23 = (f32[256,128]{1,0:T(8,128)S(1)}, f32[256,128]{1,0:T(8,128)S(1)}, u32[]{:S(2)}, u32[]{:S(2)}) collective-permute-start(f32[256,128]{1,0:T(8,128)S(1)} %copy-done.46), channel_id=1, source_target_pairs={{0,24},{2,26},{4,28},{6,30},{8,16},{10,18},{12,20},{14,22},{16,8},... | collective-permute-start | bytes 393224 | tf_op jit(solution)/shard_map/ppermute | solution.py:305
  82.3 16.8 %collective-permute-start.19 = (f32[256,128]{1,0:T(8,128)S(1)}, f32[256,128]{1,0:T(8,128)S(1)}, u32[]{:S(2)}, u32[]{:S(2)}) collective-permute-start(f32[256,128]{1,0:T(8,128)S(1)} %copy-done.43), channel_id=1, source_target_pairs={{0,28},{2,30},{4,24},{6,26},{8,20},{10,22},{12,16},{14,18},{16,12}... | collective-permute-start | bytes 393224 | tf_op jit(solution)/shard_map/ppermute | solution.py:305
  84.0 15.1 %collective-permute-start.22 = (f32[256,128]{1,0:T(8,128)S(1)}, f32[256,128]{1,0:T(8,128)S(1)}, u32[]{:S(2)}, u32[]{:S(2)}) collective-permute-start(f32[256,128]{1,0:T(8,128)S(1)} %copy-done.42), channel_id=1, source_target_pairs={{0,10},{2,8},{4,14},{6,12},{8,2},{10,0},{12,6},{14,4},{16,26},{18,... | collective-permute-start | bytes 393224 | tf_op jit(solution)/shard_map/ppermute | solution.py:305
  88.2 16.2 %collective-permute-start.24 = (f32[256,128]{1,0:T(8,128)S(1)}, f32[256,128]{1,0:T(8,128)S(1)}, u32[]{:S(2)}, u32[]{:S(2)}) collective-permute-start(f32[256,128]{1,0:T(8,128)S(1)} %copy-done.41), channel_id=1, source_target_pairs={{0,18},{2,16},{4,22},{6,20},{8,26},{10,24},{12,30},{14,28},{16,2},... | collective-permute-start | bytes 393224 | tf_op jit(solution)/shard_map/ppermute | solution.py:305
  93.9 15.0 %collective-permute-start.28 = (f32[256,128]{1,0:T(8,128)S(1)}, f32[256,128]{1,0:T(8,128)S(1)}, u32[]{:S(2)}, u32[]{:S(2)}) collective-permute-start(f32[256,128]{1,0:T(8,128)S(1)} %copy-done.39), channel_id=1, source_target_pairs={{0,22},{2,20},{4,18},{6,16},{8,30},{10,28},{12,26},{14,24},{16,6},... | collective-permute-start | bytes 393224 | tf_op jit(solution)/shard_map/ppermute | solution.py:305
  104.4 14.6 %collective-permute-start.25 = (f32[256,128]{1,0:T(8,128)S(1)}, f32[256,128]{1,0:T(8,128)S(1)}, u32[]{:S(2)}, u32[]{:S(2)}) collective-permute-start(f32[256,128]{1,0:T(8,128)S(1)} %copy-done.36), channel_id=1, source_target_pairs={{0,12},{2,14},{4,8},{6,10},{8,4},{10,6},{12,0},{14,2},{16,28},{18,... | collective-permute-start | bytes 393224 | tf_op jit(solution)/shard_map/ppermute | solution.py:305
  105.2 21.4 %collective-permute-start.30 = (f32[256,128]{1,0:T(8,128)S(1)}, f32[256,128]{1,0:T(8,128)S(1)}, u32[]{:S(2)}, u32[]{:S(2)}) collective-permute-start(f32[256,128]{1,0:T(8,128)S(1)} %get-tuple-element.277), channel_id=1, source_target_pairs={{0,2},{2,0},{4,6},{6,4},{8,10},{10,8},{12,14},{14,12},{16,18},{18,... | collective-permute-start | bytes 393224 | tf_op jit(solution)/shard_map/ppermute | solution.py:305
  108.8 18.7 %collective-permute-start.34 = (f32[256,128]{1,0:T(8,128)S(1)}, f32[256,128]{1,0:T(8,128)S(1)}, u32[]{:S(2)}, u32[]{:S(2)}) collective-permute-start(f32[256,128]{1,0:T(8,128)S(1)} %get-tuple-element.287), channel_id=1, source_target_pairs={{0,26},{2,24},{4,30},{6,28},{8,18},{10,16},{12,22},{14,20},{16,10}... | collective-permute-start | bytes 393224 | tf_op jit(solution)/shard_map/ppermute | solution.py:305
  113.7 18.0 %collective-permute-start.45 = (f32[256,128]{1,0:T(8,128)S(1)}, f32[256,128]{1,0:T(8,128)S(1)}, u32[]{:S(2)}, u32[]{:S(2)}) collective-permute-start(f32[256,128]{1,0:T(8,128)S(1)} %get-tuple-element.308), channel_id=1, source_target_pairs={{0,8},{2,10},{4,12},{6,14},{8,0},{10,2},{12,4},{14,6},{16,24},{18,... | collective-permute-start | bytes 393224 | tf_op jit(solution)/shard_map/ppermute | solution.py:305
  113.7 15.4 %collective-permute-start.39 = (f32[256,128]{1,0:T(8,128)S(1)}, f32[256,128]{1,0:T(8,128)S(1)}, u32[]{:S(2)}, u32[]{:S(2)}) collective-permute-start(f32[256,128]{1,0:T(8,128)S(1)} %get-tuple-element.298), channel_id=1, source_target_pairs={{0,16},{2,18},{4,20},{6,22},{8,24},{10,26},{12,28},{14,30},{16,0},... | collective-permute-start | bytes 393224 | tf_op jit(solution)/shard_map/ppermute | solution.py:305
  132.4 18.5 %collective-permute-start.53 = (f32[256,128]{1,0:T(8,128)S(1)}, f32[256,128]{1,0:T(8,128)S(1)}, u32[]{:S(2)}, u32[]{:S(2)}) collective-permute-start(f32[256,128]{1,0:T(8,128)S(1)} %get-tuple-element.327), channel_id=1, source_target_pairs={{0,18},{2,16},{4,22},{6,20},{8,26},{10,24},{12,30},{14,28},{16,2},... | collective-permute-start | bytes 393224 | tf_op jit(solution)/shard_map/ppermute | solution.py:305
  137.9 16.8 %collective-permute-start.36 = (f32[256,128]{1,0:T(8,128)S(1)}, f32[256,128]{1,0:T(8,128)S(1)}, u32[]{:S(2)}, u32[]{:S(2)}) collective-permute-start(f32[256,128]{1,0:T(8,128)S(1)} %get-tuple-element.289), channel_id=1, source_target_pairs={{0,22},{2,20},{4,18},{6,16},{8,30},{10,28},{12,26},{14,24},{16,6},... | collective-permute-start | bytes 393224 | tf_op jit(solution)/shard_map/ppermute | solution.py:305
  142.1 16.3 %collective-permute-start.41 = (f32[256,128]{1,0:T(8,128)S(1)}, f32[256,128]{1,0:T(8,128)S(1)}, u32[]{:S(2)}, u32[]{:S(2)}) collective-permute-start(f32[256,128]{1,0:T(8,128)S(1)} %get-tuple-element.300), channel_id=1, source_target_pairs={{0,30},{2,28},{4,26},{6,24},{8,22},{10,20},{12,18},{14,16},{16,14}... | collective-permute-start | bytes 393224 | tf_op jit(solution)/shard_map/ppermute | solution.py:305
  144.0 17.2 %collective-permute-start.47 = (f32[256,128]{1,0:T(8,128)S(1)}, f32[256,128]{1,0:T(8,128)S(1)}, u32[]{:S(2)}, u32[]{:S(2)}) collective-permute-start(f32[256,128]{1,0:T(8,128)S(1)} %get-tuple-element.310), channel_id=1, source_target_pairs={{0,6},{2,4},{4,2},{6,0},{8,14},{10,12},{12,10},{14,8},{16,22},{18,... | collective-permute-start | bytes 393224 | tf_op jit(solution)/shard_map/ppermute | solution.py:305
  170.6 14.7 %collective-permute-start.43 = (f32[256,128]{1,0:T(8,128)S(1)}, f32[256,128]{1,0:T(8,128)S(1)}, u32[]{:S(2)}, u32[]{:S(2)}) collective-permute-start(f32[256,128]{1,0:T(8,128)S(1)} %get-tuple-element.302), channel_id=1, source_target_pairs={{0,10},{2,8},{4,14},{6,12},{8,2},{10,0},{12,6},{14,4},{16,26},{18,... | collective-permute-start | bytes 393224 | tf_op jit(solution)/shard_map/ppermute | solution.py:305
  170.6 14.7 %collective-permute-start.50 = (f32[256,128]{1,0:T(8,128)S(1)}, f32[256,128]{1,0:T(8,128)S(1)}, u32[]{:S(2)}, u32[]{:S(2)}) collective-permute-start(f32[256,128]{1,0:T(8,128)S(1)} %get-tuple-element.318), channel_id=1, source_target_pairs={{0,28},{2,30},{4,24},{6,26},{8,20},{10,22},{12,16},{14,18},{16,12}... | collective-permute-start | bytes 393224 | tf_op jit(solution)/shard_map/ppermute | solution.py:305
  172.8 19.1 %collective-permute-start.56 = (f32[256,128]{1,0:T(8,128)S(1)}, f32[256,128]{1,0:T(8,128)S(1)}, u32[]{:S(2)}, u32[]{:S(2)}) collective-permute-start(f32[256,128]{1,0:T(8,128)S(1)} %get-tuple-element.330), channel_id=1, source_target_pairs={{0,18},{2,16},{4,22},{6,20},{8,26},{10,24},{12,30},{14,28},{16,2},... | collective-permute-start | bytes 393224 | tf_op jit(solution)/shard_map/ppermute | solution.py:305
  175.4 19.8 %collective-permute-start.58 = (f32[256,128]{1,0:T(8,128)S(1)}, f32[256,128]{1,0:T(8,128)S(1)}, u32[]{:S(2)}, u32[]{:S(2)}) collective-permute-start(f32[256,128]{1,0:T(8,128)S(1)} %get-tuple-element.333), channel_id=1, source_target_pairs={{0,22},{2,20},{4,18},{6,16},{8,30},{10,28},{12,26},{14,24},{16,6},... | collective-permute-start | bytes 393224 | tf_op jit(solution)/shard_map/ppermute | solution.py:305
  178.0 17.3 %collective-permute-start.59 = (f32[256,128]{1,0:T(8,128)S(1)}, f32[256,128]{1,0:T(8,128)S(1)}, u32[]{:S(2)}, u32[]{:S(2)}) collective-permute-start(f32[256,128]{1,0:T(8,128)S(1)} %get-tuple-element.337), channel_id=1, source_target_pairs={{0,30},{2,28},{4,26},{6,24},{8,22},{10,20},{12,18},{14,16},{16,14}... | collective-permute-start | bytes 393224 | tf_op jit(solution)/shard_map/ppermute | solution.py:305
  (79 other events, 1594.8 us)

commit v3 on v2

--- a/solution.py
+++ b/solution.py
@@ -19,6 +19,7 @@
 PAIR_PAD = 8
 UNROLL = 8
 VMEM_LIMIT = 60 << 20
+PLACE_LIMIT = 16 << 20
 RIGHT_LIMIT = 24 << 20
 IN_FLIGHT = 5
 PATTERNS = ('ffnfnfnfnnfnnff', 'ffnfnfnfnfnfnfn', 'ffnfnfnfnfnfnfn', 'ffnfnfnfnnfnnff')
@@ -204,22 +205,16 @@
 
 
 def place_body(parts, lane, held, *rest):
-    blocks, out, landed, came, went = rest[:parts], rest[parts + held], rest[-3], rest[-2], rest[-1]
+    blocks, out, sems = rest[:parts], rest[parts + held], rest[-1]
     local = out.shape[1] // parts
     copies = []
     for mask in range(parts):
         start = pl.multiple_of(partner(parts, mask) * local + lane, LANES)
-        copies.append((
-            pltpu.make_async_copy(blocks[mask], landed.at[mask], came.at[mask]),
-            pltpu.make_async_copy(landed.at[mask], out.at[:, pl.ds(start, LANES)], went.at[mask]),
-        ))
-    for copy, _ in copies:
+        copies.append(pltpu.make_async_copy(blocks[mask], out.at[:, pl.ds(start, LANES)], sems.at[mask]))
+    for copy in copies:
         copy.start()
-    for copy, onward in copies:
+    for copy in copies:
         copy.wait()
-        onward.start()
-    for _, onward in copies:
-        onward.wait()
 
 
 def place(parts, lane, blocks, held=None):
@@ -228,12 +223,12 @@
     anywhere = pl.BlockSpec(memory_space=pl.ANY)
     return pl.pallas_call(
         functools.partial(place_body, parts, lane, len(held)),
-        in_specs=[anywhere] * (parts + len(held)),
+        in_specs=[pl.BlockSpec(memory_space=pltpu.VMEM)] * parts + [anywhere] * len(held),
         out_specs=anywhere,
         out_shape=jax.ShapeDtypeStruct((rows, rows * parts), F32),
-        scratch_shapes=[pltpu.VMEM((parts, rows, LANES), F32)] + [pltpu.SemaphoreType.DMA((parts,))] * 2,
+        scratch_shapes=[pltpu.SemaphoreType.DMA((parts,))],
         input_output_aliases={parts: 0} if held else {},
-        compiler_params=pltpu.CompilerParams(vmem_limit_bytes=VMEM_LIMIT),
+        compiler_params=pltpu.CompilerParams(vmem_limit_bytes=PLACE_LIMIT),
         cost_estimate=pl.CostEstimate(flops=0, bytes_accessed=rows * LANES * parts * 8, transcendentals=0),
         name="place",
     )(*blocks, *held)

time: 203 us -> 201 us (level)
  Pallas kernels: 30.5 us -> 28 us
    pallas_call x2, Pallas kernels: 5.15 us -> 2.87 us  [place(): pl.pallas_call(functools.partial(place_body, parts, lane, len(held)), in_...]
  transfers between devices with their start and end apart: 60 -> 60, of which waited for: 16 -> 17; matrix products, arithmetic and copies ran while one was open for 0% -> 0% of each run, Pallas kernels for 8% -> 7%
where the time goes in v3:
time: 201 us
  starting transfers between devices  122 us (61%)
  waiting for transfers between devices  49.4 us (25%)
  Pallas kernels  28 us (14%)
    ppermute x60, starting transfers between devices, send(): lax.ppermute(block, 'cols', [(s, s ^ mask) for s in range(self.parts)])  122 us
    ppermute x60, waiting for transfers between devices, send(): lax.ppermute(block, 'cols', [(s, s ^ mask) for s in range(self.parts)])  49.4 us
    pallas_call x2, Pallas kernels, right_chain(): pl.pallas_call(functools.partial(right_body, parts), grid=(1,), in_specs=...  13.3 us
    pallas_call x1, Pallas kernels, left_chain(): pl.pallas_call(functools.partial(left_body, parts), grid=(rows // block,)...  11.8 us
  transfers between devices with their start and end apart: 60, of which 17 were waited for; matrix products, arithmetic and copies ran while one was open for 0% of the time, Pallas kernels for 7%

profile of v3, /device:TPU:0, one launch (start us, length us, event | category | flops | bytes accessed | tf_op | source)
XLA Modules:
  0.0 201.0 jit_solution(2419538771457330084)
XLA Ops:
  0.0 11.8 %left_chain.1 = (f32[256,128]{1,0:T(8,128)}, f32[256,128]{1,0:T(8,128)}, f32[256,128]{1,0:T(8,128)}, f32[256,128]{1,0:T(8,128)}, f32[256,128]{1,0:T(8,128)}, /*i...) custom-call(f32[256,4096]{1,0:T(8,128)} %bitcast.8, ...), custom_call_target="tpu_custom_call" | custom-call | flops 3221225472 | bytes 8388608 | tf_op jit(solution)/shard_map/left_chain/pallas_call | solution.py:132
  11.9 3.0 %collective-permute-start = (f32[256,128]{1,0:T(8,128)}, f32[256,128]{1,0:T(8,128)S(1)}, u32[]{:S(2)}, u32[]{:S(2)}) collective-permute-start(f32[256,128]{1,0:T(8,128)} %get-tuple-element.183), channel_id=1, source_target_pairs={{0,2},{2,0},{4,6},{6,4},{8,10},{10,8},{12,14},{14,12},{16,18},{18,... | collective-permute-start | bytes 393224 | tf_op jit(solution)/shard_map/ppermute | solution.py:300
  14.9 3.6 %collective-permute-start.1 = (f32[256,128]{1,0:T(8,128)}, f32[256,128]{1,0:T(8,128)S(1)}, u32[]{:S(2)}, u32[]{:S(2)}) collective-permute-start(f32[256,128]{1,0:T(8,128)} %get-tuple-element.187), channel_id=1, source_target_pairs={{0,26},{2,24},{4,30},{6,28},{8,18},{10,16},{12,22},{14,20},{16,10}... | collective-permute-start | bytes 393224 | tf_op jit(solution)/shard_map/ppermute | solution.py:300
  19.0 3.8 %collective-permute-start.10 = (f32[256,128]{1,0:T(8,128)}, f32[256,128]{1,0:T(8,128)S(1)}, u32[]{:S(2)}, u32[]{:S(2)}) collective-permute-start(f32[256,128]{1,0:T(8,128)} %get-tuple-element.212), channel_id=1, source_target_pairs={{0,24},{2,26},{4,28},{6,30},{8,16},{10,18},{12,20},{14,22},{16,8},... | collective-permute-start | bytes 393224 | tf_op jit(solution)/shard_map/ppermute | solution.py:300
  25.9 7.4 %collective-permute-done.3.rest_8_ = f32[256,128]{1,0:T(8,128)S(1)} collective-permute-done((f32[256,128]{1,0:T(8,128)}, f32[256,128]{1,0:T(8,128)S(1)}, u32[]{:S(2)}, u32[]{:S(2)}) %collective-permute-start.3) | collective-permute-done | bytes 131104 | tf_op jit(solution)/shard_map/ppermute | solution.py:300
  34.4 2.7 %collective-permute-start.8 = (f32[256,128]{1,0:T(8,128)}, f32[256,128]{1,0:T(8,128)S(1)}, u32[]{:S(2)}, u32[]{:S(2)}) collective-permute-start(f32[256,128]{1,0:T(8,128)} %get-tuple-element.206), channel_id=1, source_target_pairs={{0,28},{2,30},{4,24},{6,26},{8,20},{10,22},{12,16},{14,18},{16,12}... | collective-permute-start | bytes 393224 | tf_op jit(solution)/shard_map/ppermute | solution.py:300
  37.1 2.9 %collective-permute-start.11 = (f32[256,128]{1,0:T(8,128)}, f32[256,128]{1,0:T(8,128)S(1)}, u32[]{:S(2)}, u32[]{:S(2)}) collective-permute-start(f32[256,128]{1,0:T(8,128)} %get-tuple-element.213), channel_id=1, source_target_pairs={{0,18},{2,16},{4,22},{6,20},{8,26},{10,24},{12,30},{14,28},{16,2},... | collective-permute-start | bytes 393224 | tf_op jit(solution)/shard_map/ppermute | solution.py:300
  46.1 8.0 %collective-permute-start.9 = (f32[256,128]{1,0:T(8,128)}, f32[256,128]{1,0:T(8,128)S(1)}, u32[]{:S(2)}, u32[]{:S(2)}) collective-permute-start(f32[256,128]{1,0:T(8,128)} %get-tuple-element.207), channel_id=1, source_target_pairs={{0,14},{2,12},{4,10},{6,8},{8,6},{10,4},{12,2},{14,0},{16,30},{18,... | collective-permute-start | bytes 393224 | tf_op jit(solution)/shard_map/ppermute | solution.py:300
  57.0 3.1 %collective-permute-done.13.rest_11_ = f32[256,128]{1,0:T(8,128)S(1)} collective-permute-done((f32[256,128]{1,0:T(8,128)}, f32[256,128]{1,0:T(8,128)S(1)}, u32[]{:S(2)}, u32[]{:S(2)}) %collective-permute-start.13) | collective-permute-done | bytes 131104 | tf_op jit(solution)/shard_map/ppermute | solution.py:300
  61.3 3.3 %collective-permute-start.16 = (f32[256,128]{1,0:T(8,128)S(1)}, f32[256,128]{1,0:T(8,128)S(1)}, u32[]{:S(2)}, u32[]{:S(2)}) collective-permute-start(f32[256,128]{1,0:T(8,128)S(1)} %copy-done.17), channel_id=1, source_target_pairs={{0,26},{2,24},{4,30},{6,28},{8,18},{10,16},{12,22},{14,20},{16,10}... | collective-permute-start | bytes 393224 | tf_op jit(solution)/shard_map/ppermute | solution.py:300
  64.6 4.8 %collective-permute-start.21 = (f32[256,128]{1,0:T(8,128)S(1)}, f32[256,128]{1,0:T(8,128)S(1)}, u32[]{:S(2)}, u32[]{:S(2)}) collective-permute-start(f32[256,128]{1,0:T(8,128)S(1)} %copy-done.15), channel_id=1, source_target_pairs={{0,16},{2,18},{4,20},{6,22},{8,24},{10,26},{12,28},{14,30},{16,0},... | collective-permute-start | bytes 393224 | tf_op jit(solution)/shard_map/ppermute | solution.py:300
  70.7 4.1 %collective-permute-start.23 = (f32[256,128]{1,0:T(8,128)S(1)}, f32[256,128]{1,0:T(8,128)S(1)}, u32[]{:S(2)}, u32[]{:S(2)}) collective-permute-start(f32[256,128]{1,0:T(8,128)S(1)} %copy-done.14), channel_id=1, source_target_pairs={{0,24},{2,26},{4,28},{6,30},{8,16},{10,18},{12,20},{14,22},{16,8},... | collective-permute-start | bytes 393224 | tf_op jit(solution)/shard_map/ppermute | solution.py:300
  74.9 6.6 %right_chain.2 = (f32[256,128]{1,0:T(8,128)S(1)}, f32[256,128]{1,0:T(8,128)S(1)}, f32[256,128]{1,0:T(8,128)S(1)}, f32[256,128]{1,0:T(8,128)S(1)}, f32[256,128]{1...) custom-call(f32[4096,3]{1,0:T(8,128)S(1)} %exponential_bitcast_fusio, ...), custom_call_target="tpu_custom_call" | custom-call | flops 1610612736 | bytes 6291456 | tf_op jit(solution)/shard_map/right_chain/pallas_call | solution.py:194
  83.5 4.2 %collective-permute-start.22 = (f32[256,128]{1,0:T(8,128)S(1)}, f32[256,128]{1,0:T(8,128)S(1)}, u32[]{:S(2)}, u32[]{:S(2)}) collective-permute-start(f32[256,128]{1,0:T(8,128)S(1)} %copy-done.10), channel_id=1, source_target_pairs={{0,10},{2,8},{4,14},{6,12},{8,2},{10,0},{12,6},{14,4},{16,26},{18,... | collective-permute-start | bytes 393224 | tf_op jit(solution)/shard_map/ppermute | solution.py:300
  87.7 3.9 %collective-permute-start.24 = (f32[256,128]{1,0:T(8,128)S(1)}, f32[256,128]{1,0:T(8,128)S(1)}, u32[]{:S(2)}, u32[]{:S(2)}) collective-permute-start(f32[256,128]{1,0:T(8,128)S(1)} %copy-done.9), channel_id=1, source_target_pairs={{0,18},{2,16},{4,22},{6,20},{8,26},{10,24},{12,30},{14,28},{16,2},... | collective-permute-start | bytes 393224 | tf_op jit(solution)/shard_map/ppermute | solution.py:300
  93.6 4.9 %collective-permute-start.28 = (f32[256,128]{1,0:T(8,128)S(1)}, f32[256,128]{1,0:T(8,128)S(1)}, u32[]{:S(2)}, u32[]{:S(2)}) collective-permute-start(f32[256,128]{1,0:T(8,128)S(1)} %copy-done.7), channel_id=1, source_target_pairs={{0,22},{2,20},{4,18},{6,16},{8,30},{10,28},{12,26},{14,24},{16,6},... | collective-permute-start | bytes 393224 | tf_op jit(solution)/shard_map/ppermute | solution.py:300
  99.2 2.9 %collective-permute-start.29 = (f32[256,128]{1,0:T(8,128)S(1)}, f32[256,128]{1,0:T(8,128)S(1)}, u32[]{:S(2)}, u32[]{:S(2)}) collective-permute-start(f32[256,128]{1,0:T(8,128)S(1)} %copy-done.5), channel_id=1, source_target_pairs={{0,30},{2,28},{4,26},{6,24},{8,22},{10,20},{12,18},{14,16},{16,14}... | collective-permute-start | bytes 393224 | tf_op jit(solution)/shard_map/ppermute | solution.py:300
  108.6 5.1 %collective-permute-start.34 = (f32[256,128]{1,0:T(8,128)S(1)}, f32[256,128]{1,0:T(8,128)S(1)}, u32[]{:S(2)}, u32[]{:S(2)}) collective-permute-start(f32[256,128]{1,0:T(8,128)S(1)} %get-tuple-element.287), channel_id=1, source_target_pairs={{0,26},{2,24},{4,30},{6,28},{8,18},{10,16},{12,22},{14,20},{16,10}... | collective-permute-start | bytes 393224 | tf_op jit(solution)/shard_map/ppermute | solution.py:300
  113.6 5.4 %collective-permute-start.39 = (f32[256,128]{1,0:T(8,128)S(1)}, f32[256,128]{1,0:T(8,128)S(1)}, u32[]{:S(2)}, u32[]{:S(2)}) collective-permute-start(f32[256,128]{1,0:T(8,128)S(1)} %get-tuple-element.298), channel_id=1, source_target_pairs={{0,16},{2,18},{4,20},{6,22},{8,24},{10,26},{12,28},{14,30},{16,0},... | collective-permute-start | bytes 393224 | tf_op jit(solution)/shard_map/ppermute | solution.py:300
  119.1 6.6 %right_chain.3 = (f32[256,128]{1,0:T(8,128)S(1)}, f32[256,128]{1,0:T(8,128)S(1)}, f32[256,128]{1,0:T(8,128)S(1)}, f32[256,128]{1,0:T(8,128)S(1)}, f32[256,128]{1...) custom-call(f32[4096,3]{1,0:T(8,128)S(1)} %exponential_bitcast_fusio, ...), custom_call_target="tpu_custom_call" | custom-call | flops 1610612736 | bytes 6291456 | tf_op jit(solution)/shard_map/right_chain/pallas_call | solution.py:194
  128.2 2.7 %collective-permute-start.40 = (f32[256,128]{1,0:T(8,128)S(1)}, f32[256,128]{1,0:T(8,128)S(1)}, u32[]{:S(2)}, u32[]{:S(2)}) collective-permute-start(f32[256,128]{1,0:T(8,128)S(1)} %get-tuple-element.299), channel_id=1, source_target_pairs={{0,10},{2,8},{4,14},{6,12},{8,2},{10,0},{12,6},{14,4},{16,26},{18,... | collective-permute-start | bytes 393224 | tf_op jit(solution)/shard_map/ppermute | solution.py:300
  131.8 3.7 %collective-permute-start.53 = (f32[256,128]{1,0:T(8,128)S(1)}, f32[256,128]{1,0:T(8,128)S(1)}, u32[]{:S(2)}, u32[]{:S(2)}) collective-permute-start(f32[256,128]{1,0:T(8,128)S(1)} %get-tuple-element.327), channel_id=1, source_target_pairs={{0,18},{2,16},{4,22},{6,20},{8,26},{10,24},{12,30},{14,28},{16,2},... | collective-permute-start | bytes 393224 | tf_op jit(solution)/shard_map/ppermute | solution.py:300
  137.1 5.5 %collective-permute-start.36 = (f32[256,128]{1,0:T(8,128)S(1)}, f32[256,128]{1,0:T(8,128)S(1)}, u32[]{:S(2)}, u32[]{:S(2)}) collective-permute-start(f32[256,128]{1,0:T(8,128)S(1)} %get-tuple-element.289), channel_id=1, source_target_pairs={{0,22},{2,20},{4,18},{6,16},{8,30},{10,28},{12,26},{14,24},{16,6},... | collective-permute-start | bytes 393224 | tf_op jit(solution)/shard_map/ppermute | solution.py:300
  145.7 5.2 %collective-permute-done.53.rest_9_ = f32[256,128]{1,0:T(8,128)S(1)} collective-permute-done((f32[256,128]{1,0:T(8,128)S(1)}, f32[256,128]{1,0:T(8,128)S(1)}, u32[]{:S(2)}, u32[]{:S(2)}) %collective-permute-start.53) | collective-permute-done | bytes 131104 | tf_op jit(solution)/shard_map/ppermute | solution.py:300
  154.6 4.1 %collective-permute-start.37 = (f32[256,128]{1,0:T(8,128)S(1)}, f32[256,128]{1,0:T(8,128)S(1)}, u32[]{:S(2)}, u32[]{:S(2)}) collective-permute-start(f32[256,128]{1,0:T(8,128)S(1)} %get-tuple-element.290), channel_id=1, source_target_pairs={{0,26},{2,24},{4,30},{6,28},{8,18},{10,16},{12,22},{14,20},{16,10}... | collective-permute-start | bytes 393224 | tf_op jit(solution)/shard_map/ppermute | solution.py:300
  158.7 3.9 %collective-permute-start.42 = (f32[256,128]{1,0:T(8,128)S(1)}, f32[256,128]{1,0:T(8,128)S(1)}, u32[]{:S(2)}, u32[]{:S(2)}) collective-permute-start(f32[256,128]{1,0:T(8,128)S(1)} %get-tuple-element.301), channel_id=1, source_target_pairs={{0,16},{2,18},{4,20},{6,22},{8,24},{10,26},{12,28},{14,30},{16,0},... | collective-permute-start | bytes 393224 | tf_op jit(solution)/shard_map/ppermute | solution.py:300
  166.3 3.1 %collective-permute-done.42.rest_8_ = f32[256,128]{1,0:T(8,128)S(1)} collective-permute-done((f32[256,128]{1,0:T(8,128)S(1)}, f32[256,128]{1,0:T(8,128)S(1)}, u32[]{:S(2)}, u32[]{:S(2)}) %collective-permute-start.42) | collective-permute-done | bytes 131104 | tf_op jit(solution)/shard_map/ppermute | solution.py:300
  169.3 3.5 %collective-permute-done.48.rest_4_ = f32[256,128]{1,0:T(8,128)S(1)} collective-permute-done((f32[256,128]{1,0:T(8,128)S(1)}, f32[256,128]{1,0:T(8,128)S(1)}, u32[]{:S(2)}, u32[]{:S(2)}) %collective-permute-start.48) | collective-permute-done | bytes 131104 | tf_op jit(solution)/shard_map/ppermute | solution.py:300
  172.9 5.8 %collective-permute-start.56 = (f32[256,128]{1,0:T(8,128)S(1)}, f32[256,128]{1,0:T(8,128)S(1)}, u32[]{:S(2)}, u32[]{:S(2)}) collective-permute-start(f32[256,128]{1,0:T(8,128)S(1)} %get-tuple-element.330), channel_id=1, source_target_pairs={{0,18},{2,16},{4,22},{6,20},{8,26},{10,24},{12,30},{14,28},{16,2},... | collective-permute-start | bytes 393224 | tf_op jit(solution)/shard_map/ppermute | solution.py:300
  178.6 3.6 %collective-permute-start.58 = (f32[256,128]{1,0:T(8,128)S(1)}, f32[256,128]{1,0:T(8,128)S(1)}, u32[]{:S(2)}, u32[]{:S(2)}) collective-permute-start(f32[256,128]{1,0:T(8,128)S(1)} %get-tuple-element.333), channel_id=1, source_target_pairs={{0,22},{2,20},{4,18},{6,16},{8,30},{10,28},{12,26},{14,24},{16,6},... | collective-permute-start | bytes 393224 | tf_op jit(solution)/shard_map/ppermute | solution.py:300
  187.4 4.1 %collective-permute-done.56.rest_9_ = f32[256,128]{1,0:T(8,128)S(1)} collective-permute-done((f32[256,128]{1,0:T(8,128)S(1)}, f32[256,128]{1,0:T(8,128)S(1)}, u32[]{:S(2)}, u32[]{:S(2)}) %collective-permute-start.56) | collective-permute-done | bytes 131104 | tf_op jit(solution)/shard_map/ppermute | solution.py:300
  194.8 4.8 %collective-permute-done.57.rest_10_ = f32[256,128]{1,0:T(8,128)S(1)} collective-permute-done((f32[256,128]{1,0:T(8,128)S(1)}, f32[256,128]{1,0:T(8,128)S(1)}, u32[]{:S(2)}, u32[]{:S(2)}) %collective-permute-start.57) | collective-permute-done | bytes 131104 | tf_op jit(solution)/shard_map/ppermute | solution.py:300
  (134 shorter events, 52.5 us)
Async XLA Ops:
  18.4 14.8 %collective-permute-start.3 = (f32[256,128]{1,0:T(8,128)}, f32[256,128]{1,0:T(8,128)S(1)}, u32[]{:S(2)}, u32[]{:S(2)}) collective-permute-start(f32[256,128]{1,0:T(8,128)} %get-tuple-element.193), channel_id=1, source_target_pairs={{0,16},{2,18},{4,20},{6,22},{8,24},{10,26},{12,28},{14,30},{16,0},... | collective-permute-start | bytes 393224 | tf_op jit(solution)/shard_map/ppermute | solution.py:300
  18.4 16.0 %collective-permute-start.6 = (f32[256,128]{1,0:T(8,128)}, f32[256,128]{1,0:T(8,128)S(1)}, u32[]{:S(2)}, u32[]{:S(2)}) collective-permute-start(f32[256,128]{1,0:T(8,128)} %get-tuple-element.198), channel_id=1, source_target_pairs={{0,8},{2,10},{4,12},{6,14},{8,0},{10,2},{12,4},{14,6},{16,24},{18,... | collective-permute-start | bytes 393224 | tf_op jit(solution)/shard_map/ppermute | solution.py:300
  19.0 18.1 %collective-permute-start.10 = (f32[256,128]{1,0:T(8,128)}, f32[256,128]{1,0:T(8,128)S(1)}, u32[]{:S(2)}, u32[]{:S(2)}) collective-permute-start(f32[256,128]{1,0:T(8,128)} %get-tuple-element.212), channel_id=1, source_target_pairs={{0,24},{2,26},{4,28},{6,30},{8,16},{10,18},{12,20},{14,22},{16,8},... | collective-permute-start | bytes 393224 | tf_op jit(solution)/shard_map/ppermute | solution.py:300
  22.8 18.0 %collective-permute-start.7 = (f32[256,128]{1,0:T(8,128)}, f32[256,128]{1,0:T(8,128)S(1)}, u32[]{:S(2)}, u32[]{:S(2)}) collective-permute-start(f32[256,128]{1,0:T(8,128)} %get-tuple-element.202), channel_id=1, source_target_pairs={{0,12},{2,14},{4,8},{6,10},{8,4},{10,6},{12,0},{14,2},{16,28},{18,... | collective-permute-start | bytes 393224 | tf_op jit(solution)/shard_map/ppermute | solution.py:300
  24.3 18.3 %collective-permute-start.2 = (f32[256,128]{1,0:T(8,128)}, f32[256,128]{1,0:T(8,128)S(1)}, u32[]{:S(2)}, u32[]{:S(2)}) collective-permute-start(f32[256,128]{1,0:T(8,128)} %get-tuple-element.188), channel_id=1, source_target_pairs={{0,4},{2,6},{4,0},{6,2},{8,12},{10,14},{12,8},{14,10},{16,20},{18,... | collective-permute-start | bytes 393224 | tf_op jit(solution)/shard_map/ppermute | solution.py:300
  37.1 19.5 %collective-permute-start.11 = (f32[256,128]{1,0:T(8,128)}, f32[256,128]{1,0:T(8,128)S(1)}, u32[]{:S(2)}, u32[]{:S(2)}) collective-permute-start(f32[256,128]{1,0:T(8,128)} %get-tuple-element.213), channel_id=1, source_target_pairs={{0,18},{2,16},{4,22},{6,20},{8,26},{10,24},{12,30},{14,28},{16,2},... | collective-permute-start | bytes 393224 | tf_op jit(solution)/shard_map/ppermute | solution.py:300
  40.8 19.3 %collective-permute-start.13 = (f32[256,128]{1,0:T(8,128)}, f32[256,128]{1,0:T(8,128)S(1)}, u32[]{:S(2)}, u32[]{:S(2)}) collective-permute-start(f32[256,128]{1,0:T(8,128)} %get-tuple-element.219), channel_id=1, source_target_pairs={{0,22},{2,20},{4,18},{6,16},{8,30},{10,28},{12,26},{14,24},{16,6},... | collective-permute-start | bytes 393224 | tf_op jit(solution)/shard_map/ppermute | solution.py:300
  42.6 18.7 %collective-permute-start.14 = (f32[256,128]{1,0:T(8,128)}, f32[256,128]{1,0:T(8,128)S(1)}, u32[]{:S(2)}, u32[]{:S(2)}) collective-permute-start(f32[256,128]{1,0:T(8,128)} %get-tuple-element.225), channel_id=1, source_target_pairs={{0,30},{2,28},{4,26},{6,24},{8,22},{10,20},{12,18},{14,16},{16,14}... | collective-permute-start | bytes 393224 | tf_op jit(solution)/shard_map/ppermute | solution.py:300
  44.7 20.0 %collective-permute-start.5 = (f32[256,128]{1,0:T(8,128)}, f32[256,128]{1,0:T(8,128)S(1)}, u32[]{:S(2)}, u32[]{:S(2)}) collective-permute-start(f32[256,128]{1,0:T(8,128)} %get-tuple-element.195), channel_id=1, source_target_pairs={{0,6},{2,4},{4,2},{6,0},{8,14},{10,12},{12,10},{14,8},{16,22},{18,... | collective-permute-start | bytes 393224 | tf_op jit(solution)/shard_map/ppermute | solution.py:300
  46.1 23.3 %collective-permute-start.9 = (f32[256,128]{1,0:T(8,128)}, f32[256,128]{1,0:T(8,128)S(1)}, u32[]{:S(2)}, u32[]{:S(2)}) collective-permute-start(f32[256,128]{1,0:T(8,128)} %get-tuple-element.207), channel_id=1, source_target_pairs={{0,14},{2,12},{4,10},{6,8},{8,6},{10,4},{12,2},{14,0},{16,30},{18,... | collective-permute-start | bytes 393224 | tf_op jit(solution)/shard_map/ppermute | solution.py:300
  60.1 21.4 %collective-permute-start.15 = (f32[256,128]{1,0:T(8,128)S(1)}, f32[256,128]{1,0:T(8,128)S(1)}, u32[]{:S(2)}, u32[]{:S(2)}) collective-permute-start(f32[256,128]{1,0:T(8,128)S(1)} %copy-done.18), channel_id=1, source_target_pairs={{0,2},{2,0},{4,6},{6,4},{8,10},{10,8},{12,14},{14,12},{16,18},{18,... | collective-permute-start | bytes 393224 | tf_op jit(solution)/shard_map/ppermute | solution.py:300
  61.3 20.3 %collective-permute-start.16 = (f32[256,128]{1,0:T(8,128)S(1)}, f32[256,128]{1,0:T(8,128)S(1)}, u32[]{:S(2)}, u32[]{:S(2)}) collective-permute-start(f32[256,128]{1,0:T(8,128)S(1)} %copy-done.17), channel_id=1, source_target_pairs={{0,26},{2,24},{4,30},{6,28},{8,18},{10,16},{12,22},{14,20},{16,10}... | collective-permute-start | bytes 393224 | tf_op jit(solution)/shard_map/ppermute | solution.py:300
  64.6 18.8 %collective-permute-start.21 = (f32[256,128]{1,0:T(8,128)S(1)}, f32[256,128]{1,0:T(8,128)S(1)}, u32[]{:S(2)}, u32[]{:S(2)}) collective-permute-start(f32[256,128]{1,0:T(8,128)S(1)} %copy-done.15), channel_id=1, source_target_pairs={{0,16},{2,18},{4,20},{6,22},{8,24},{10,26},{12,28},{14,30},{16,0},... | collective-permute-start | bytes 393224 | tf_op jit(solution)/shard_map/ppermute | solution.py:300
  70.7 17.0 %collective-permute-start.23 = (f32[256,128]{1,0:T(8,128)S(1)}, f32[256,128]{1,0:T(8,128)S(1)}, u32[]{:S(2)}, u32[]{:S(2)}) collective-permute-start(f32[256,128]{1,0:T(8,128)S(1)} %copy-done.14), channel_id=1, source_target_pairs={{0,24},{2,26},{4,28},{6,30},{8,16},{10,18},{12,20},{14,22},{16,8},... | collective-permute-start | bytes 393224 | tf_op jit(solution)/shard_map/ppermute | solution.py:300
  81.7 16.8 %collective-permute-start.19 = (f32[256,128]{1,0:T(8,128)S(1)}, f32[256,128]{1,0:T(8,128)S(1)}, u32[]{:S(2)}, u32[]{:S(2)}) collective-permute-start(f32[256,128]{1,0:T(8,128)S(1)} %copy-done.11), channel_id=1, source_target_pairs={{0,28},{2,30},{4,24},{6,26},{8,20},{10,22},{12,16},{14,18},{16,12}... | collective-permute-start | bytes 393224 | tf_op jit(solution)/shard_map/ppermute | solution.py:300
  83.5 15.8 %collective-permute-start.22 = (f32[256,128]{1,0:T(8,128)S(1)}, f32[256,128]{1,0:T(8,128)S(1)}, u32[]{:S(2)}, u32[]{:S(2)}) collective-permute-start(f32[256,128]{1,0:T(8,128)S(1)} %copy-done.10), channel_id=1, source_target_pairs={{0,10},{2,8},{4,14},{6,12},{8,2},{10,0},{12,6},{14,4},{16,26},{18,... | collective-permute-start | bytes 393224 | tf_op jit(solution)/shard_map/ppermute | solution.py:300
  87.7 16.7 %collective-permute-start.24 = (f32[256,128]{1,0:T(8,128)S(1)}, f32[256,128]{1,0:T(8,128)S(1)}, u32[]{:S(2)}, u32[]{:S(2)}) collective-permute-start(f32[256,128]{1,0:T(8,128)S(1)} %copy-done.9), channel_id=1, source_target_pairs={{0,18},{2,16},{4,22},{6,20},{8,26},{10,24},{12,30},{14,28},{16,2},... | collective-permute-start | bytes 393224 | tf_op jit(solution)/shard_map/ppermute | solution.py:300
  93.6 15.0 %collective-permute-start.28 = (f32[256,128]{1,0:T(8,128)S(1)}, f32[256,128]{1,0:T(8,128)S(1)}, u32[]{:S(2)}, u32[]{:S(2)}) collective-permute-start(f32[256,128]{1,0:T(8,128)S(1)} %copy-done.7), channel_id=1, source_target_pairs={{0,22},{2,20},{4,18},{6,16},{8,30},{10,28},{12,26},{14,24},{16,6},... | collective-permute-start | bytes 393224 | tf_op jit(solution)/shard_map/ppermute | solution.py:300
  98.5 15.1 %collective-permute-start.20 = (f32[256,128]{1,0:T(8,128)S(1)}, f32[256,128]{1,0:T(8,128)S(1)}, u32[]{:S(2)}, u32[]{:S(2)}) collective-permute-start(f32[256,128]{1,0:T(8,128)S(1)} %copy-done.6), channel_id=1, source_target_pairs={{0,6},{2,4},{4,2},{6,0},{8,14},{10,12},{12,10},{14,8},{16,22},{18,... | collective-permute-start | bytes 393224 | tf_op jit(solution)/shard_map/ppermute | solution.py:300
  104.4 14.6 %collective-permute-start.25 = (f32[256,128]{1,0:T(8,128)S(1)}, f32[256,128]{1,0:T(8,128)S(1)}, u32[]{:S(2)}, u32[]{:S(2)}) collective-permute-start(f32[256,128]{1,0:T(8,128)S(1)} %copy-done.4), channel_id=1, source_target_pairs={{0,12},{2,14},{4,8},{6,10},{8,4},{10,6},{12,0},{14,2},{16,28},{18,... | collective-permute-start | bytes 393224 | tf_op jit(solution)/shard_map/ppermute | solution.py:300
  106.4 19.4 %collective-permute-start.30 = (f32[256,128]{1,0:T(8,128)S(1)}, f32[256,128]{1,0:T(8,128)S(1)}, u32[]{:S(2)}, u32[]{:S(2)}) collective-permute-start(f32[256,128]{1,0:T(8,128)S(1)} %get-tuple-element.277), channel_id=1, source_target_pairs={{0,2},{2,0},{4,6},{6,4},{8,10},{10,8},{12,14},{14,12},{16,18},{18,... | collective-permute-start | bytes 393224 | tf_op jit(solution)/shard_map/ppermute | solution.py:300
  108.6 17.2 %collective-permute-start.34 = (f32[256,128]{1,0:T(8,128)S(1)}, f32[256,128]{1,0:T(8,128)S(1)}, u32[]{:S(2)}, u32[]{:S(2)}) collective-permute-start(f32[256,128]{1,0:T(8,128)S(1)} %get-tuple-element.287), channel_id=1, source_target_pairs={{0,26},{2,24},{4,30},{6,28},{8,18},{10,16},{12,22},{14,20},{16,10}... | collective-permute-start | bytes 393224 | tf_op jit(solution)/shard_map/ppermute | solution.py:300
  113.6 17.2 %collective-permute-start.45 = (f32[256,128]{1,0:T(8,128)S(1)}, f32[256,128]{1,0:T(8,128)S(1)}, u32[]{:S(2)}, u32[]{:S(2)}) collective-permute-start(f32[256,128]{1,0:T(8,128)S(1)} %get-tuple-element.308), channel_id=1, source_target_pairs={{0,8},{2,10},{4,12},{6,14},{8,0},{10,2},{12,4},{14,6},{16,24},{18,... | collective-permute-start | bytes 393224 | tf_op jit(solution)/shard_map/ppermute | solution.py:300
  113.6 14.6 %collective-permute-start.39 = (f32[256,128]{1,0:T(8,128)S(1)}, f32[256,128]{1,0:T(8,128)S(1)}, u32[]{:S(2)}, u32[]{:S(2)}) collective-permute-start(f32[256,128]{1,0:T(8,128)S(1)} %get-tuple-element.298), channel_id=1, source_target_pairs={{0,16},{2,18},{4,20},{6,22},{8,24},{10,26},{12,28},{14,30},{16,0},... | collective-permute-start | bytes 393224 | tf_op jit(solution)/shard_map/ppermute | solution.py:300
  131.8 19.0 %collective-permute-start.53 = (f32[256,128]{1,0:T(8,128)S(1)}, f32[256,128]{1,0:T(8,128)S(1)}, u32[]{:S(2)}, u32[]{:S(2)}) collective-permute-start(f32[256,128]{1,0:T(8,128)S(1)} %get-tuple-element.327), channel_id=1, source_target_pairs={{0,18},{2,16},{4,22},{6,20},{8,26},{10,24},{12,30},{14,28},{16,2},... | collective-permute-start | bytes 393224 | tf_op jit(solution)/shard_map/ppermute | solution.py:300
  137.1 17.5 %collective-permute-start.36 = (f32[256,128]{1,0:T(8,128)S(1)}, f32[256,128]{1,0:T(8,128)S(1)}, u32[]{:S(2)}, u32[]{:S(2)}) collective-permute-start(f32[256,128]{1,0:T(8,128)S(1)} %get-tuple-element.289), channel_id=1, source_target_pairs={{0,22},{2,20},{4,18},{6,16},{8,30},{10,28},{12,26},{14,24},{16,6},... | collective-permute-start | bytes 393224 | tf_op jit(solution)/shard_map/ppermute | solution.py:300
  142.7 16.1 %collective-permute-start.41 = (f32[256,128]{1,0:T(8,128)S(1)}, f32[256,128]{1,0:T(8,128)S(1)}, u32[]{:S(2)}, u32[]{:S(2)}) collective-permute-start(f32[256,128]{1,0:T(8,128)S(1)} %get-tuple-element.300), channel_id=1, source_target_pairs={{0,30},{2,28},{4,26},{6,24},{8,22},{10,20},{12,18},{14,16},{16,14}... | collective-permute-start | bytes 393224 | tf_op jit(solution)/shard_map/ppermute | solution.py:300
  143.9 18.8 %collective-permute-start.47 = (f32[256,128]{1,0:T(8,128)S(1)}, f32[256,128]{1,0:T(8,128)S(1)}, u32[]{:S(2)}, u32[]{:S(2)}) collective-permute-start(f32[256,128]{1,0:T(8,128)S(1)} %get-tuple-element.310), channel_id=1, source_target_pairs={{0,6},{2,4},{4,2},{6,0},{8,14},{10,12},{12,10},{14,8},{16,22},{18,... | collective-permute-start | bytes 393224 | tf_op jit(solution)/shard_map/ppermute | solution.py:300
  164.2 14.5 %collective-permute-start.49 = (f32[256,128]{1,0:T(8,128)S(1)}, f32[256,128]{1,0:T(8,128)S(1)}, u32[]{:S(2)}, u32[]{:S(2)}) collective-permute-start(f32[256,128]{1,0:T(8,128)S(1)} %get-tuple-element.315), channel_id=1, source_target_pairs={{0,12},{2,14},{4,8},{6,10},{8,4},{10,6},{12,0},{14,2},{16,28},{18,... | collective-permute-start | bytes 393224 | tf_op jit(solution)/shard_map/ppermute | solution.py:300
  164.2 18.0 %collective-permute-start.38 = (f32[256,128]{1,0:T(8,128)S(1)}, f32[256,128]{1,0:T(8,128)S(1)}, u32[]{:S(2)}, u32[]{:S(2)}) collective-permute-start(f32[256,128]{1,0:T(8,128)S(1)} %get-tuple-element.291), channel_id=1, source_target_pairs={{0,4},{2,6},{4,0},{6,2},{8,12},{10,14},{12,8},{14,10},{16,20},{18,... | collective-permute-start | bytes 393224 | tf_op jit(solution)/shard_map/ppermute | solution.py:300
  172.9 18.6 %collective-permute-start.56 = (f32[256,128]{1,0:T(8,128)S(1)}, f32[256,128]{1,0:T(8,128)S(1)}, u32[]{:S(2)}, u32[]{:S(2)}) collective-permute-start(f32[256,128]{1,0:T(8,128)S(1)} %get-tuple-element.330), channel_id=1, source_target_pairs={{0,18},{2,16},{4,22},{6,20},{8,26},{10,24},{12,30},{14,28},{16,2},... | collective-permute-start | bytes 393224 | tf_op jit(solution)/shard_map/ppermute | solution.py:300
  178.6 16.1 %collective-permute-start.58 = (f32[256,128]{1,0:T(8,128)S(1)}, f32[256,128]{1,0:T(8,128)S(1)}, u32[]{:S(2)}, u32[]{:S(2)}) collective-permute-start(f32[256,128]{1,0:T(8,128)S(1)} %get-tuple-element.333), channel_id=1, source_target_pairs={{0,22},{2,20},{4,18},{6,16},{8,30},{10,28},{12,26},{14,24},{16,6},... | collective-permute-start | bytes 393224 | tf_op jit(solution)/shard_map/ppermute | solution.py:300
  (47 other events, 652.5 us)

commit v4 on v3

--- a/solution.py
+++ b/solution.py
@@ -22,7 +22,7 @@
 PLACE_LIMIT = 16 << 20
 RIGHT_LIMIT = 24 << 20
 IN_FLIGHT = 5
-PATTERNS = ('ffnfnfnfnnfnnff', 'ffnfnfnfnfnfnfn', 'ffnfnfnfnfnfnfn', 'ffnfnfnfnnfnnff')
+PATTERNS = ('ffnfnfnfnnfnnff', 'ffnfnfnfnfnfnfn', 'ffnfnfnfnfnfnfn', 'nfnfnfnfnfnfnff')
 LATE = 5
 AHEAD = 5
 BF = jnp.bfloat16
@@ -39,6 +39,19 @@
 def split_matrix(matrix):
     high = matrix.astype(ml_dtypes.bfloat16)
     return high, (matrix - high.astype(np.float64)).astype(ml_dtypes.bfloat16)
+
+
+def steady(matrix):
+    column = matrix[:, 0]
+    spectrum = np.fft.fft(column).real
+
+    def fault(factor):
+        high, low = split_matrix(factor * column)
+        kept = (high.astype(np.float64) + low.astype(np.float64)) / factor
+        return np.abs(np.fft.fft(kept - column).real / spectrum).max()
+
+    factor = min((1.0 + step / 1000.0 for step in range(1000)), key=fault)
+    return factor * matrix, factor
 
 
 def lane_side(matrix):
@@ -85,13 +98,13 @@
     return lax.axis_index("cols").astype(jnp.int32) ^ mask
 
 
-def left_body(parts, x_ref, field_ref, right_ref, left_ref, *rest):
+def left_body(parts, shrink, x_ref, field_ref, right_ref, left_ref, *rest):
     outs, gain_ref, work = rest[:-2], rest[-2], rest[-1]
     rows = x_ref.shape[0]
 
     @pl.when(pl.program_id(0) == 0)
     def _():
-        gain = [jnp.exp(coupling * (2.0 * field_ref[moment].astype(F32) - 1.0)) for moment in range(SLICES)]
+        gain = [shrink * jnp.exp(coupling * (2.0 * field_ref[moment].astype(F32) - 1.0)) for moment in range(SLICES)]
         for moment in range(SLICES):
             for c in range(LX // 2):
                 row = jnp.broadcast_to(gain[moment][:, c * LANES : (c + 1) * LANES], (8, LANES))
@@ -126,11 +139,11 @@
                 ref[group * 16 + 8 : group * 16 + 16, :] = below
 
 
-def left_chain(parts, block, x, field, right, left):
+def left_chain(parts, shrink, block, x, field, right, left):
     rows, sites = x.shape
     whole = lambda array: pl.BlockSpec(array.shape, lambda g: (0,) * array.ndim)
     outs = pl.pallas_call(
-        functools.partial(left_body, parts),
+        functools.partial(left_body, parts, shrink),
         grid=(rows // block,),
         in_specs=[pl.BlockSpec((block, sites), lambda g: (g, 0)), whole(field), whole(right), whole(left)],
         out_specs=[pl.BlockSpec((block, LANES), lambda g: (g, 0))] * (2 * parts),
@@ -317,17 +330,17 @@
     _, rows, sites = green_by_column.shape
     parts = lax.axis_size("cols")
     x = green_by_column.reshape(rows, sites)
-    loss = jnp.exp(-coupling * (2.0 * field[0].astype(F32) - 1.0)).T
-    right = lane_side(circulant(LY, hop_rate))
-    left = row_side(circulant(LX, hop_rate))
-    left_y = row_side(circulant(LY, -hop_rate))
-    left_x = row_side(circulant(LX, -hop_rate))
+    (fwd_x, fwd_x_factor), (fwd_y, fwd_y_factor) = steady(circulant(LX, hop_rate)), steady(circulant(LY, hop_rate))
+    (inv_x, inv_x_factor), (inv_y, inv_y_factor) = steady(circulant(LX, -hop_rate)), steady(circulant(LY, -hop_rate))
+    loss = jnp.exp(-coupling * (2.0 * field[0].astype(F32) - 1.0)).T / (inv_x_factor * inv_y_factor)
+    shrink = 1.0 / (fwd_x_factor * fwd_y_factor)
+    right, left, left_y, left_x = lane_side(fwd_y), row_side(fwd_x), row_side(inv_y), row_side(inv_x)
     links = Links(parts)
 
     def chain(pieces):
         return right_chain(parts, loss, left_y, left_x, [pieces[mask]["value"] for mask in range(parts)])
 
-    halves_ = left_chain(parts, rows // 4, x, field.transpose(1, 0, 2), right, left)
+    halves_ = left_chain(parts, shrink, rows // 4, x, field.transpose(1, 0, 2), right, left)
     sent = [{0: {"value": blocks[0]}} for blocks in halves_]
     done = []
     for h in range(2):

time: 201 us -> 203 us (level)
  waiting for transfers between devices: 49.4 us -> 54.2 us
  starting transfers between devices: 122 us -> 119 us
    ppermute x60, waiting for transfers between devices: 49.4 us -> 54.2 us  [send(): lax.ppermute(block, 'cols', [(s, s ^ mask) for s in range(self.parts)])]
    ppermute x60, starting transfers between devices: 122 us -> 119 us  [send(): lax.ppermute(block, 'cols', [(s, s ^ mask) for s in range(self.parts)])]
  transfers between devices with their start and end apart: 60 -> 60, of which waited for: 17 -> 16; matrix products, arithmetic and copies ran while one was open for 0% -> 0% of each run, Pallas kernels for 7% -> 7%
where the time goes in v4:
time: 203 us; the launch traced here: 202 us
  starting transfers between devices  119 us (59%)
  waiting for transfers between devices  54.2 us (27%)
  Pallas kernels  28 us (14%)
    ppermute x60, starting transfers between devices, send(): lax.ppermute(block, 'cols', [(s, s ^ mask) for s in range(self.parts)])  119 us
    ppermute x60, waiting for transfers between devices, send(): lax.ppermute(block, 'cols', [(s, s ^ mask) for s in range(self.parts)])  54.2 us
    pallas_call x2, Pallas kernels, right_chain(): pl.pallas_call(functools.partial(right_body, parts), grid=(1,), in_specs=...  13.2 us
    pallas_call x1, Pallas kernels, left_chain(): pl.pallas_call(functools.partial(left_body, parts, shrink), grid=(rows //...  11.9 us
  transfers between devices with their start and end apart: 60, of which 16 were waited for; matrix products, arithmetic and copies ran while one was open for 0% of the time, Pallas kernels for 7%

profile of v4, /device:TPU:0, one launch (start us, length us, event | category | flops | bytes accessed | tf_op | source)
XLA Modules:
  0.0 202.4 jit_solution(15478079834085788880)
XLA Ops:
  0.0 11.9 %left_chain.1 = (f32[256,128]{1,0:T(8,128)}, f32[256,128]{1,0:T(8,128)}, f32[256,128]{1,0:T(8,128)}, f32[256,128]{1,0:T(8,128)}, f32[256,128]{1,0:T(8,128)}, /*i...) custom-call(f32[256,4096]{1,0:T(8,128)} %bitcast.8, ...), custom_call_target="tpu_custom_call" | custom-call | flops 3221225472 | bytes 8388608 | tf_op jit(solution)/shard_map/left_chain/pallas_call | solution.py:145
  11.9 3.0 %collective-permute-start = (f32[256,128]{1,0:T(8,128)}, f32[256,128]{1,0:T(8,128)S(1)}, u32[]{:S(2)}, u32[]{:S(2)}) collective-permute-start(f32[256,128]{1,0:T(8,128)} %get-tuple-element.183), channel_id=1, source_target_pairs={{0,2},{2,0},{4,6},{6,4},{8,10},{10,8},{12,14},{14,12},{16,18},{18,... | collective-permute-start | bytes 393224 | tf_op jit(solution)/shard_map/ppermute | solution.py:313
  14.9 3.6 %collective-permute-start.1 = (f32[256,128]{1,0:T(8,128)}, f32[256,128]{1,0:T(8,128)S(1)}, u32[]{:S(2)}, u32[]{:S(2)}) collective-permute-start(f32[256,128]{1,0:T(8,128)} %get-tuple-element.187), channel_id=1, source_target_pairs={{0,26},{2,24},{4,30},{6,28},{8,18},{10,16},{12,22},{14,20},{16,10}... | collective-permute-start | bytes 393224 | tf_op jit(solution)/shard_map/ppermute | solution.py:313
  19.0 3.8 %collective-permute-start.10 = (f32[256,128]{1,0:T(8,128)}, f32[256,128]{1,0:T(8,128)S(1)}, u32[]{:S(2)}, u32[]{:S(2)}) collective-permute-start(f32[256,128]{1,0:T(8,128)} %get-tuple-element.212), channel_id=1, source_target_pairs={{0,24},{2,26},{4,28},{6,30},{8,16},{10,18},{12,20},{14,22},{16,8},... | collective-permute-start | bytes 393224 | tf_op jit(solution)/shard_map/ppermute | solution.py:313
  25.8 7.5 %collective-permute-done.3.rest_8_ = f32[256,128]{1,0:T(8,128)S(1)} collective-permute-done((f32[256,128]{1,0:T(8,128)}, f32[256,128]{1,0:T(8,128)S(1)}, u32[]{:S(2)}, u32[]{:S(2)}) %collective-permute-start.3) | collective-permute-done | bytes 131104 | tf_op jit(solution)/shard_map/ppermute | solution.py:313
  34.4 2.7 %collective-permute-start.8 = (f32[256,128]{1,0:T(8,128)}, f32[256,128]{1,0:T(8,128)S(1)}, u32[]{:S(2)}, u32[]{:S(2)}) collective-permute-start(f32[256,128]{1,0:T(8,128)} %get-tuple-element.206), channel_id=1, source_target_pairs={{0,28},{2,30},{4,24},{6,26},{8,20},{10,22},{12,16},{14,18},{16,12}... | collective-permute-start | bytes 393224 | tf_op jit(solution)/shard_map/ppermute | solution.py:313
  37.1 2.9 %collective-permute-start.11 = (f32[256,128]{1,0:T(8,128)}, f32[256,128]{1,0:T(8,128)S(1)}, u32[]{:S(2)}, u32[]{:S(2)}) collective-permute-start(f32[256,128]{1,0:T(8,128)} %get-tuple-element.213), channel_id=1, source_target_pairs={{0,18},{2,16},{4,22},{6,20},{8,26},{10,24},{12,30},{14,28},{16,2},... | collective-permute-start | bytes 393224 | tf_op jit(solution)/shard_map/ppermute | solution.py:313
  46.1 7.9 %collective-permute-start.9 = (f32[256,128]{1,0:T(8,128)}, f32[256,128]{1,0:T(8,128)S(1)}, u32[]{:S(2)}, u32[]{:S(2)}) collective-permute-start(f32[256,128]{1,0:T(8,128)} %get-tuple-element.207), channel_id=1, source_target_pairs={{0,14},{2,12},{4,10},{6,8},{8,6},{10,4},{12,2},{14,0},{16,30},{18,... | collective-permute-start | bytes 393224 | tf_op jit(solution)/shard_map/ppermute | solution.py:313
  54.0 2.6 %collective-permute-done.11.rest_9_ = f32[256,128]{1,0:T(8,128)S(1)} collective-permute-done((f32[256,128]{1,0:T(8,128)}, f32[256,128]{1,0:T(8,128)S(1)}, u32[]{:S(2)}, u32[]{:S(2)}) %collective-permute-start.11) | collective-permute-done | bytes 131104 | tf_op jit(solution)/shard_map/ppermute | solution.py:313
  57.0 4.1 %collective-permute-done.13.rest_11_ = f32[256,128]{1,0:T(8,128)S(1)} collective-permute-done((f32[256,128]{1,0:T(8,128)}, f32[256,128]{1,0:T(8,128)S(1)}, u32[]{:S(2)}, u32[]{:S(2)}) %collective-permute-start.13) | collective-permute-done | bytes 131104 | tf_op jit(solution)/shard_map/ppermute | solution.py:313
  61.3 3.3 %collective-permute-start.16 = (f32[256,128]{1,0:T(8,128)S(1)}, f32[256,128]{1,0:T(8,128)S(1)}, u32[]{:S(2)}, u32[]{:S(2)}) collective-permute-start(f32[256,128]{1,0:T(8,128)S(1)} %copy-done.17), channel_id=1, source_target_pairs={{0,26},{2,24},{4,30},{6,28},{8,18},{10,16},{12,22},{14,20},{16,10}... | collective-permute-start | bytes 393224 | tf_op jit(solution)/shard_map/ppermute | solution.py:313
  64.6 4.8 %collective-permute-start.21 = (f32[256,128]{1,0:T(8,128)S(1)}, f32[256,128]{1,0:T(8,128)S(1)}, u32[]{:S(2)}, u32[]{:S(2)}) collective-permute-start(f32[256,128]{1,0:T(8,128)S(1)} %copy-done.15), channel_id=1, source_target_pairs={{0,16},{2,18},{4,20},{6,22},{8,24},{10,26},{12,28},{14,30},{16,0},... | collective-permute-start | bytes 393224 | tf_op jit(solution)/shard_map/ppermute | solution.py:313
  70.7 3.6 %collective-permute-start.23 = (f32[256,128]{1,0:T(8,128)S(1)}, f32[256,128]{1,0:T(8,128)S(1)}, u32[]{:S(2)}, u32[]{:S(2)}) collective-permute-start(f32[256,128]{1,0:T(8,128)S(1)} %copy-done.14), channel_id=1, source_target_pairs={{0,24},{2,26},{4,28},{6,30},{8,16},{10,18},{12,20},{14,22},{16,8},... | collective-permute-start | bytes 393224 | tf_op jit(solution)/shard_map/ppermute | solution.py:313
  74.4 6.6 %right_chain.2 = (f32[256,128]{1,0:T(8,128)S(1)}, f32[256,128]{1,0:T(8,128)S(1)}, f32[256,128]{1,0:T(8,128)S(1)}, f32[256,128]{1,0:T(8,128)S(1)}, f32[256,128]{1...) custom-call(f32[4096,3]{1,0:T(8,128)S(1)} %multiply_bitcast_fusion.l, ...), custom_call_target="tpu_custom_call" | custom-call | flops 1610612736 | bytes 6291456 | tf_op jit(solution)/shard_map/right_chain/pallas_call | solution.py:207
  83.5 4.2 %collective-permute-start.22 = (f32[256,128]{1,0:T(8,128)S(1)}, f32[256,128]{1,0:T(8,128)S(1)}, u32[]{:S(2)}, u32[]{:S(2)}) collective-permute-start(f32[256,128]{1,0:T(8,128)S(1)} %copy-done.10), channel_id=1, source_target_pairs={{0,10},{2,8},{4,14},{6,12},{8,2},{10,0},{12,6},{14,4},{16,26},{18,... | collective-permute-start | bytes 393224 | tf_op jit(solution)/shard_map/ppermute | solution.py:313
  87.7 4.1 %collective-permute-start.24 = (f32[256,128]{1,0:T(8,128)S(1)}, f32[256,128]{1,0:T(8,128)S(1)}, u32[]{:S(2)}, u32[]{:S(2)}) collective-permute-start(f32[256,128]{1,0:T(8,128)S(1)} %copy-done.9), channel_id=1, source_target_pairs={{0,18},{2,16},{4,22},{6,20},{8,26},{10,24},{12,30},{14,28},{16,2},... | collective-permute-start | bytes 393224 | tf_op jit(solution)/shard_map/ppermute | solution.py:313
  94.4 3.4 %collective-permute-start.28 = (f32[256,128]{1,0:T(8,128)S(1)}, f32[256,128]{1,0:T(8,128)S(1)}, u32[]{:S(2)}, u32[]{:S(2)}) collective-permute-start(f32[256,128]{1,0:T(8,128)S(1)} %copy-done.7), channel_id=1, source_target_pairs={{0,22},{2,20},{4,18},{6,16},{8,30},{10,28},{12,26},{14,24},{16,6},... | collective-permute-start | bytes 393224 | tf_op jit(solution)/shard_map/ppermute | solution.py:313
  99.4 2.8 %collective-permute-start.29 = (f32[256,128]{1,0:T(8,128)S(1)}, f32[256,128]{1,0:T(8,128)S(1)}, u32[]{:S(2)}, u32[]{:S(2)}) collective-permute-start(f32[256,128]{1,0:T(8,128)S(1)} %copy-done.5), channel_id=1, source_target_pairs={{0,30},{2,28},{4,26},{6,24},{8,22},{10,20},{12,18},{14,16},{16,14}... | collective-permute-start | bytes 393224 | tf_op jit(solution)/shard_map/ppermute | solution.py:313
  102.2 2.7 %collective-permute-done.24.rest_9_ = f32[256,128]{1,0:T(8,128)S(1)} collective-permute-done((f32[256,128]{1,0:T(8,128)S(1)}, f32[256,128]{1,0:T(8,128)S(1)}, u32[]{:S(2)}, u32[]{:S(2)}) %collective-permute-start.24) | collective-permute-done | bytes 131104 | tf_op jit(solution)/shard_map/ppermute | solution.py:313
  105.5 5.3 %collective-permute-done.28.rest_11_ = f32[256,128]{1,0:T(8,128)S(1)} collective-permute-done((f32[256,128]{1,0:T(8,128)S(1)}, f32[256,128]{1,0:T(8,128)S(1)}, u32[]{:S(2)}, u32[]{:S(2)}) %collective-permute-start.28) | collective-permute-done | bytes 131104 | tf_op jit(solution)/shard_map/ppermute | solution.py:313
  113.3 5.7 %collective-permute-start.34 = (f32[256,128]{1,0:T(8,128)S(1)}, f32[256,128]{1,0:T(8,128)S(1)}, u32[]{:S(2)}, u32[]{:S(2)}) collective-permute-start(f32[256,128]{1,0:T(8,128)S(1)} %get-tuple-element.287), channel_id=1, source_target_pairs={{0,16},{2,18},{4,20},{6,22},{8,24},{10,26},{12,28},{14,30},{16,0},... | collective-permute-start | bytes 393224 | tf_op jit(solution)/shard_map/ppermute | solution.py:313
  120.8 6.6 %right_chain.3 = (f32[256,128]{1,0:T(8,128)S(1)}, f32[256,128]{1,0:T(8,128)S(1)}, f32[256,128]{1,0:T(8,128)S(1)}, f32[256,128]{1,0:T(8,128)S(1)}, f32[256,128]{1...) custom-call(f32[4096,3]{1,0:T(8,128)S(1)} %multiply_bitcast_fusion.l, ...), custom_call_target="tpu_custom_call" | custom-call | flops 1610612736 | bytes 6291456 | tf_op jit(solution)/shard_map/right_chain/pallas_call | solution.py:207
  130.5 3.3 %collective-permute-start.46 = (f32[256,128]{1,0:T(8,128)S(1)}, f32[256,128]{1,0:T(8,128)S(1)}, u32[]{:S(2)}, u32[]{:S(2)}) collective-permute-start(f32[256,128]{1,0:T(8,128)S(1)} %get-tuple-element.310), channel_id=1, source_target_pairs={{0,20},{2,22},{4,16},{6,18},{8,28},{10,30},{12,24},{14,26},{16,4},... | collective-permute-start | bytes 393224 | tf_op jit(solution)/shard_map/ppermute | solution.py:313
  135.4 2.7 %collective-permute-start.40 = (f32[256,128]{1,0:T(8,128)S(1)}, f32[256,128]{1,0:T(8,128)S(1)}, u32[]{:S(2)}, u32[]{:S(2)}) collective-permute-start(f32[256,128]{1,0:T(8,128)S(1)} %get-tuple-element.299), channel_id=1, source_target_pairs={{0,18},{2,16},{4,22},{6,20},{8,26},{10,24},{12,30},{14,28},{16,2},... | collective-permute-start | bytes 393224 | tf_op jit(solution)/shard_map/ppermute | solution.py:313
  138.1 3.6 %collective-permute-start.36 = (f32[256,128]{1,0:T(8,128)S(1)}, f32[256,128]{1,0:T(8,128)S(1)}, u32[]{:S(2)}, u32[]{:S(2)}) collective-permute-start(f32[256,128]{1,0:T(8,128)S(1)} %get-tuple-element.289), channel_id=1, source_target_pairs={{0,30},{2,28},{4,26},{6,24},{8,22},{10,20},{12,18},{14,16},{16,14}... | collective-permute-start | bytes 393224 | tf_op jit(solution)/shard_map/ppermute | solution.py:313
  141.7 6.8 %collective-permute-done.46.rest_10_ = f32[256,128]{1,0:T(8,128)S(1)} collective-permute-done((f32[256,128]{1,0:T(8,128)S(1)}, f32[256,128]{1,0:T(8,128)S(1)}, u32[]{:S(2)}, u32[]{:S(2)}) %collective-permute-start.46) | collective-permute-done | bytes 131104 | tf_op jit(solution)/shard_map/ppermute | solution.py:313
  163.5 2.6 %collective-permute-start.54 = (f32[256,128]{1,0:T(8,128)S(1)}, f32[256,128]{1,0:T(8,128)S(1)}, u32[]{:S(2)}, u32[]{:S(2)}) collective-permute-start(f32[256,128]{1,0:T(8,128)S(1)} %get-tuple-element.326), channel_id=1, source_target_pairs={{0,18},{2,16},{4,22},{6,20},{8,26},{10,24},{12,30},{14,28},{16,2},... | collective-permute-start | bytes 393224 | tf_op jit(solution)/shard_map/ppermute | solution.py:313
  166.1 4.4 %collective-permute-start.57 = (f32[256,128]{1,0:T(8,128)S(1)}, f32[256,128]{1,0:T(8,128)S(1)}, u32[]{:S(2)}, u32[]{:S(2)}) collective-permute-start(f32[256,128]{1,0:T(8,128)S(1)} %get-tuple-element.332), channel_id=1, source_target_pairs={{0,28},{2,30},{4,24},{6,26},{8,20},{10,22},{12,16},{14,18},{16,12}... | collective-permute-start | bytes 393224 | tf_op jit(solution)/shard_map/ppermute | solution.py:313
  170.5 4.3 %collective-permute-done.52.rest_8_ = f32[256,128]{1,0:T(8,128)S(1)} collective-permute-done((f32[256,128]{1,0:T(8,128)S(1)}, f32[256,128]{1,0:T(8,128)S(1)}, u32[]{:S(2)}, u32[]{:S(2)}) %collective-permute-start.52) | collective-permute-done | bytes 131104 | tf_op jit(solution)/shard_map/ppermute | solution.py:313
  177.2 6.9 %collective-permute-done.54.rest_9_ = f32[256,128]{1,0:T(8,128)S(1)} collective-permute-done((f32[256,128]{1,0:T(8,128)S(1)}, f32[256,128]{1,0:T(8,128)S(1)}, u32[]{:S(2)}, u32[]{:S(2)}) %collective-permute-start.54) | collective-permute-done | bytes 131104 | tf_op jit(solution)/shard_map/ppermute | solution.py:313
  184.1 5.9 %collective-permute-start.58 = (f32[256,128]{1,0:T(8,128)S(1)}, f32[256,128]{1,0:T(8,128)S(1)}, u32[]{:S(2)}, u32[]{:S(2)}) collective-permute-start(f32[256,128]{1,0:T(8,128)S(1)} %get-tuple-element.333), channel_id=1, source_target_pairs={{0,22},{2,20},{4,18},{6,16},{8,30},{10,28},{12,26},{14,24},{16,6},... | collective-permute-start | bytes 393224 | tf_op jit(solution)/shard_map/ppermute | solution.py:313
  196.0 4.1 %collective-permute-done.58.rest_11_ = f32[256,128]{1,0:T(8,128)S(1)} collective-permute-done((f32[256,128]{1,0:T(8,128)S(1)}, f32[256,128]{1,0:T(8,128)S(1)}, u32[]{:S(2)}, u32[]{:S(2)}) %collective-permute-start.58) | collective-permute-done | bytes 131104 | tf_op jit(solution)/shard_map/ppermute | solution.py:313
  (134 shorter events, 54.4 us)
Async XLA Ops:
  18.4 14.8 %collective-permute-start.3 = (f32[256,128]{1,0:T(8,128)}, f32[256,128]{1,0:T(8,128)S(1)}, u32[]{:S(2)}, u32[]{:S(2)}) collective-permute-start(f32[256,128]{1,0:T(8,128)} %get-tuple-element.193), channel_id=1, source_target_pairs={{0,16},{2,18},{4,20},{6,22},{8,24},{10,26},{12,28},{14,30},{16,0},... | collective-permute-start | bytes 393224 | tf_op jit(solution)/shard_map/ppermute | solution.py:313
  18.4 16.0 %collective-permute-start.6 = (f32[256,128]{1,0:T(8,128)}, f32[256,128]{1,0:T(8,128)S(1)}, u32[]{:S(2)}, u32[]{:S(2)}) collective-permute-start(f32[256,128]{1,0:T(8,128)} %get-tuple-element.198), channel_id=1, source_target_pairs={{0,8},{2,10},{4,12},{6,14},{8,0},{10,2},{12,4},{14,6},{16,24},{18,... | collective-permute-start | bytes 393224 | tf_op jit(solution)/shard_map/ppermute | solution.py:313
  19.0 18.1 %collective-permute-start.10 = (f32[256,128]{1,0:T(8,128)}, f32[256,128]{1,0:T(8,128)S(1)}, u32[]{:S(2)}, u32[]{:S(2)}) collective-permute-start(f32[256,128]{1,0:T(8,128)} %get-tuple-element.212), channel_id=1, source_target_pairs={{0,24},{2,26},{4,28},{6,30},{8,16},{10,18},{12,20},{14,22},{16,8},... | collective-permute-start | bytes 393224 | tf_op jit(solution)/shard_map/ppermute | solution.py:313
  22.8 18.0 %collective-permute-start.7 = (f32[256,128]{1,0:T(8,128)}, f32[256,128]{1,0:T(8,128)S(1)}, u32[]{:S(2)}, u32[]{:S(2)}) collective-permute-start(f32[256,128]{1,0:T(8,128)} %get-tuple-element.202), channel_id=1, source_target_pairs={{0,12},{2,14},{4,8},{6,10},{8,4},{10,6},{12,0},{14,2},{16,28},{18,... | collective-permute-start | bytes 393224 | tf_op jit(solution)/shard_map/ppermute | solution.py:313
  24.3 18.3 %collective-permute-start.2 = (f32[256,128]{1,0:T(8,128)}, f32[256,128]{1,0:T(8,128)S(1)}, u32[]{:S(2)}, u32[]{:S(2)}) collective-permute-start(f32[256,128]{1,0:T(8,128)} %get-tuple-element.188), channel_id=1, source_target_pairs={{0,4},{2,6},{4,0},{6,2},{8,12},{10,14},{12,8},{14,10},{16,20},{18,... | collective-permute-start | bytes 393224 | tf_op jit(solution)/shard_map/ppermute | solution.py:313
  37.1 19.5 %collective-permute-start.11 = (f32[256,128]{1,0:T(8,128)}, f32[256,128]{1,0:T(8,128)S(1)}, u32[]{:S(2)}, u32[]{:S(2)}) collective-permute-start(f32[256,128]{1,0:T(8,128)} %get-tuple-element.213), channel_id=1, source_target_pairs={{0,18},{2,16},{4,22},{6,20},{8,26},{10,24},{12,30},{14,28},{16,2},... | collective-permute-start | bytes 393224 | tf_op jit(solution)/shard_map/ppermute | solution.py:313
  40.8 20.2 %collective-permute-start.13 = (f32[256,128]{1,0:T(8,128)}, f32[256,128]{1,0:T(8,128)S(1)}, u32[]{:S(2)}, u32[]{:S(2)}) collective-permute-start(f32[256,128]{1,0:T(8,128)} %get-tuple-element.219), channel_id=1, source_target_pairs={{0,22},{2,20},{4,18},{6,16},{8,30},{10,28},{12,26},{14,24},{16,6},... | collective-permute-start | bytes 393224 | tf_op jit(solution)/shard_map/ppermute | solution.py:313
  42.6 18.7 %collective-permute-start.14 = (f32[256,128]{1,0:T(8,128)}, f32[256,128]{1,0:T(8,128)S(1)}, u32[]{:S(2)}, u32[]{:S(2)}) collective-permute-start(f32[256,128]{1,0:T(8,128)} %get-tuple-element.225), channel_id=1, source_target_pairs={{0,30},{2,28},{4,26},{6,24},{8,22},{10,20},{12,18},{14,16},{16,14}... | collective-permute-start | bytes 393224 | tf_op jit(solution)/shard_map/ppermute | solution.py:313
  44.7 19.9 %collective-permute-start.5 = (f32[256,128]{1,0:T(8,128)}, f32[256,128]{1,0:T(8,128)S(1)}, u32[]{:S(2)}, u32[]{:S(2)}) collective-permute-start(f32[256,128]{1,0:T(8,128)} %get-tuple-element.195), channel_id=1, source_target_pairs={{0,6},{2,4},{4,2},{6,0},{8,14},{10,12},{12,10},{14,8},{16,22},{18,... | collective-permute-start | bytes 393224 | tf_op jit(solution)/shard_map/ppermute | solution.py:313
  46.1 23.3 %collective-permute-start.9 = (f32[256,128]{1,0:T(8,128)}, f32[256,128]{1,0:T(8,128)S(1)}, u32[]{:S(2)}, u32[]{:S(2)}) collective-permute-start(f32[256,128]{1,0:T(8,128)} %get-tuple-element.207), channel_id=1, source_target_pairs={{0,14},{2,12},{4,10},{6,8},{8,6},{10,4},{12,2},{14,0},{16,30},{18,... | collective-permute-start | bytes 393224 | tf_op jit(solution)/shard_map/ppermute | solution.py:313
  61.0 20.0 %collective-permute-start.15 = (f32[256,128]{1,0:T(8,128)S(1)}, f32[256,128]{1,0:T(8,128)S(1)}, u32[]{:S(2)}, u32[]{:S(2)}) collective-permute-start(f32[256,128]{1,0:T(8,128)S(1)} %copy-done.18), channel_id=1, source_target_pairs={{0,2},{2,0},{4,6},{6,4},{8,10},{10,8},{12,14},{14,12},{16,18},{18,... | collective-permute-start | bytes 393224 | tf_op jit(solution)/shard_map/ppermute | solution.py:313
  61.3 19.8 %collective-permute-start.16 = (f32[256,128]{1,0:T(8,128)S(1)}, f32[256,128]{1,0:T(8,128)S(1)}, u32[]{:S(2)}, u32[]{:S(2)}) collective-permute-start(f32[256,128]{1,0:T(8,128)S(1)} %copy-done.17), channel_id=1, source_target_pairs={{0,26},{2,24},{4,30},{6,28},{8,18},{10,16},{12,22},{14,20},{16,10}... | collective-permute-start | bytes 393224 | tf_op jit(solution)/shard_map/ppermute | solution.py:313
  64.6 18.8 %collective-permute-start.21 = (f32[256,128]{1,0:T(8,128)S(1)}, f32[256,128]{1,0:T(8,128)S(1)}, u32[]{:S(2)}, u32[]{:S(2)}) collective-permute-start(f32[256,128]{1,0:T(8,128)S(1)} %copy-done.15), channel_id=1, source_target_pairs={{0,16},{2,18},{4,20},{6,22},{8,24},{10,26},{12,28},{14,30},{16,0},... | collective-permute-start | bytes 393224 | tf_op jit(solution)/shard_map/ppermute | solution.py:313
  70.7 17.0 %collective-permute-start.23 = (f32[256,128]{1,0:T(8,128)S(1)}, f32[256,128]{1,0:T(8,128)S(1)}, u32[]{:S(2)}, u32[]{:S(2)}) collective-permute-start(f32[256,128]{1,0:T(8,128)S(1)} %copy-done.14), channel_id=1, source_target_pairs={{0,24},{2,26},{4,28},{6,30},{8,16},{10,18},{12,20},{14,22},{16,8},... | collective-permute-start | bytes 393224 | tf_op jit(solution)/shard_map/ppermute | solution.py:313
  81.5 16.4 %collective-permute-start.19 = (f32[256,128]{1,0:T(8,128)S(1)}, f32[256,128]{1,0:T(8,128)S(1)}, u32[]{:S(2)}, u32[]{:S(2)}) collective-permute-start(f32[256,128]{1,0:T(8,128)S(1)} %copy-done.11), channel_id=1, source_target_pairs={{0,28},{2,30},{4,24},{6,26},{8,20},{10,22},{12,16},{14,18},{16,12}... | collective-permute-start | bytes 393224 | tf_op jit(solution)/shard_map/ppermute | solution.py:313
  83.5 15.9 %collective-permute-start.22 = (f32[256,128]{1,0:T(8,128)S(1)}, f32[256,128]{1,0:T(8,128)S(1)}, u32[]{:S(2)}, u32[]{:S(2)}) collective-permute-start(f32[256,128]{1,0:T(8,128)S(1)} %copy-done.10), channel_id=1, source_target_pairs={{0,10},{2,8},{4,14},{6,12},{8,2},{10,0},{12,6},{14,4},{16,26},{18,... | collective-permute-start | bytes 393224 | tf_op jit(solution)/shard_map/ppermute | solution.py:313
  87.7 17.2 %collective-permute-start.24 = (f32[256,128]{1,0:T(8,128)S(1)}, f32[256,128]{1,0:T(8,128)S(1)}, u32[]{:S(2)}, u32[]{:S(2)}) collective-permute-start(f32[256,128]{1,0:T(8,128)S(1)} %copy-done.9), channel_id=1, source_target_pairs={{0,18},{2,16},{4,22},{6,20},{8,26},{10,24},{12,30},{14,28},{16,2},... | collective-permute-start | bytes 393224 | tf_op jit(solution)/shard_map/ppermute | solution.py:313
  94.4 16.4 %collective-permute-start.28 = (f32[256,128]{1,0:T(8,128)S(1)}, f32[256,128]{1,0:T(8,128)S(1)}, u32[]{:S(2)}, u32[]{:S(2)}) collective-permute-start(f32[256,128]{1,0:T(8,128)S(1)} %copy-done.7), channel_id=1, source_target_pairs={{0,22},{2,20},{4,18},{6,16},{8,30},{10,28},{12,26},{14,24},{16,6},... | collective-permute-start | bytes 393224 | tf_op jit(solution)/shard_map/ppermute | solution.py:313
  97.8 15.4 %collective-permute-start.20 = (f32[256,128]{1,0:T(8,128)S(1)}, f32[256,128]{1,0:T(8,128)S(1)}, u32[]{:S(2)}, u32[]{:S(2)}) collective-permute-start(f32[256,128]{1,0:T(8,128)S(1)} %copy-done.6), channel_id=1, source_target_pairs={{0,6},{2,4},{4,2},{6,0},{8,14},{10,12},{12,10},{14,8},{16,22},{18,... | collective-permute-start | bytes 393224 | tf_op jit(solution)/shard_map/ppermute | solution.py:313
  105.3 25.2 %collective-permute-start.45 = (f32[256,128]{1,0:T(8,128)S(1)}, f32[256,128]{1,0:T(8,128)S(1)}, u32[]{:S(2)}, u32[]{:S(2)}) collective-permute-start(f32[256,128]{1,0:T(8,128)S(1)} %get-tuple-element.309), channel_id=1, source_target_pairs={{0,2},{2,0},{4,6},{6,4},{8,10},{10,8},{12,14},{14,12},{16,18},{18,... | collective-permute-start | bytes 393224 | tf_op jit(solution)/shard_map/ppermute | solution.py:313
  110.8 23.0 %collective-permute-start.49 = (f32[256,128]{1,0:T(8,128)S(1)}, f32[256,128]{1,0:T(8,128)S(1)}, u32[]{:S(2)}, u32[]{:S(2)}) collective-permute-start(f32[256,128]{1,0:T(8,128)S(1)} %get-tuple-element.319), channel_id=1, source_target_pairs={{0,26},{2,24},{4,30},{6,28},{8,18},{10,16},{12,22},{14,20},{16,10}... | collective-permute-start | bytes 393224 | tf_op jit(solution)/shard_map/ppermute | solution.py:313
  113.3 14.7 %collective-permute-start.34 = (f32[256,128]{1,0:T(8,128)S(1)}, f32[256,128]{1,0:T(8,128)S(1)}, u32[]{:S(2)}, u32[]{:S(2)}) collective-permute-start(f32[256,128]{1,0:T(8,128)S(1)} %get-tuple-element.287), channel_id=1, source_target_pairs={{0,16},{2,18},{4,20},{6,22},{8,24},{10,26},{12,28},{14,30},{16,0},... | collective-permute-start | bytes 393224 | tf_op jit(solution)/shard_map/ppermute | solution.py:313
  119.0 16.4 %collective-permute-start.39 = (f32[256,128]{1,0:T(8,128)S(1)}, f32[256,128]{1,0:T(8,128)S(1)}, u32[]{:S(2)}, u32[]{:S(2)}) collective-permute-start(f32[256,128]{1,0:T(8,128)S(1)} %get-tuple-element.298), channel_id=1, source_target_pairs={{0,24},{2,26},{4,28},{6,30},{8,16},{10,18},{12,20},{14,22},{16,8},... | collective-permute-start | bytes 393224 | tf_op jit(solution)/shard_map/ppermute | solution.py:313
  130.5 17.9 %collective-permute-start.46 = (f32[256,128]{1,0:T(8,128)S(1)}, f32[256,128]{1,0:T(8,128)S(1)}, u32[]{:S(2)}, u32[]{:S(2)}) collective-permute-start(f32[256,128]{1,0:T(8,128)S(1)} %get-tuple-element.310), channel_id=1, source_target_pairs={{0,20},{2,22},{4,16},{6,18},{8,28},{10,30},{12,24},{14,26},{16,4},... | collective-permute-start | bytes 393224 | tf_op jit(solution)/shard_map/ppermute | solution.py:313
  135.4 14.9 %collective-permute-start.40 = (f32[256,128]{1,0:T(8,128)S(1)}, f32[256,128]{1,0:T(8,128)S(1)}, u32[]{:S(2)}, u32[]{:S(2)}) collective-permute-start(f32[256,128]{1,0:T(8,128)S(1)} %get-tuple-element.299), channel_id=1, source_target_pairs={{0,18},{2,16},{4,22},{6,20},{8,26},{10,24},{12,30},{14,28},{16,2},... | collective-permute-start | bytes 393224 | tf_op jit(solution)/shard_map/ppermute | solution.py:313
  138.1 15.0 %collective-permute-start.36 = (f32[256,128]{1,0:T(8,128)S(1)}, f32[256,128]{1,0:T(8,128)S(1)}, u32[]{:S(2)}, u32[]{:S(2)}) collective-permute-start(f32[256,128]{1,0:T(8,128)S(1)} %get-tuple-element.289), channel_id=1, source_target_pairs={{0,30},{2,28},{4,26},{6,24},{8,22},{10,20},{12,18},{14,16},{16,14}... | collective-permute-start | bytes 393224 | tf_op jit(solution)/shard_map/ppermute | solution.py:313
  163.5 20.6 %collective-permute-start.54 = (f32[256,128]{1,0:T(8,128)S(1)}, f32[256,128]{1,0:T(8,128)S(1)}, u32[]{:S(2)}, u32[]{:S(2)}) collective-permute-start(f32[256,128]{1,0:T(8,128)S(1)} %get-tuple-element.326), channel_id=1, source_target_pairs={{0,18},{2,16},{4,22},{6,20},{8,26},{10,24},{12,30},{14,28},{16,2},... | collective-permute-start | bytes 393224 | tf_op jit(solution)/shard_map/ppermute | solution.py:313
  166.1 18.0 %collective-permute-start.38 = (f32[256,128]{1,0:T(8,128)S(1)}, f32[256,128]{1,0:T(8,128)S(1)}, u32[]{:S(2)}, u32[]{:S(2)}) collective-permute-start(f32[256,128]{1,0:T(8,128)S(1)} %get-tuple-element.291), channel_id=1, source_target_pairs={{0,4},{2,6},{4,0},{6,2},{8,12},{10,14},{12,8},{14,10},{16,20},{18,... | collective-permute-start | bytes 393224 | tf_op jit(solution)/shard_map/ppermute | solution.py:313
  166.1 18.0 %collective-permute-start.57 = (f32[256,128]{1,0:T(8,128)S(1)}, f32[256,128]{1,0:T(8,128)S(1)}, u32[]{:S(2)}, u32[]{:S(2)}) collective-permute-start(f32[256,128]{1,0:T(8,128)S(1)} %get-tuple-element.332), channel_id=1, source_target_pairs={{0,28},{2,30},{4,24},{6,26},{8,20},{10,22},{12,16},{14,18},{16,12}... | collective-permute-start | bytes 393224 | tf_op jit(solution)/shard_map/ppermute | solution.py:313
  174.8 15.2 %collective-permute-start.53 = (f32[256,128]{1,0:T(8,128)S(1)}, f32[256,128]{1,0:T(8,128)S(1)}, u32[]{:S(2)}, u32[]{:S(2)}) collective-permute-start(f32[256,128]{1,0:T(8,128)S(1)} %get-tuple-element.323), channel_id=1, source_target_pairs={{0,12},{2,14},{4,8},{6,10},{8,4},{10,6},{12,0},{14,2},{16,28},{18,... | collective-permute-start | bytes 393224 | tf_op jit(solution)/shard_map/ppermute | solution.py:313
  174.8 17.7 %collective-permute-start.43 = (f32[256,128]{1,0:T(8,128)S(1)}, f32[256,128]{1,0:T(8,128)S(1)}, u32[]{:S(2)}, u32[]{:S(2)}) collective-permute-start(f32[256,128]{1,0:T(8,128)S(1)} %get-tuple-element.302), channel_id=1, source_target_pairs={{0,26},{2,24},{4,30},{6,28},{8,18},{10,16},{12,22},{14,20},{16,10}... | collective-permute-start | bytes 393224 | tf_op jit(solution)/shard_map/ppermute | solution.py:313
  184.1 16.0 %collective-permute-start.58 = (f32[256,128]{1,0:T(8,128)S(1)}, f32[256,128]{1,0:T(8,128)S(1)}, u32[]{:S(2)}, u32[]{:S(2)}) collective-permute-start(f32[256,128]{1,0:T(8,128)S(1)} %get-tuple-element.333), channel_id=1, source_target_pairs={{0,22},{2,20},{4,18},{6,16},{8,30},{10,28},{12,26},{14,24},{16,6},... | collective-permute-start | bytes 393224 | tf_op jit(solution)/shard_map/ppermute | solution.py:313
  (47 other events, 660.9 us)
